TPU v7x, 512 devices: a whole 4x4x16 slice. The times are simulated.
512 devices in a mesh: rows: 64 (over y_hi, z, core), tp: 8 (over x, y_lo).
Axes of the slice: x: 4, y: 4 (y_hi: 2, y_lo: 2; y = y_hi * 2 + y_lo), z: 16, core: 2. Of those that a mesh axis runs over, the one named last changes fastest.
Arguments:
- resid: bfloat16 [49152, 8192], P('rows', 'tp'), may hold values from -41 to 41
- attention_heads_output: bfloat16 [49152, 8192], P('rows', 'tp'), may hold values from -6 to 6
- adapter_down_matrix: bfloat16 [8192, 64], P('tp'), may hold values from -0.0625 to 0.0625
- adapter_up_matrix: bfloat16 [64, 8192], P(None, 'tp'), may hold values from -0.75 to 0.75
- drafter_norm_scale: bfloat16 [8192], P('tp'), may hold values from 0.099609375 to 1.8984375
- drafter_value_matrix: bfloat16 [8192, 512], P('tp'), may hold values from -0.0625 to 0.0625
- target: bfloat16 [49152, 512], P(('rows', 'tp')), may hold values from -6 to 6
Outputs:
- values: bfloat16 [49152, 512], P(('rows', 'tp'))
- value_grad: bfloat16 [8192, 512], P(('tp', 'rows'))
- a_grad: float32 [8192, 64], P('tp')
- b_grad: float32 [64, 8192], P(None, 'tp')
- gain_grad: float32 [8192], P('tp')
All inputs are finite; a program needn't handle non-finite values.
Results may differ from a plain program's by a relative error of at most 0.0052.
Values may be sent and summed in bfloat16 or wider, within the bound.
No kernel may reach another device: no remote copies, remote signals or barrier semaphores. Data moves between devices by JAX's collectives and lax.ppermute only.
A program may use at most 64 MiB of HBM per device.

v0:
```python
import jax
import jax.numpy as jnp
from jax import lax
from jax.sharding import PartitionSpec as P

MODEL_WIDTH = 8192


EPSILON = 1e-06


def body(
    resid,
    attention_heads_output,
    adapter_down_matrix,
    adapter_up_matrix,
    drafter_norm_scale,
    drafter_value_matrix,
    target,
):
    member = lax.axis_index("tp")
    share_rows = target.shape[0]
    total_tokens = resid.shape[0] * lax.axis_size("rows")
    loss_scale = 1.0 / total_tokens**0.5
    contract_rows = (((0,), (0,)), ((), ()))
    input_rows = resid.astype(jnp.float32)
    up_matrix_wide = adapter_up_matrix.astype(jnp.float32)
    gain_wide = drafter_norm_scale.astype(jnp.float32)
    down_partial = jnp.dot(
        attention_heads_output, adapter_down_matrix, preferred_element_type=jnp.float32
    )
    down_projected = lax.psum(down_partial, "tp")
    down_times_up = down_projected.astype(jnp.bfloat16)
    hidden_rows = input_rows + 0.5 * jnp.dot(
        down_times_up, adapter_up_matrix, preferred_element_type=jnp.float32
    )
    square_sums = lax.psum(jnp.sum(hidden_rows * hidden_rows, axis=1), "tp")
    inverse_rms = lax.rsqrt(square_sums / MODEL_WIDTH + EPSILON)
    normed = (hidden_rows * inverse_rms[:, None] * gain_wide).astype(jnp.bfloat16)
    partial_values = jnp.dot(normed, drafter_value_matrix, preferred_element_type=jnp.float32)
    summed = lax.psum(partial_values, "tp")
    sums = lax.dynamic_slice_in_dim(summed, member * share_rows, share_rows, 0)
    value_error = ((sums - target.astype(jnp.float32)) * loss_scale).astype(jnp.bfloat16)
    errors_all = lax.all_gather(value_error, "tp", axis=0, tiled=True)
    value_grad = lax.dot_general(
        normed, errors_all, contract_rows, preferred_element_type=jnp.float32
    )
    normed_grad = lax.dot_general(
        errors_all,
        drafter_value_matrix,
        (((1,), (1,)), ((), ())),
        preferred_element_type=jnp.float32,
    )
    gain_grad = jnp.sum(normed_grad * hidden_rows * inverse_rms[:, None], axis=0)
    scaled_grad = normed_grad * gain_wide
    inner_part = jnp.sum(scaled_grad * hidden_rows, axis=1)
    inner = lax.psum(inner_part, "tp")
    factor = inner * inverse_rms**3 / MODEL_WIDTH
    hidden_grad = inverse_rms[:, None] * scaled_grad - hidden_rows * factor[:, None]
    down_local = 0.5 * jnp.dot(hidden_grad, up_matrix_wide.T, precision=lax.Precision.HIGHEST)
    down_grad = lax.psum(down_local, "tp")
    b_grad = 0.5 * lax.dot_general(
        down_times_up.astype(jnp.float32),
        hidden_grad,
        contract_rows,
        precision=lax.Precision.HIGHEST,
    )
    a_grad = lax.dot_general(
        attention_heads_output,
        down_grad.astype(jnp.bfloat16),
        contract_rows,
        preferred_element_type=jnp.float32,
    )
    a_grad, b_grad, gain_grad = lax.psum((a_grad, b_grad, gain_grad), "rows")
    value_grad = lax.psum_scatter(value_grad, "rows", scatter_dimension=0, tiled=True)
    return (sums.astype(jnp.bfloat16), value_grad.astype(jnp.bfloat16), a_grad, b_grad, gain_grad)


def solution(mesh):
    in_specs = (
        P("rows", "tp"),
        P("rows", "tp"),
        P("tp", None),
        P(None, "tp"),
        P("tp"),
        P("tp", None),
        P(("rows", "tp"), None),
    )
    out_specs = (
        P(("rows", "tp"), None),
        P(("tp", "rows"), None),
        P("tp", None),
        P(None, "tp"),
        P("tp"),
    )
    return jax.shard_map(body, mesh=mesh, in_specs=in_specs, out_specs=out_specs, check_vma=False)
```

profile of v0, /device:TPU:1, one launch (start us, length us, event | category | flops | bytes accessed | tf_op | source)
XLA Modules:
  0.0 954.7 jit_solution(18395389908304868690)
XLA Ops:
  7.2 0.0 copy-start
  7.2 0.0 all-reduce.6.cloned.1.call-start
  7.2 0.8 convert_element_type.31
  8.0 0.6 copy-done
  8.6 0.0 copy-start.2
  8.6 1.6 fusion.7
  10.2 30.3 %all-reduce.9 = bf16[768,64]{0,1:T(8,128)(2,1)S(1)} all-reduce(f32[768,64]{0,1:T(8,128)S(1)} %fusion.7), channel_id=1, replica_groups=mesh['rows'=64,'tp'=8] {'tp'}, use_global_device_ids=true, to_apply=%region_0.0 | all-reduce | flops 49152 | bytes 294912 | tf_op jit(solution)/shard_map/psum | solution.py:32
  40.5 3.8 multiply_reduce_fusion.2
  44.3 12.5 %psum.57 = f32[768]{0:T(1024)S(1)} all-reduce(f32[768]{0:T(1024)S(1)} %get-tuple-element.9), channel_id=1, replica_groups=mesh['rows'=64,'tp'=8] {'tp'}, use_global_device_ids=true, to_apply=%region_2.0 | all-reduce | flops 768 | bytes 6144 | tf_op jit(solution)/shard_map/psum | solution.py:37
  56.8 0.0 copy-done.2
  56.8 0.0 copy-start.4
  56.8 4.1 fusion.6
  60.9 0.0 all-reduce.6.cloned.1.call-update
  60.9 0.0 reduce-scatter.2.cloned.1.call-start
  61.0 113.0 %all-reduce.6.cloned.1.call-done = f32[768,512]{1,0:T(8,128)} async-done(((f32[768,512]{1,0:T(8,128)}), f32[768,512]{1,0:T(8,128)}) %all-reduce.6.cloned.1.call-update) | async-done | bytes 1572880 | tf_op jit(solution)/shard_map/psum | solution.py:41
  174.0 0.0 copy-done.4
  174.0 1.0 multiply_convert_fusion.1
  175.0 24.2 %all_gather.3 = bf16[768,512]{1,0:T(8,128)(2,1)S(1)} all-gather(bf16[96,512]{1,0:T(8,128)(2,1)S(1)} %multiply_convert_fusion.1), channel_id=1, replica_groups=mesh['rows'=64,'tp'=8] {'tp'}, dimensions={0}, use_global_device_ids=true | all-gather | bytes 884736 | tf_op jit(solution)/shard_map/all_gather | solution.py:44
  199.2 4.3 fusion.5
  203.5 0.0 reduce-scatter.2.cloned.1.call-update
  203.5 0.0 all-reduce.8.cloned.1.call-start
  203.6 4.7 multiply_reduce_fusion
  208.3 14.4 %psum.59 = f32[768]{0:T(1024)S(1)} all-reduce(f32[768]{0:T(1024)S(1)} %get-tuple-element.6), channel_id=1, replica_groups=mesh['rows'=64,'tp'=8] {'tp'}, use_global_device_ids=true, to_apply=%region_6.0 | all-reduce | flops 768 | bytes 6144 | tf_op jit(solution)/shard_map/psum | solution.py:57
  222.7 0.0 copy-start.3
  222.7 3.4 multiply_subtract_fusion
  226.1 0.0 copy-start.1
  226.1 1.7 copy-done.1
  227.8 0.0 copy-done.3
  227.8 1.5 convolution_multiply_fusion
  229.3 28.8 %all-reduce.10 = bf16[768,64]{1,0:T(8,128)(2,1)S(1)} all-reduce(f32[768,64]{1,0:T(8,128)S(1)} %convolution_multiply_fusion), channel_id=1, replica_groups=mesh['rows'=64,'tp'=8] {'tp'}, use_global_device_ids=true, to_apply=%region_7.0 | all-reduce | flops 49152 | bytes 294912 | tf_op jit(solution)/shard_map/psum | solution.py:61
  258.1 1.1 convolution_bitcast_fusion
  259.2 3.9 convolution_multiply_fusion.1
  263.1 0.0 all-reduce.8.cloned.1.call-update
  263.1 149.0 %psum.63 = f32[1024]{0:T(1024)} all-reduce(f32[1024]{0:T(1024)S(1)} %get-tuple-element.5), channel_id=1, replica_groups=mesh['rows'=64,'tp'=8] {'rows'}, use_global_device_ids=true, to_apply=%region_11.0 | all-reduce | flops 1024 | bytes 8192 | tf_op jit(solution)/shard_map/psum | solution.py:74
  412.1 1.6 dynamic-slice_convert_fusion
  413.7 1.1 reduce-scatter.2.cloned.1.call-done
  414.8 1.4 convert_element_type.36
  416.1 528.7 %all-reduce.8.cloned.1.call-done = (f32[1024,64]{0,1:T(8,128)}, f32[64,1024]{1,0:T(8,128)}) async-done(((f32[1024,64]{0,1:T(8,128)}, f32[64,1024]{1,0:T(8,128)}), (f32[1024,64]{0,1:T(8,128)}, f32[64,1024]{1,0:T(8,128)})) %all-reduce.8.cloned.1.call-update) | async-done | bytes 524304 | tf_op jit(solution)/shard_map/psum | solution.py:74
  944.9 1.7 copy.19
  946.5 1.7 copy.20
  (2 shorter events, 0.0 us)
Async XLA Ops:
  7.2 1.4 copy-start
  7.2 166.8 %all-reduce.6.cloned.1.call-start = ((), (), s32[]{:S(2)}) async-start(), calls=%async_computation.1 | async-start | bytes 3145728 | tf_op jit(solution)/shard_map/psum | solution.py:41
  8.6 48.2 %copy-start.2 = (bf16[1024,512]{1,0:T(8,128)(2,1)S(1)}, bf16[1024,512]{1,0:T(8,128)(2,1)}, u32[]{:S(2)}) copy-start(bf16[1024,512]{1,0:T(8,128)(2,1)} %param.12) | copy-start | bytes 3145732
  56.8 117.2 %copy-start.4 = (bf16[96,512]{1,0:T(8,128)(2,1)S(1)}, bf16[96,512]{1,0:T(8,128)(2,1)}, u32[]{:S(2)}) copy-start(bf16[96,512]{1,0:T(8,128)(2,1)} %param.13) | copy-start | bytes 294916
  60.9 353.8 %reduce-scatter.2.cloned.1.call-start = ((), (), s32[]{:S(2)}) async-start(), calls=%async_computation.2 | async-start | bytes 2129920 | tf_op jit(solution)/shard_map/reduce_scatter | solution.py:75
  203.5 741.3 %all-reduce.8.cloned.1.call-start = ((), (), s32[]{:S(2)}) async-start(), calls=%async_computation.3 | async-start | bytes 1048576 | tf_op jit(solution)/shard_map/psum | solution.py:74
  222.7 5.1 copy-start.3
  226.1 1.7 copy-start.1
Sparse Core Ops, SparseCore 0:
  61.1 112.9 all-reduce.5
  203.7 211.0 reduce-scatter.1
  418.5 526.2 all-reduce.7
where the time goes:
time: 955 us
  waiting for transfers between devices  643 us (67%)
  blocking collectives  259 us (27%)
  matrix products  25.1 us (3%)
  between operations  13.8 us (1%)
    psum x1, waiting for transfers between devices, body(): a_grad, b_grad, gain_grad = lax.psum((a_grad, b_grad, gain_grad), 'rows')  529 us
    psum x1, blocking collectives, body(): a_grad, b_grad, gain_grad = lax.psum((a_grad, b_grad, gain_grad), 'rows')  149 us
    psum x1, waiting for transfers between devices, body(): summed = lax.psum(partial_values, 'tp')  113 us
    psum x1, blocking collectives, body(): down_projected = lax.psum(down_partial, 'tp')  30.3 us
    psum x1, blocking collectives, body(): down_grad = lax.psum(down_local, 'tp')  28.8 us
    all_gather x1, blocking collectives, body(): errors_all = lax.all_gather(value_error, 'tp', axis=0, tiled=True)  24.2 us
  transfers between devices with their start and end apart: 3, of which 3 were waited for; matrix products, arithmetic and copies ran while one was open for 2% of the time, Pallas kernels for 0%

commit v1 on v0

v1 whole, which is shorter than its diff:
```python
import jax
import jax.numpy as jnp
from jax import lax
from jax.sharding import Mesh, PartitionSpec as P

MODEL_WIDTH = 8192
EPSILON = 1e-06
TP = ("x", "y_lo")
ROWS = ("y_hi", "z", "core")
bf16 = jnp.bfloat16
f32 = jnp.float32


def dot(a, b, dims=(((1,), (0,)), ((), ()))):
    return lax.dot_general(a, b, dims, preferred_element_type=f32)


NT = (((1,), (1,)), ((), ()))
TN = (((0,), (0,)), ((), ()))


def split(x):
    high = lax.reduce_precision(x, 8, 7)
    return high.astype(bf16), (x - high).astype(bf16)


def dot_split(a, b, dims=(((1,), (0,)), ((), ()))):
    return dot(a, b[0], dims) + dot(a, b[1], dims)


def body(resid, heads, down_matrix, up, scale, value_matrix, target):
    share = target.shape[0]
    tp = resid.shape[0] // share
    tokens = resid.shape[0] * lax.axis_size(ROWS)
    loss_scale = 1.0 / tokens**0.5
    gain = scale.astype(f32)
    rank = up.shape[0]
    width = target.shape[1]

    up_high, up_low = split(up.astype(f32) * gain)
    weights = jnp.concatenate(
        [
            dot(up_high, value_matrix) + dot(up_low, value_matrix),
            dot(up, up, NT),
            jnp.zeros((rank, rank), f32),
        ],
        axis=1,
    )
    columns = weights.shape[1]

    wide = resid.astype(f32)
    part = jnp.concatenate(
        [
            dot((wide * gain).astype(bf16), value_matrix),
            dot(heads, down_matrix),
            dot(resid, up, NT),
        ],
        axis=1,
    )
    squares = jnp.sum(wide * wide, axis=1).reshape(tp, 1, share)
    tail = jnp.concatenate(split(squares), axis=1)
    tail = jnp.pad(tail, ((0, 0), (0, 14), (0, columns - share)))
    pieces = jnp.concatenate(
        [
            part.astype(bf16).reshape(tp, share, columns),
            jnp.broadcast_to(weights.astype(bf16), (tp, rank, columns)),
            tail,
        ],
        axis=1,
    )
    pieces = lax.all_to_all(pieces, TP, 0, 0, tiled=True)
    total = jnp.sum(pieces.astype(f32), axis=0)
    through = split(total[share : share + rank, :width])
    gram = split(total[share : share + rank, width : width + rank])
    square_sums = total[share + rank, :share] + total[share + rank + 1, :share]

    down_b = total[:share, width : width + rank].astype(bf16)
    down_wide = down_b.astype(f32)
    along = total[:share, width + rank :]
    hidden_up = along + 0.5 * dot_split(down_b, gram)
    square_sums = square_sums + 0.5 * jnp.sum(down_wide * (along + hidden_up), axis=1)
    inverse_rms = lax.rsqrt(square_sums / MODEL_WIDTH + EPSILON)[:, None]
    sums = inverse_rms * (total[:share, :width] + 0.5 * dot_split(down_b, through))
    error = ((sums - target.astype(f32)) * loss_scale).astype(bf16)
    error_wide = error.astype(f32)
    inner = jnp.sum(error_wide * sums, axis=1, keepdims=True) / MODEL_WIDTH
    down_grad = 0.5 * inverse_rms * (dot_split(error, through, NT) - inner * inverse_rms * hidden_up)
    sent = jnp.concatenate(
        [
            error_wide * inverse_rms,
            down_wide,
            down_grad,
            down_wide * (inner * inverse_rms * inverse_rms),
        ],
        axis=1,
    ).astype(bf16)
    every = lax.all_to_all(jnp.broadcast_to(sent, (tp, *sent.shape)), TP, 0, 0, tiled=True)
    every = every.reshape(tp * share, -1)

    error_all = every[:, :width]
    down_all = every[:, width : width + rank]
    grad_all = every[:, width + rank : width + 2 * rank]
    weighted_all = every[:, width + 2 * rank :]
    hidden = (wide + 0.5 * dot(down_all, up)).astype(bf16)
    value_part = dot(hidden, error_all, TN)
    a_part = dot(heads, grad_all, TN)
    cross = split(dot(error_all, down_all, TN))
    b_part = 0.5 * (gain[:, None] * dot_split(value_matrix, cross) - dot(hidden, weighted_all, TN))
    part = jnp.concatenate([value_part, a_part, b_part], axis=1)

    blocks = [lax.axis_size(a) for a in ROWS]
    own = part.shape[0] // (blocks[0] * blocks[1] * blocks[2])
    part = part.reshape(*blocks, own, columns)
    part = pair_sum(part, "core", 2)
    part = pair_sum(part, "y_hi", 0)
    part = lax.all_to_all(part.astype(bf16), "z", 0, 0, tiled=True)
    part = jnp.sum(part.astype(f32), axis=0)

    first = lax.axis_index(ROWS) * own
    own_gain = lax.dynamic_slice_in_dim(gain, first, own, 0)
    own_matrix = lax.dynamic_slice_in_dim(value_matrix, first, own, 0).astype(f32)
    value_grad = (part[:, :width] * own_gain[:, None]).astype(bf16)
    gain_part = jnp.sum(part[:, :width] * own_matrix, axis=1)

    small = jnp.concatenate(
        [part[:, width:], jnp.pad(gain_part[None, :], ((0, 7), (0, 2 * rank - own)))], axis=0
    )
    small = pair_gather(small, "y_hi")
    small = lax.all_to_all(
        jnp.broadcast_to(small, (blocks[1], *small.shape)), "z", 0, 0, tiled=True
    )
    small = pair_gather(small, "core")
    small = small.transpose(2, 1, 0, 3, 4)
    a_b = small[:, :, :, :own].reshape(-1, 2 * rank)
    gain_grad = small[:, :, :, own, :own].reshape(-1)
    return (sums.astype(bf16), value_grad, a_b[:, :rank], a_b[:, rank:].T, gain_grad)


def swap(x, axis):
    return lax.ppermute(x, axis, [(0, 1), (1, 0)])


def pair_sum(x, axis, dim):
    me = lax.axis_index(axis)
    mine = lax.dynamic_index_in_dim(x, me, dim, keepdims=False)
    other = lax.dynamic_index_in_dim(x, 1 - me, dim, keepdims=False)
    return mine.astype(f32) + swap(other.astype(bf16), axis).astype(f32)


def pair_gather(x, axis):
    me = lax.axis_index(axis)
    other = swap(x, axis)
    first = me == 0
    return jnp.stack([jnp.where(first, x, other), jnp.where(first, other, x)])


def solution(mesh):
    rows, tp = mesh.shape["rows"], mesh.shape["tp"]
    y_hi, core, y_lo = 2, 2, 2
    fine = Mesh(
        mesh.devices.reshape(y_hi, rows // (y_hi * core), core, tp // y_lo, y_lo), (*ROWS, *TP)
    )
    in_specs = (
        P(ROWS, TP),
        P(ROWS, TP),
        P(TP, None),
        P(None, TP),
        P(TP),
        P(TP, None),
        P((*ROWS, *TP), None),
    )
    out_specs = (
        P((*ROWS, *TP), None),
        P((*TP, *ROWS), None),
        P(TP, None),
        P(None, TP),
        P(TP),
    )
    return jax.shard_map(body, mesh=fine, in_specs=in_specs, out_specs=out_specs, check_vma=False)
```

time: 955 us -> 183 us (0.19)
  waiting for transfers between devices: 643 us -> 39.3 us
  blocking collectives: 259 us -> 55.3 us
  starting transfers between devices: 0.12 us -> 46.6 us
  between operations: 13.8 us -> 0.99 us
    psum x2 -> x0, waiting for transfers between devices: 642 us -> none  [the longest x1 529 us: body(): a_grad, b_grad, gain_grad = lax.psum((a_grad, b_grad, gain_grad), 'rows')]
    psum x5 -> x0, blocking collectives: 235 us -> none  [the longest x1 149 us: body(): a_grad, b_grad, gain_grad = lax.psum((a_grad, b_grad, gain_grad), 'rows')]
    all_to_all x0 -> x2, blocking collectives: none -> 55.3 us  [the longest x1 29.9 us: body(): lax.all_to_all(jnp.broadcast_to(small, (blocks[1], *small.shape)), 'z', 0...]
    ppermute x0 -> x4, starting transfers between devices: none -> 27.3 us  [swap(): return lax.ppermute(x, axis, [(0, 1), (1, 0)])]
    all_to_all x0 -> x2, waiting for transfers between devices: none -> 26.7 us  [the longest x1 13.5 us: body(): part = lax.all_to_all(part.astype(bf16), 'z', 0, 0, tiled=True)]
    all_gather x1 -> x0, blocking collectives: 24.2 us -> none  [body(): errors_all = lax.all_gather(value_error, 'tp', axis=0, tiled=True)]
    all_to_all x0 -> x2, starting transfers between devices: none -> 19.2 us  [the longest x1 15 us: body(): part = lax.all_to_all(part.astype(bf16), 'z', 0, 0, tiled=True)]
    ppermute x0 -> x4, waiting for transfers between devices: none -> 12.6 us  [swap(): return lax.ppermute(x, axis, [(0, 1), (1, 0)])]
  transfers between devices with their start and end apart: 3 -> 6, of which waited for: 3 -> 6; matrix products, arithmetic and copies ran while one was open for 2% -> 0% of each run, Pallas kernels for 0% -> 0%
where the time goes in v1:
time: 183 us; the launch traced here: 182 us
  blocking collectives  55.3 us (30%)
  starting transfers between devices  46.6 us (25%)
  waiting for transfers between devices  39.3 us (21%)
  matrix products  18.4 us (10%)
  local copies, waits for them, and re-layouts  11.4 us (6%)
  other arithmetic  9.98 us (5%)
    all_to_all x1, blocking collectives, body(): lax.all_to_all(jnp.broadcast_to(small, (blocks[1], *small.shape)), 'z', 0...  29.9 us
    ppermute x4, starting transfers between devices, swap(): return lax.ppermute(x, axis, [(0, 1), (1, 0)])  27.3 us
    all_to_all x1, blocking collectives, body(): pieces = lax.all_to_all(pieces, TP, 0, 0, tiled=True)  25.4 us
    dot_general x19, matrix products, dot(): return lax.dot_general(a, b, dims, preferred_element_type=f32)  18.4 us
    all_to_all x1, starting transfers between devices, body(): part = lax.all_to_all(part.astype(bf16), 'z', 0, 0, tiled=True)  15 us
    all_to_all x1, waiting for transfers between devices, body(): part = lax.all_to_all(part.astype(bf16), 'z', 0, 0, tiled=True)  13.5 us
    all_to_all x1, waiting for transfers between devices, body(): lax.all_to_all(jnp.broadcast_to(sent, (tp, *sent.shape)), TP, 0, 0, tiled...  13.2 us
    ppermute x4, waiting for transfers between devices, swap(): return lax.ppermute(x, axis, [(0, 1), (1, 0)])  12.6 us
  transfers between devices with their start and end apart: 6, of which 6 were waited for; matrix products, arithmetic and copies ran while one was open for 0% of the time, Pallas kernels for 0%

profile of v1, /device:TPU:1, one launch (start us, length us, event | category | flops | bytes accessed | tf_op | source)
XLA Modules:
  0.0 181.8 jit_solution(11925253192158899982)
XLA Ops:
  0.6 0.8 convert_element_type.119
  1.4 1.1 convolution_convert_fusion.2
  2.6 1.6 fusion.40
  4.2 3.7 %fusion.8 = bf16[768,512]{1,0:T(8,128)(2,1)} fusion(bf16[1024,512]{1,0:T(8,128)(2,1)} %param.12, bf16[768,1024]{1,0:T(8,128)(2,1)} %param.7, f32[1024]{0:T(1024)S(1)} %convert_element_type.119), kind=kOutput, calls=%fused_computation.13 | convolution fusion | flops 808058880 | bytes 3411968 | tf_op jit(solution)/shard_map/dot_general | solution.py:15
  7.9 0.4 fusion.2
  8.3 0.6 convolution_convert_fusion
  8.9 0.2 copy-done.1
  9.1 0.3 fusion.17
  9.6 0.6 convolution_convert_fusion.1
  10.7 1.4 fusion.4
  12.0 25.4 %all_to_all.20 = bf16[8,176,640]{2,1,0:T(8,128)(2,1)S(1)} all-to-all(bf16[8,176,640]{2,1,0:T(8,128)(2,1)S(1)} %fusion.4), channel_id=1, replica_groups=mesh['y_hi'=2,'z'=16,'core'=2,'x'=4,'y_lo'=2] {'x','y_lo'}, dimensions={0} | all-to-all | bytes 3604480 | tf_op jit(solution)/shard_map/all_to_all | solution.py:71
  37.4 0.2 convert_reduce_fusion
  38.0 0.2 fusion.45
  38.3 0.2 fusion.31
  38.7 0.8 fusion.32
  39.8 1.1 broadcast_in_dim.23
  40.9 4.2 %all-to-all-start.1 = ((bf16[8,96,704]{2,1,0:T(8,128)(2,1)}), bf16[8,96,704]{2,1,0:T(8,128)(2,1)}, u32[]{:S(2)}, u32[]{:S(2)}) async-start(bf16[8,96,704]{2,1,0:T(8,128)(2,1)} %broadcast_in_dim.23), calls=%async_computation.1 | async-start | bytes 2359296 | tf_op jit(solution)/shard_map/all_to_all | solution.py:97
  45.2 13.2 %all-to-all-done.1 = bf16[8,96,704]{2,1,0:T(8,128)(2,1)} async-done(((bf16[8,96,704]{2,1,0:T(8,128)(2,1)}), bf16[8,96,704]{2,1,0:T(8,128)(2,1)}, u32[]{:S(2)}, u32[]{:S(2)}) %all-to-all-start.1) | async-done | bytes 1081376 | tf_op jit(solution)/shard_map/all_to_all | solution.py:97
  58.4 2.1 %fusion.3 = bf16[768,1024]{1,0:T(8,128)(2,1)S(1)} fusion(bf16[768,1024]{1,0:T(8,128)(2,1)} %param.7, bf16[64,1024]{1,0:T(8,128)(2,1)S(1)} %copy-done.3, bf16[768,704]{1,0:T(8,128)(2,1)} %bitcast.4), kind=kOutput, calls=%fused_computation.8 | convolution fusion | flops 103809024 | bytes 3473408 | tf_op jit(solution)/shard_map/dot_general | solution.py:15
  60.5 1.5 fusion.23
  61.9 1.4 convolution_bitcast_fusion
  63.4 2.2 %fusion.25 = f32[1024,512]{0,1:T(8,128)S(1)} fusion(bf16[768,1024]{1,0:T(8,128)(2,1)S(1)} %fusion.3, bf16[768,704]{1,0:T(8,128)(2,1)} %bitcast.4), kind=kOutput, calls=%fused_computation.41 | convolution fusion | flops 805306368 | bytes 4456448 | tf_op jit(solution)/shard_map/dot_general | solution.py:15
  65.5 0.4 fusion.44
  66.0 0.5 fusion.13
  66.4 1.4 fusion.11
  67.8 1.7 pad_maximum_fusion
  69.5 3.2 %copy.53 = f32[1024,640]{1,0:T(8,128)} copy(f32[1024,640]{0,1:T(8,128)} %pad_maximum_fusion) | data formatting | bytes 5242880 | tf_op jit(solution)/shard_map/concatenate | solution.py:109
  72.7 1.4 fusion.27
  74.1 6.9 %collective-permute-start = (bf16[2,16,16,640]{3,2,1,0:T(8,128)(2,1)S(1)}, bf16[2,16,16,640]{3,2,1,0:T(8,128)(2,1)}, u32[]{:S(2)}, u32[]{:S(2)}) collective-permute-start(bf16[2,16,16,640]{3,2,1,0:T(8,128)(2,1)S(1)} %fusion.27), channel_id=1, source_target_pairs={{0,8},{8,0},{1,9},{9,1},{2,10},{10,2},{3,11},{11,3},{4,12},{12,4},... | collective-permute-start | bytes 1966088 | tf_op jit(solution)/shard_map/ppermute | solution.py:140
  81.0 1.8 %collective-permute-done = bf16[2,16,16,640]{3,2,1,0:T(8,128)(2,1)} collective-permute-done((bf16[2,16,16,640]{3,2,1,0:T(8,128)(2,1)S(1)}, bf16[2,16,16,640]{3,2,1,0:T(8,128)(2,1)}, u32[]{:S(2)}, u32[]{:S(2)}) %collective-permute-start) | collective-permute-done | bytes 655392 | tf_op jit(solution)/shard_map/ppermute | solution.py:140
  82.8 1.6 bitcast_add_fusion
  84.5 1.1 copy-done.4
  85.6 7.3 %collective-permute-start.1 = (bf16[16,16,640]{2,1,0:T(8,128)(2,1)S(1)}, bf16[16,16,640]{2,1,0:T(8,128)(2,1)S(1)}, u32[]{:S(2)}, u32[]{:S(2)}) collective-permute-start(bf16[16,16,640]{2,1,0:T(8,128)(2,1)S(1)} %fusion.29), channel_id=1, source_target_pairs={{0,256},{256,0},{1,257},{257,1},{2,258},{258,2},{3,259},{259,3},{4... | collective-permute-start | bytes 983048 | tf_op jit(solution)/shard_map/ppermute | solution.py:140
  92.8 7.8 %collective-permute-done.1 = bf16[16,16,640]{2,1,0:T(8,128)(2,1)S(1)} collective-permute-done((bf16[16,16,640]{2,1,0:T(8,128)(2,1)S(1)}, bf16[16,16,640]{2,1,0:T(8,128)(2,1)S(1)}, u32[]{:S(2)}, u32[]{:S(2)}) %collective-permute-start.1) | collective-permute-done | bytes 327712 | tf_op jit(solution)/shard_map/ppermute | solution.py:140
  100.6 1.9 %fusion.28 = bf16[16,16,640]{2,1,0:T(8,128)(2,1)} fusion(bf16[16,16,640]{2,1,0:T(8,128)(2,1)S(1)} %collective-permute-done.1, f32[2,16,16,640]{3,2,1,0:T(8,128)} %copy-done.4, s32[]{:T(128)S(6)} %select_n.44), kind=kLoop, calls=%fused_computation.45 | loop fusion | flops 491520 | bytes 1310724 | tf_op jit(solution)/shard_map/convert_element_type | solution.py:116
  102.5 15.0 %all-to-all-start.2 = ((bf16[16,16,640]{2,1,0:T(8,128)(2,1)}), bf16[16,16,640]{2,1,0:T(8,128)(2,1)S(1)}, u32[]{:S(2)}, u32[]{:S(2)}) async-start(bf16[16,16,640]{2,1,0:T(8,128)(2,1)} %fusion.28), calls=%async_computation.2 | async-start | bytes 655360 | tf_op jit(solution)/shard_map/all_to_all | solution.py:116
  117.5 0.8 dynamic_slice.24
  118.2 13.5 %all-to-all-done.2 = bf16[16,16,640]{2,1,0:T(8,128)(2,1)S(1)} async-done(((bf16[16,16,640]{2,1,0:T(8,128)(2,1)}), bf16[16,16,640]{2,1,0:T(8,128)(2,1)S(1)}, u32[]{:S(2)}, u32[]{:S(2)}) %all-to-all-start.2) | async-done | bytes 327712 | tf_op jit(solution)/shard_map/all_to_all | solution.py:116
  131.8 0.8 multiply_reduce_fusion
  132.6 4.5 %collective-permute-start.2 = (f32[24,128]{1,0:T(8,128)S(1)}, f32[24,128]{1,0:T(8,128)S(1)}, u32[]{:S(2)}, u32[]{:S(2)}) collective-permute-start(f32[24,128]{1,0:T(8,128)S(1)} %select_maximum_fusion), channel_id=1, source_target_pairs={{0,256},{256,0},{1,257},{257,1},{2,258},{258,2},{3,259},{259,3},{4... | collective-permute-start | bytes 36872 | tf_op jit(solution)/shard_map/ppermute | solution.py:140
  137.1 1.7 collective-permute-done.2
  138.9 29.9 %all_to_all.21 = f32[16,2,24,128]{3,2,1,0:T(8,128)S(1)} all-to-all(f32[16,2,24,128]{3,2,1,0:T(8,128)S(1)} %broadcast_in_dim.25), channel_id=1, replica_groups=mesh['y_hi'=2,'z'=16,'core'=2,'x'=4,'y_lo'=2] {'z'}, dimensions={0} | all-to-all | bytes 786432 | tf_op jit(solution)/shard_map/all_to_all | solution.py:129
  168.8 8.7 %collective-permute-start.3 = (f32[16,2,24,128]{3,2,0,1:T(8,128)S(1)}, f32[16,2,24,128]{3,2,0,1:T(8,128)S(1)}, u32[]{:S(2)}, u32[]{:S(2)}) collective-permute-start(f32[16,2,24,128]{3,2,0,1:T(8,128)S(1)} %copy.55), channel_id=1, source_target_pairs={{0,8},{8,0},{1,9},{9,1},{2,10},{10,2},{3,11},{11,3},{4,12},{12,4},... | collective-permute-start | bytes 1179656 | tf_op jit(solution)/shard_map/ppermute | solution.py:140
  177.6 1.3 collective-permute-done.3
  179.2 0.2 slice_bitcast_fusion
  179.4 0.9 copy.58
  180.3 0.9 copy.59
  181.2 0.7 reshape_squeeze.3
  (43 shorter events, 2.0 us)
Async XLA Ops:
  0.6 8.9 %copy-start = (bf16[768,1024]{1,0:T(8,128)(2,1)S(1)}, bf16[768,1024]{1,0:T(8,128)(2,1)}, u32[]{:S(2)}) copy-start(bf16[768,1024]{1,0:T(8,128)(2,1)} %param.8) | copy-start | bytes 4718596
  4.2 3.7 %copy-start.2 = (bf16[768,1024]{1,0:T(8,128)(2,1)S(1)}, bf16[768,1024]{1,0:T(8,128)(2,1)}, u32[]{:S(2)}) copy-start(bf16[768,1024]{1,0:T(8,128)(2,1)} %param.7) | copy-start | bytes 4718596
  4.2 4.1 %copy-start.3 = (bf16[64,1024]{1,0:T(8,128)(2,1)S(1)}, bf16[64,1024]{1,0:T(8,128)(2,1)}, u32[]{:S(2)}) copy-start(bf16[64,1024]{1,0:T(8,128)(2,1)} %param.10) | copy-start | bytes 393220
  7.9 1.2 copy-start.1
  8.3 1.2 copy-start.5
  37.4 0.9 copy-start.6
  40.9 17.4 %all-to-all-start.1 = ((bf16[8,96,704]{2,1,0:T(8,128)(2,1)}), bf16[8,96,704]{2,1,0:T(8,128)(2,1)}, u32[]{:S(2)}, u32[]{:S(2)}) async-start(bf16[8,96,704]{2,1,0:T(8,128)(2,1)} %broadcast_in_dim.23), calls=%async_computation.1 | async-start | bytes 2359296 | tf_op jit(solution)/shard_map/all_to_all | solution.py:97
  74.1 8.7 %collective-permute-start = (bf16[2,16,16,640]{3,2,1,0:T(8,128)(2,1)S(1)}, bf16[2,16,16,640]{3,2,1,0:T(8,128)(2,1)}, u32[]{:S(2)}, u32[]{:S(2)}) collective-permute-start(bf16[2,16,16,640]{3,2,1,0:T(8,128)(2,1)S(1)} %fusion.27), channel_id=1, source_target_pairs={{0,8},{8,0},{1,9},{9,1},{2,10},{10,2},{3,11},{11,3},{4,12},{12,4},... | collective-permute-start | bytes 1966088 | tf_op jit(solution)/shard_map/ppermute | solution.py:140
  84.5 1.1 copy-start.4
  85.6 15.0 %collective-permute-start.1 = (bf16[16,16,640]{2,1,0:T(8,128)(2,1)S(1)}, bf16[16,16,640]{2,1,0:T(8,128)(2,1)S(1)}, u32[]{:S(2)}, u32[]{:S(2)}) collective-permute-start(bf16[16,16,640]{2,1,0:T(8,128)(2,1)S(1)} %fusion.29), channel_id=1, source_target_pairs={{0,256},{256,0},{1,257},{257,1},{2,258},{258,2},{3,259},{259,3},{4... | collective-permute-start | bytes 983048 | tf_op jit(solution)/shard_map/ppermute | solution.py:140
  102.5 29.2 %all-to-all-start.2 = ((bf16[16,16,640]{2,1,0:T(8,128)(2,1)}), bf16[16,16,640]{2,1,0:T(8,128)(2,1)S(1)}, u32[]{:S(2)}, u32[]{:S(2)}) async-start(bf16[16,16,640]{2,1,0:T(8,128)(2,1)} %fusion.28), calls=%async_computation.2 | async-start | bytes 655360 | tf_op jit(solution)/shard_map/all_to_all | solution.py:116
  132.6 6.2 %collective-permute-start.2 = (f32[24,128]{1,0:T(8,128)S(1)}, f32[24,128]{1,0:T(8,128)S(1)}, u32[]{:S(2)}, u32[]{:S(2)}) collective-permute-start(f32[24,128]{1,0:T(8,128)S(1)} %select_maximum_fusion), channel_id=1, source_target_pairs={{0,256},{256,0},{1,257},{257,1},{2,258},{258,2},{3,259},{259,3},{4... | collective-permute-start | bytes 36872 | tf_op jit(solution)/shard_map/ppermute | solution.py:140
  168.8 10.0 %collective-permute-start.3 = (f32[16,2,24,128]{3,2,0,1:T(8,128)S(1)}, f32[16,2,24,128]{3,2,0,1:T(8,128)S(1)}, u32[]{:S(2)}, u32[]{:S(2)}) collective-permute-start(f32[16,2,24,128]{3,2,0,1:T(8,128)S(1)} %copy.55), channel_id=1, source_target_pairs={{0,8},{8,0},{1,9},{9,1},{2,10},{10,2},{3,11},{11,3},{4,12},{12,4},... | collective-permute-start | bytes 1179656 | tf_op jit(solution)/shard_map/ppermute | solution.py:140

commit v2 on v1

--- a/solution.py
+++ b/solution.py
@@ -81,13 +81,14 @@
     square_sums = square_sums + 0.5 * jnp.sum(down_wide * (along + hidden_up), axis=1)
     inverse_rms = lax.rsqrt(square_sums / MODEL_WIDTH + EPSILON)[:, None]
     sums = inverse_rms * (total[:share, :width] + 0.5 * dot_split(down_b, through))
-    error = ((sums - target.astype(f32)) * loss_scale).astype(bf16)
-    error_wide = error.astype(f32)
-    inner = jnp.sum(error_wide * sums, axis=1, keepdims=True) / MODEL_WIDTH
-    down_grad = 0.5 * inverse_rms * (dot_split(error, through, NT) - inner * inverse_rms * hidden_up)
+    error = (sums - target.astype(f32)) * loss_scale
+    inner = jnp.sum(error * sums, axis=1, keepdims=True) / MODEL_WIDTH
+    high, low = split(error)
+    down_grad = dot_split(high, through, NT) + dot(low, through[0], NT)
+    down_grad = 0.5 * inverse_rms * (down_grad - inner * inverse_rms * hidden_up)
     sent = jnp.concatenate(
         [
-            error_wide * inverse_rms,
+            error * inverse_rms,
             down_wide,
             down_grad,
             down_wide * (inner * inverse_rms * inverse_rms),
@@ -106,34 +107,36 @@
     a_part = dot(heads, grad_all, TN)
     cross = split(dot(error_all, down_all, TN))
     b_part = 0.5 * (gain[:, None] * dot_split(value_matrix, cross) - dot(hidden, weighted_all, TN))
-    part = jnp.concatenate([value_part, a_part, b_part], axis=1)
+    gain_part = jnp.sum(value_part * value_matrix.astype(f32), axis=1)
 
     blocks = [lax.axis_size(a) for a in ROWS]
-    own = part.shape[0] // (blocks[0] * blocks[1] * blocks[2])
-    part = part.reshape(*blocks, own, columns)
-    part = pair_sum(part, "core", 2)
-    part = pair_sum(part, "y_hi", 0)
-    part = lax.all_to_all(part.astype(bf16), "z", 0, 0, tiled=True)
-    part = jnp.sum(part.astype(f32), axis=0)
-
+    own = value_part.shape[0] // (blocks[0] * blocks[1] * blocks[2])
+    small = jnp.concatenate([a_part, b_part], axis=1).reshape(*blocks, own, 2 * rank)
+    gain_part = jnp.pad(
+        gain_part.reshape(*blocks, 1, own), ((0, 0),) * 3 + ((0, 7), (0, 2 * rank - own))
+    )
+    small = row_sum(jnp.concatenate([small, gain_part], axis=3))
+    value_part = row_sum(value_part.reshape(*blocks, own, width))
     first = lax.axis_index(ROWS) * own
     own_gain = lax.dynamic_slice_in_dim(gain, first, own, 0)
-    own_matrix = lax.dynamic_slice_in_dim(value_matrix, first, own, 0).astype(f32)
-    value_grad = (part[:, :width] * own_gain[:, None]).astype(bf16)
-    gain_part = jnp.sum(part[:, :width] * own_matrix, axis=1)
+    value_grad = (value_part * own_gain[:, None]).astype(bf16)
 
-    small = jnp.concatenate(
-        [part[:, width:], jnp.pad(gain_part[None, :], ((0, 7), (0, 2 * rank - own)))], axis=0
-    )
-    small = pair_gather(small, "y_hi")
+    small = pair_gather(small.astype(bf16), "y_hi")
     small = lax.all_to_all(
         jnp.broadcast_to(small, (blocks[1], *small.shape)), "z", 0, 0, tiled=True
     )
     small = pair_gather(small, "core")
     small = small.transpose(2, 1, 0, 3, 4)
-    a_b = small[:, :, :, :own].reshape(-1, 2 * rank)
-    gain_grad = small[:, :, :, own, :own].reshape(-1)
+    a_b = small[:, :, :, :own].reshape(-1, 2 * rank).astype(f32)
+    gain_grad = small[:, :, :, own, :own].reshape(-1).astype(f32)
     return (sums.astype(bf16), value_grad, a_b[:, :rank], a_b[:, rank:].T, gain_grad)
+
+
+def row_sum(part):
+    part = pair_sum(part, "core", 2)
+    part = pair_sum(part, "y_hi", 0)
+    part = lax.all_to_all(part.astype(bf16), "z", 0, 0, tiled=True)
+    return jnp.sum(part.astype(f32), axis=0)
 
 
 def swap(x, axis):

time: 183 us -> 171 us (0.934)
  the two profiles are of different devices: /device:TPU:1 before, /device:TPU:32 now
where the time goes in v2:
time: 171 us; the launch traced here: 170 us
  waiting for transfers between devices  53.4 us (31%)
  starting transfers between devices  50.7 us (30%)
  blocking collectives  28.6 us (17%)
  matrix products  20.6 us (12%)
  local copies, waits for them, and re-layouts  8.1 us (5%)
  other arithmetic  7.81 us (5%)
    all_to_all x1, blocking collectives, body(): pieces = lax.all_to_all(pieces, TP, 0, 0, tiled=True)  28.6 us
    all_to_all x2, waiting for transfers between devices, row_sum(): part = lax.all_to_all(part.astype(bf16), 'z', 0, 0, tiled=True)  22.9 us
    all_to_all x2, starting transfers between devices, row_sum(): part = lax.all_to_all(part.astype(bf16), 'z', 0, 0, tiled=True)  22.1 us
    dot_general x20, matrix products, dot(): return lax.dot_general(a, b, dims, preferred_element_type=f32)  20.6 us
    ppermute x6, starting transfers between devices, swap(): return lax.ppermute(x, axis, [(0, 1), (1, 0)])  20.2 us
    all_to_all x1, waiting for transfers between devices, body(): lax.all_to_all(jnp.broadcast_to(sent, (tp, *sent.shape)), TP, 0, 0, tiled...  16.2 us
    all_to_all x1, waiting for transfers between devices, body(): lax.all_to_all(jnp.broadcast_to(small, (blocks[1], *small.shape)), 'z', 0...  7.36 us
    ppermute x6, waiting for transfers between devices, swap(): return lax.ppermute(x, axis, [(0, 1), (1, 0)])  7.02 us
  transfers between devices with their start and end apart: 10, of which 7 were waited for; matrix products, arithmetic and copies ran while one was open for 5% of the time, Pallas kernels for 0%

profile of v2, /device:TPU:32, one launch (start us, length us, event | category | flops | bytes accessed | tf_op | source)
XLA Modules:
  0.0 170.3 jit_solution(12953531338747913381)
XLA Ops:
  0.6 0.8 convert_element_type.154
  1.4 1.1 convolution_convert_fusion.2
  2.6 1.6 fusion.41
  4.2 3.7 %fusion.8 = bf16[768,512]{1,0:T(8,128)(2,1)} fusion(bf16[1024,512]{1,0:T(8,128)(2,1)} %param.12, bf16[768,1024]{1,0:T(8,128)(2,1)} %param.7, f32[1024]{0:T(1024)S(1)} %convert_element_type.154), kind=kOutput, calls=%fused_computation.13 | convolution fusion | flops 808058880 | bytes 3411968 | tf_op jit(solution)/shard_map/dot_general | solution.py:15
  7.9 0.4 fusion.2
  8.3 0.6 convolution_convert_fusion
  9.1 0.3 fusion.17
  9.5 0.6 convolution_convert_fusion.1
  10.7 1.4 fusion.4
  12.0 28.6 %all_to_all.25 = bf16[8,176,640]{2,1,0:T(8,128)(2,1)S(1)} all-to-all(bf16[8,176,640]{2,1,0:T(8,128)(2,1)S(1)} %fusion.4), channel_id=1, replica_groups=mesh['y_hi'=2,'z'=16,'core'=2,'x'=4,'y_lo'=2] {'x','y_lo'}, dimensions={0} | all-to-all | bytes 3604480 | tf_op jit(solution)/shard_map/all_to_all | solution.py:71
  40.6 0.2 convert_reduce_fusion
  41.5 0.9 multiply_convert_fusion
  43.2 1.1 broadcast_in_dim.20
  44.3 4.3 %all-to-all-start.1 = ((bf16[8,96,704]{2,1,0:T(8,128)(2,1)}), bf16[8,96,704]{2,1,0:T(8,128)(2,1)}, u32[]{:S(2)}, u32[]{:S(2)}) async-start(bf16[8,96,704]{2,1,0:T(8,128)(2,1)} %broadcast_in_dim.20), calls=%async_computation.1 | async-start | bytes 2359296 | tf_op jit(solution)/shard_map/all_to_all | solution.py:98
  48.6 16.2 %all-to-all-done.1 = bf16[8,96,704]{2,1,0:T(8,128)(2,1)} async-done(((bf16[8,96,704]{2,1,0:T(8,128)(2,1)}), bf16[8,96,704]{2,1,0:T(8,128)(2,1)}, u32[]{:S(2)}, u32[]{:S(2)}) %all-to-all-start.1) | async-done | bytes 1081376 | tf_op jit(solution)/shard_map/all_to_all | solution.py:98
  64.7 1.5 fusion.23
  66.2 2.1 %fusion.3 = bf16[768,1024]{1,0:T(8,128)(2,1)S(1)} fusion(bf16[768,1024]{1,0:T(8,128)(2,1)} %param.7, bf16[64,1024]{1,0:T(8,128)(2,1)S(1)} %copy-done.3, bf16[768,704]{1,0:T(8,128)(2,1)} %bitcast.4), kind=kOutput, calls=%fused_computation.8 | convolution fusion | flops 103809024 | bytes 3473408 | tf_op jit(solution)/shard_map/dot_general | solution.py:15
  68.3 1.4 convolution_bitcast_fusion
  69.7 0.4 fusion.48
  70.1 0.5 fusion.13
  70.6 3.5 %multiply_reduce_fusion = (f32[1024]{0:T(1024)S(1)}, f32[1024,512]{1,0:T(8,128)}) fusion(bf16[1024,512]{1,0:T(8,128)(2,1)S(1)} %copy-done.1, bf16[768,1024]{1,0:T(8,128)(2,1)S(1)} %fusion.3, bf16[768,704]{1,0:T(8,128)(2,1)} %bitcast.4), kind=kOutput, calls=%fused_computation.9 | convolution fusion | flops 806878208 | bytes 5509120 | tf_op jit(solution)/shard_map/dot_general | solution.py:15
  74.1 1.4 fusion.11
  76.0 1.9 %collective-permute-start.2 = (bf16[2,16,24,128]{3,2,1,0:T(8,128)(2,1)S(1)}, bf16[2,16,24,128]{3,2,1,0:T(8,128)(2,1)S(1)}, u32[]{:S(2)}, u32[]{:S(2)}) collective-permute-start(bf16[2,16,24,128]{3,2,1,0:T(8,128)(2,1)S(1)} %fusion.32), channel_id=1, source_target_pairs={{0,8},{8,0},{1,9},{9,1},{2,10},{10,2},{3,11},{11,3},{4,12},{12,4},... | collective-permute-start | bytes 589832 | tf_op jit(solution)/shard_map/ppermute | solution.py:143
  77.9 1.4 collective-permute-done.2
  79.4 4.8 %collective-permute-start.3 = (bf16[16,24,128]{2,1,0:T(8,128)(2,1)S(1)}, bf16[16,24,128]{2,1,0:T(8,128)(2,1)S(1)}, u32[]{:S(2)}, u32[]{:S(2)}) collective-permute-start(bf16[16,24,128]{2,1,0:T(8,128)(2,1)S(1)} %fusion.44), channel_id=1, source_target_pairs={{0,256},{256,0},{1,257},{257,1},{2,258},{258,2},{3,259},{259,3},{4... | collective-permute-start | bytes 294920 | tf_op jit(solution)/shard_map/ppermute | solution.py:143
  84.2 3.4 %collective-permute-done.3 = bf16[16,24,128]{2,1,0:T(8,128)(2,1)S(1)} collective-permute-done((bf16[16,24,128]{2,1,0:T(8,128)(2,1)S(1)}, bf16[16,24,128]{2,1,0:T(8,128)(2,1)S(1)}, u32[]{:S(2)}, u32[]{:S(2)}) %collective-permute-start.3) | collective-permute-done | bytes 98336 | tf_op jit(solution)/shard_map/ppermute | solution.py:143
  87.6 0.7 fusion.35
  88.3 15.2 %all-to-all-start.3 = ((bf16[16,24,128]{2,1,0:T(8,128)(2,1)}), bf16[16,24,128]{2,1,0:T(8,128)(2,1)S(1)}, u32[]{:S(2)}, u32[]{:S(2)}) async-start(bf16[16,24,128]{2,1,0:T(8,128)(2,1)} %fusion.35), calls=%async_computation.3 | async-start | bytes 196608 | tf_op jit(solution)/shard_map/all_to_all | solution.py:138
  103.5 1.3 fusion.27
  104.8 1.9 %collective-permute-start = (bf16[2,16,16,512]{3,2,1,0:T(8,128)(2,1)S(1)}, bf16[2,16,16,512]{3,2,1,0:T(8,128)(2,1)S(1)}, u32[]{:S(2)}, u32[]{:S(2)}) collective-permute-start(bf16[2,16,16,512]{3,2,1,0:T(8,128)(2,1)S(1)} %fusion.27), channel_id=1, source_target_pairs={{0,8},{8,0},{1,9},{9,1},{2,10},{10,2},{3,11},{11,3},{4,12},{12,4},... | collective-permute-start | bytes 1572872 | tf_op jit(solution)/shard_map/ppermute | solution.py:143
  106.7 9.3 %all-to-all-done.3 = bf16[16,24,128]{2,1,0:T(8,128)(2,1)S(1)} async-done(((bf16[16,24,128]{2,1,0:T(8,128)(2,1)}), bf16[16,24,128]{2,1,0:T(8,128)(2,1)S(1)}, u32[]{:S(2)}, u32[]{:S(2)}) %all-to-all-start.3) | async-done | bytes 98336 | tf_op jit(solution)/shard_map/all_to_all | solution.py:138
  116.0 4.8 %collective-permute-start.4 = (bf16[24,128]{1,0:T(8,128)(2,1)S(1)}, bf16[24,128]{1,0:T(8,128)(2,1)S(1)}, u32[]{:S(2)}, u32[]{:S(2)}) collective-permute-start(bf16[24,128]{1,0:T(8,128)(2,1)S(1)} %reduce_sum.72), channel_id=1, source_target_pairs={{0,256},{256,0},{1,257},{257,1},{2,258},{258,2},{3,259},{259,3},{4... | collective-permute-start | bytes 18440 | tf_op jit(solution)/shard_map/ppermute | solution.py:143
  120.9 2.2 %collective-permute-done.4 = bf16[24,128]{1,0:T(8,128)(2,1)S(1)} collective-permute-done((bf16[24,128]{1,0:T(8,128)(2,1)S(1)}, bf16[24,128]{1,0:T(8,128)(2,1)S(1)}, u32[]{:S(2)}, u32[]{:S(2)}) %collective-permute-start.4) | collective-permute-done | bytes 6176 | tf_op jit(solution)/shard_map/ppermute | solution.py:143
  123.1 0.7 broadcast_in_dim.21
  123.8 4.1 %all-to-all-start.4 = ((bf16[16,2,24,128]{3,2,1,0:T(8,128)(2,1)}), bf16[16,2,24,128]{3,2,1,0:T(8,128)(2,1)S(1)}, u32[]{:S(2)}, u32[]{:S(2)}) async-start(bf16[16,2,24,128]{3,2,1,0:T(8,128)(2,1)} %broadcast_in_dim.21), calls=%async_computation.4 | async-start | bytes 393216 | tf_op jit(solution)/shard_map/all_to_all | solution.py:125
  127.9 1.4 bitcast_add_fusion
  129.4 4.8 %collective-permute-start.1 = (bf16[16,16,512]{2,1,0:T(8,128)(2,1)S(1)}, bf16[16,16,512]{2,1,0:T(8,128)(2,1)S(1)}, u32[]{:S(2)}, u32[]{:S(2)}) collective-permute-start(bf16[16,16,512]{2,1,0:T(8,128)(2,1)S(1)} %fusion.30), channel_id=1, source_target_pairs={{0,256},{256,0},{1,257},{257,1},{2,258},{258,2},{3,259},{259,3},{4... | collective-permute-start | bytes 786440 | tf_op jit(solution)/shard_map/ppermute | solution.py:143
  134.2 0.8 dynamic_slice.35
  135.0 7.4 %all-to-all-done.4 = bf16[16,2,24,128]{3,2,1,0:T(8,128)(2,1)S(1)} async-done(((bf16[16,2,24,128]{3,2,1,0:T(8,128)(2,1)}), bf16[16,2,24,128]{3,2,1,0:T(8,128)(2,1)S(1)}, u32[]{:S(2)}, u32[]{:S(2)}) %all-to-all-start.4) | async-done | bytes 196640 | tf_op jit(solution)/shard_map/all_to_all | solution.py:125
  142.4 1.9 %collective-permute-start.5 = (bf16[16,2,24,128]{3,0,2,1:T(8,128)(2,1)S(1)}, bf16[16,2,24,128]{3,0,2,1:T(8,128)(2,1)}, u32[]{:S(2)}, u32[]{:S(2)}) collective-permute-start(bf16[16,2,24,128]{3,0,2,1:T(8,128)(2,1)S(1)} %copy.74), channel_id=1, source_target_pairs={{0,8},{8,0},{1,9},{9,1},{2,10},{10,2},{3,11},{11,3},{4,12},{12,4},... | collective-permute-start | bytes 589832 | tf_op jit(solution)/shard_map/ppermute | solution.py:143
  144.3 0.8 fusion.28
  145.1 6.9 %all-to-all-start.2 = ((bf16[16,16,512]{2,1,0:T(8,128)(2,1)}), bf16[16,16,512]{2,1,0:T(8,128)(2,1)S(1)}, u32[]{:S(2)}, u32[]{:S(2)}) async-start(bf16[16,16,512]{2,1,0:T(8,128)(2,1)} %fusion.28), calls=%async_computation.2 | async-start | bytes 524288 | tf_op jit(solution)/shard_map/all_to_all | solution.py:138
  152.0 1.0 select_bitcast_fusion.1
  153.4 0.9 copy.80
  154.3 0.9 copy.81
  155.2 0.7 reshape.139
  155.9 13.6 %all-to-all-done.2 = bf16[16,16,512]{2,1,0:T(8,128)(2,1)S(1)} async-done(((bf16[16,16,512]{2,1,0:T(8,128)(2,1)}), bf16[16,16,512]{2,1,0:T(8,128)(2,1)S(1)}, u32[]{:S(2)}, u32[]{:S(2)}) %all-to-all-start.2) | async-done | bytes 262176 | tf_op jit(solution)/shard_map/all_to_all | solution.py:138
  169.6 0.7 multiply_convert_fusion.1
  (55 shorter events, 3.3 us)
Async XLA Ops:
  0.6 8.9 %copy-start = (bf16[768,1024]{1,0:T(8,128)(2,1)S(1)}, bf16[768,1024]{1,0:T(8,128)(2,1)}, u32[]{:S(2)}) copy-start(bf16[768,1024]{1,0:T(8,128)(2,1)} %param.8) | copy-start | bytes 4718596
  4.2 3.7 %copy-start.2 = (bf16[768,1024]{1,0:T(8,128)(2,1)S(1)}, bf16[768,1024]{1,0:T(8,128)(2,1)}, u32[]{:S(2)}) copy-start(bf16[768,1024]{1,0:T(8,128)(2,1)} %param.7) | copy-start | bytes 4718596
  4.2 4.1 %copy-start.3 = (bf16[64,1024]{1,0:T(8,128)(2,1)S(1)}, bf16[64,1024]{1,0:T(8,128)(2,1)}, u32[]{:S(2)}) copy-start(bf16[64,1024]{1,0:T(8,128)(2,1)} %param.10) | copy-start | bytes 393220
  7.9 1.2 copy-start.1
  8.3 1.2 copy-start.5
  40.6 0.9 copy-start.4
  44.3 20.4 %all-to-all-start.1 = ((bf16[8,96,704]{2,1,0:T(8,128)(2,1)}), bf16[8,96,704]{2,1,0:T(8,128)(2,1)}, u32[]{:S(2)}, u32[]{:S(2)}) async-start(bf16[8,96,704]{2,1,0:T(8,128)(2,1)} %broadcast_in_dim.20), calls=%async_computation.1 | async-start | bytes 2359296 | tf_op jit(solution)/shard_map/all_to_all | solution.py:98
  76.0 3.3 %collective-permute-start.2 = (bf16[2,16,24,128]{3,2,1,0:T(8,128)(2,1)S(1)}, bf16[2,16,24,128]{3,2,1,0:T(8,128)(2,1)S(1)}, u32[]{:S(2)}, u32[]{:S(2)}) collective-permute-start(bf16[2,16,24,128]{3,2,1,0:T(8,128)(2,1)S(1)} %fusion.32), channel_id=1, source_target_pairs={{0,8},{8,0},{1,9},{9,1},{2,10},{10,2},{3,11},{11,3},{4,12},{12,4},... | collective-permute-start | bytes 589832 | tf_op jit(solution)/shard_map/ppermute | solution.py:143
  79.4 8.2 %collective-permute-start.3 = (bf16[16,24,128]{2,1,0:T(8,128)(2,1)S(1)}, bf16[16,24,128]{2,1,0:T(8,128)(2,1)S(1)}, u32[]{:S(2)}, u32[]{:S(2)}) collective-permute-start(bf16[16,24,128]{2,1,0:T(8,128)(2,1)S(1)} %fusion.44), channel_id=1, source_target_pairs={{0,256},{256,0},{1,257},{257,1},{2,258},{258,2},{3,259},{259,3},{4... | collective-permute-start | bytes 294920 | tf_op jit(solution)/shard_map/ppermute | solution.py:143
  88.3 27.8 %all-to-all-start.3 = ((bf16[16,24,128]{2,1,0:T(8,128)(2,1)}), bf16[16,24,128]{2,1,0:T(8,128)(2,1)S(1)}, u32[]{:S(2)}, u32[]{:S(2)}) async-start(bf16[16,24,128]{2,1,0:T(8,128)(2,1)} %fusion.35), calls=%async_computation.3 | async-start | bytes 196608 | tf_op jit(solution)/shard_map/all_to_all | solution.py:138
  104.8 23.1 %collective-permute-start = (bf16[2,16,16,512]{3,2,1,0:T(8,128)(2,1)S(1)}, bf16[2,16,16,512]{3,2,1,0:T(8,128)(2,1)S(1)}, u32[]{:S(2)}, u32[]{:S(2)}) collective-permute-start(bf16[2,16,16,512]{3,2,1,0:T(8,128)(2,1)S(1)} %fusion.27), channel_id=1, source_target_pairs={{0,8},{8,0},{1,9},{9,1},{2,10},{10,2},{3,11},{11,3},{4,12},{12,4},... | collective-permute-start | bytes 1572872 | tf_op jit(solution)/shard_map/ppermute | solution.py:143
  116.0 7.0 %collective-permute-start.4 = (bf16[24,128]{1,0:T(8,128)(2,1)S(1)}, bf16[24,128]{1,0:T(8,128)(2,1)S(1)}, u32[]{:S(2)}, u32[]{:S(2)}) collective-permute-start(bf16[24,128]{1,0:T(8,128)(2,1)S(1)} %reduce_sum.72), channel_id=1, source_target_pairs={{0,256},{256,0},{1,257},{257,1},{2,258},{258,2},{3,259},{259,3},{4... | collective-permute-start | bytes 18440 | tf_op jit(solution)/shard_map/ppermute | solution.py:143
  123.8 18.5 %all-to-all-start.4 = ((bf16[16,2,24,128]{3,2,1,0:T(8,128)(2,1)}), bf16[16,2,24,128]{3,2,1,0:T(8,128)(2,1)S(1)}, u32[]{:S(2)}, u32[]{:S(2)}) async-start(bf16[16,2,24,128]{3,2,1,0:T(8,128)(2,1)} %broadcast_in_dim.21), calls=%async_computation.4 | async-start | bytes 393216 | tf_op jit(solution)/shard_map/all_to_all | solution.py:125
  129.4 14.9 %collective-permute-start.1 = (bf16[16,16,512]{2,1,0:T(8,128)(2,1)S(1)}, bf16[16,16,512]{2,1,0:T(8,128)(2,1)S(1)}, u32[]{:S(2)}, u32[]{:S(2)}) collective-permute-start(bf16[16,16,512]{2,1,0:T(8,128)(2,1)S(1)} %fusion.30), channel_id=1, source_target_pairs={{0,256},{256,0},{1,257},{257,1},{2,258},{258,2},{3,259},{259,3},{4... | collective-permute-start | bytes 786440 | tf_op jit(solution)/shard_map/ppermute | solution.py:143
  142.4 9.6 %collective-permute-start.5 = (bf16[16,2,24,128]{3,0,2,1:T(8,128)(2,1)S(1)}, bf16[16,2,24,128]{3,0,2,1:T(8,128)(2,1)}, u32[]{:S(2)}, u32[]{:S(2)}) collective-permute-start(bf16[16,2,24,128]{3,0,2,1:T(8,128)(2,1)S(1)} %copy.74), channel_id=1, source_target_pairs={{0,8},{8,0},{1,9},{9,1},{2,10},{10,2},{3,11},{11,3},{4,12},{12,4},... | collective-permute-start | bytes 589832 | tf_op jit(solution)/shard_map/ppermute | solution.py:143
  145.1 24.4 %all-to-all-start.2 = ((bf16[16,16,512]{2,1,0:T(8,128)(2,1)}), bf16[16,16,512]{2,1,0:T(8,128)(2,1)S(1)}, u32[]{:S(2)}, u32[]{:S(2)}) async-start(bf16[16,16,512]{2,1,0:T(8,128)(2,1)} %fusion.28), calls=%async_computation.2 | async-start | bytes 524288 | tf_op jit(solution)/shard_map/all_to_all | solution.py:138

commit v3 on v2

v3 whole, which is shorter than its diff:
```python
import functools

import jax
import jax.numpy as jnp
from jax import lax
from jax.experimental import pallas as pl
from jax.experimental.pallas import tpu as pltpu
from jax.sharding import Mesh, PartitionSpec as P

MODEL_WIDTH = 8192
EPSILON = 1e-06
TP = ("x", "y_lo")
ROWS = ("y_hi", "z", "core")
bf16 = jnp.bfloat16
f32 = jnp.float32
NN = (((1,), (0,)), ((), ()))
NT = (((1,), (1,)), ((), ()))
TN = (((0,), (0,)), ((), ()))
VMEM_LIMIT = 48 * 2**20


def dot(a, b, dims=NN):
    return lax.dot_general(a, b, dims, preferred_element_type=f32)


def split(x):
    high = lax.reduce_precision(x, 8, 7)
    return high.astype(bf16), (x - high).astype(bf16)


def dot_split(a, b, dims=NN):
    return dot(a, b[0], dims) + dot(a, b[1], dims)


def halves(x):
    high = x.astype(bf16)
    return high, (x - high.astype(f32)).astype(bf16)


def weights_kernel(half_ref, up_ref, gain_ref, matrix_ref, out_ref):
    half = half_ref[...]
    high, low = halves(half.astype(f32) * gain_ref[...])
    width = matrix_ref.shape[1]
    out_ref[:, :width] = dot(high, matrix_ref[...]) + dot(low, matrix_ref[...])
    gram = dot(half, up_ref[...], NT)
    out_ref[:, width:] = jnp.concatenate([gram, jnp.zeros_like(gram)], axis=1)


def weight_products(half, up, gain, matrix):
    columns = matrix.shape[1] + 2 * up.shape[0]
    return pl.pallas_call(
        weights_kernel,
        out_shape=jax.ShapeDtypeStruct((half.shape[0], columns), f32),
        compiler_params=pltpu.CompilerParams(vmem_limit_bytes=VMEM_LIMIT),
        cost_estimate=pl.CostEstimate(
            flops=4 * half.size * matrix.shape[1], bytes_accessed=2 * matrix.size, transcendentals=0
        ),
    )(half, up, gain, matrix)


def project_kernel(share, resid_ref, heads_ref, gain_ref, matrix_ref, down_ref, up_ref, out_ref):
    width = matrix_ref.shape[1]
    resid = resid_ref[...]
    wide = resid.astype(f32)
    values = dot((wide * gain_ref[...]).astype(bf16), matrix_ref[...])
    small = dot(heads_ref[...], down_ref[...]) + dot(resid, up_ref[...])
    high, low = halves(wide * wide)
    ones = jnp.ones((16, wide.shape[1]), bf16)
    line = lax.broadcasted_iota(jnp.int32, (16, share), 0)
    for piece in range(out_ref.shape[0]):
        rows = slice(piece * share, (piece + 1) * share)
        out_ref[piece, :share, :width] = values[rows].astype(bf16)
        out_ref[piece, :share, width:] = small[rows].astype(bf16)
        squares = dot(ones, high[rows], NT) + dot(ones, low[rows], NT)
        first = squares.astype(bf16).astype(f32)
        tail = jnp.where(line == 0, first, jnp.where(line == 1, squares - first, 0.0))
        out_ref[piece, share:, :] = jnp.zeros((16, out_ref.shape[2]), bf16)
        out_ref[piece, share:, :share] = tail.astype(bf16)


def project(resid, heads, gain, matrix, down, up, share):
    tokens, features = resid.shape
    width = matrix.shape[1]
    pieces, group = tokens // share, 2
    rows = group * share
    whole = lambda i: (0, 0)
    return pl.pallas_call(
        functools.partial(project_kernel, share),
        grid=(pieces // group,),
        in_specs=[
            pl.BlockSpec((rows, features), lambda i: (i, 0)),
            pl.BlockSpec((rows, features), lambda i: (i, 0)),
            pl.BlockSpec((1, features), whole),
            pl.BlockSpec((features, width), whole),
            pl.BlockSpec(down.shape, whole),
            pl.BlockSpec(up.shape, whole),
        ],
        out_specs=pl.BlockSpec((group, share + 16, width + 128), lambda i: (i, 0, 0)),
        out_shape=jax.ShapeDtypeStruct((pieces, share + 16, width + 128), bf16),
        compiler_params=pltpu.CompilerParams(vmem_limit_bytes=VMEM_LIMIT),
        cost_estimate=pl.CostEstimate(
            flops=2 * tokens * features * (width + 256),
            bytes_accessed=4 * tokens * features + 2 * features * width,
            transcendentals=0,
        ),
    )(resid, heads, gain, matrix, down, up)


def gradients_kernel(
    core_ref, every_ref, resid_ref, heads_ref, up_ref, gain_ref, matrix_ref,
    value_ref, value_sent_ref, small_ref, small_sent_ref, cross_ref,
):
    width = matrix_ref.shape[1]
    rank = up_ref.shape[0]
    error = every_ref[:, :width]
    down = every_ref[:, width : width + rank]

    @pl.when(pl.program_id(0) == 0)
    def _():
        high, low = halves(dot(error, down, TN))
        cross_ref[0] = high
        cross_ref[1] = low

    core = core_ref[0]
    matrix = matrix_ref[...]
    hidden = (resid_ref[...].astype(f32) + 0.5 * dot(down, up_ref[...])).astype(bf16)
    value = dot(hidden, error, TN)
    a_part = dot(heads_ref[...], every_ref[:, width + rank : width + 2 * rank], TN)
    b_part = dot(hidden, every_ref[:, width + 2 * rank :], TN)
    crossed = dot(matrix, cross_ref[0]) + dot(matrix, cross_ref[1])
    b_part = 0.5 * (gain_ref[...] * crossed - b_part)
    small = jnp.concatenate([a_part, b_part], axis=1)
    gain_part = jnp.sum(value * matrix.astype(f32), axis=1, keepdims=True)
    pieces, own = 2 * value_ref.shape[0], value_ref.shape[1]
    lane = lax.broadcasted_iota(jnp.int32, small.shape, 1)
    line = lax.rem(lax.broadcasted_iota(jnp.int32, small.shape, 0), own)
    spread = jnp.where(lane == line, gain_part, 0.0).reshape(pieces, own, -1)
    gain_row = jnp.sum(spread, axis=1, keepdims=True)
    row = lax.broadcasted_iota(jnp.int32, (pieces // 2, 16, small.shape[1]), 1)

    value = value.reshape(pieces // 2, 2, own, width)
    small = small.reshape(pieces // 2, 2, own, -1)
    gain_row = gain_row.reshape(pieces // 2, 2, 1, -1)
    first = core == 0
    value_ref[...] = jnp.where(first, value[:, 0], value[:, 1]).astype(bf16)
    value_sent_ref[...] = jnp.where(first, value[:, 1], value[:, 0]).astype(bf16)
    small_ref[:, :own] = jnp.where(first, small[:, 0], small[:, 1])
    small_sent_ref[:, :own] = jnp.where(first, small[:, 1], small[:, 0]).astype(bf16)
    kept = jnp.where(first, gain_row[:, 0], gain_row[:, 1])
    sent = jnp.where(first, gain_row[:, 1], gain_row[:, 0])
    small_ref[:, own:] = jnp.where(row == 0, kept, 0.0)
    small_sent_ref[:, own:] = jnp.where(row == 0, sent, 0.0).astype(bf16)


def gradients(core, every, resid, heads, up, gain, matrix, own):
    tokens, features = resid.shape
    width, rank = matrix.shape[1], up.shape[0]
    block = 256
    pieces, group = features // (2 * own), block // (2 * own)
    value = jax.ShapeDtypeStruct((pieces, own, width), bf16)
    small = jax.ShapeDtypeStruct((pieces, own + 16, 2 * rank), f32)
    small_sent = jax.ShapeDtypeStruct((pieces, own + 16, 2 * rank), bf16)
    return pl.pallas_call(
        gradients_kernel,
        grid=(features // block,),
        in_specs=[
            pl.BlockSpec(memory_space=pltpu.SMEM),
            pl.BlockSpec(every.shape, lambda i: (0, 0)),
            pl.BlockSpec((tokens, block), lambda i: (0, i)),
            pl.BlockSpec((tokens, block), lambda i: (0, i)),
            pl.BlockSpec((rank, block), lambda i: (0, i)),
            pl.BlockSpec((block, 1), lambda i: (i, 0)),
            pl.BlockSpec((block, width), lambda i: (i, 0)),
        ],
        out_specs=[
            pl.BlockSpec((group, own, width), lambda i: (i, 0, 0)),
            pl.BlockSpec((group, own, width), lambda i: (i, 0, 0)),
            pl.BlockSpec((group, own + 16, 2 * rank), lambda i: (i, 0, 0)),
            pl.BlockSpec((group, own + 16, 2 * rank), lambda i: (i, 0, 0)),
        ],
        out_shape=[value, value, small, small_sent],
        scratch_shapes=[pltpu.VMEM((2, width, rank), bf16)],
        compiler_params=pltpu.CompilerParams(vmem_limit_bytes=VMEM_LIMIT),
        cost_estimate=pl.CostEstimate(
            flops=2 * tokens * features * (width + 4 * rank),
            bytes_accessed=4 * tokens * features + 8 * features * width,
            transcendentals=0,
        ),
    )(core, every, resid, heads, up, gain, matrix)


def body(resid, heads, down_matrix, up, scale, value_matrix, target):
    share, width = target.shape
    tp = resid.shape[0] // share
    tokens = resid.shape[0] * lax.axis_size(ROWS)
    loss_scale = 1.0 / tokens**0.5
    rank, features = up.shape
    core = lax.axis_index("core")
    gain = scale.astype(f32)

    half = lax.dynamic_slice_in_dim(up, core * (rank // 2), rank // 2, 0)
    weights = weight_products(half, up, gain[None, :], value_matrix)
    weights = weights + swap(weights, "y_lo")

    pieces = project(
        resid,
        heads,
        gain[None, :],
        value_matrix,
        jnp.pad(down_matrix, ((0, 0), (0, rank))),
        jnp.pad(up.T, ((0, 0), (rank, 0))),
        share,
    )
    pieces = lax.all_to_all(pieces, TP, 0, 0, tiled=True)
    for distance in (1, 2):
        weights = weights + swap(weights, "x", distance)
    weights = pair_gather(weights, "core").reshape(rank, -1)
    through = split(weights[:, :width])
    gram = split(weights[:, width : width + rank])
    total = jnp.sum(pieces.astype(f32), axis=0)
    square_sums = total[share, :share] + total[share + 1, :share]

    down_b = total[:share, width : width + rank].astype(bf16)
    down_wide = down_b.astype(f32)
    along = total[:share, width + rank :]
    hidden_up = along + 0.5 * dot_split(down_b, gram)
    square_sums = square_sums + 0.5 * jnp.sum(down_wide * (along + hidden_up), axis=1)
    inverse_rms = lax.rsqrt(square_sums / MODEL_WIDTH + EPSILON)[:, None]
    sums = inverse_rms * (total[:share, :width] + 0.5 * dot_split(down_b, through))
    error = (sums - target.astype(f32)) * loss_scale
    inner = jnp.sum(error * sums, axis=1, keepdims=True) / MODEL_WIDTH
    high, low = split(error)
    down_grad = dot_split(high, through, NT) + dot(low, through[0], NT)
    down_grad = 0.5 * inverse_rms * (down_grad - inner * inverse_rms * hidden_up)
    sent = jnp.concatenate(
        [
            error * inverse_rms,
            down_wide,
            down_grad,
            down_wide * (inner * inverse_rms * inverse_rms),
        ],
        axis=1,
    ).astype(bf16)
    every = lax.all_to_all(jnp.broadcast_to(sent, (tp, *sent.shape)), TP, 0, 0, tiled=True)
    every = every.reshape(tp * share, -1)

    y_size, z_size, core_size = (lax.axis_size(a) for a in ROWS)
    own = features // (y_size * z_size * core_size)
    value, value_sent, small, small_sent = gradients(
        core.reshape(1), every, resid, heads, up, gain[:, None], value_matrix, own
    )

    rows = own + 8
    small_got = swap(small_sent, "core")
    value_got = swap(value_sent, "core")
    small = (small[:, :rows] + small_got[:, :rows].astype(f32)).astype(bf16)
    small = small.reshape(y_size, z_size, rows, -1).transpose(1, 0, 2, 3)
    small, value, value_got = lax.optimization_barrier((small, value, value_got))
    small = lax.all_to_all(small, "z", 0, 0, tiled=True)

    me = lax.axis_index("y_hi")
    value = value.reshape(y_size, z_size, own, width)
    value_got = value_got.reshape(y_size, z_size, own, width)
    pick = lambda x, i: lax.dynamic_index_in_dim(x, i, 0, keepdims=False).astype(f32)
    other = swap((pick(value, 1 - me) + pick(value_got, 1 - me)).astype(bf16), "y_hi")
    value = (pick(value, me) + pick(value_got, me) + other.astype(f32)).astype(bf16)
    small, value = lax.optimization_barrier((small, value))
    small = jnp.sum(small.astype(f32), axis=0)
    small = (small + swap(small, "y_hi")).astype(bf16)

    small = jnp.broadcast_to(small.reshape(1, own, -1), (z_size, own, y_size * rows * 2 * rank // own))
    value = lax.all_to_all(jnp.concatenate([value, small], axis=2), "z", 0, 0, tiled=True)
    small = pair_gather(value[:, :, width:], "core")
    small = small.reshape(core_size, z_size, y_size, rows, 2 * rank).transpose(2, 1, 0, 3, 4)
    a_b = small[:, :, :, :own].reshape(-1, 2 * rank).astype(f32)
    gain_grad = small[:, :, :, own, :own].reshape(-1).astype(f32)

    value = jnp.sum(value[:, :, :width].astype(f32), axis=0)
    own_gain = lax.dynamic_slice_in_dim(gain, lax.axis_index(ROWS) * own, own, 0)
    value_grad = (value * own_gain[:, None]).astype(bf16)
    return (sums.astype(bf16), value_grad, a_b[:, :rank], a_b[:, rank:].T, gain_grad)


def swap(x, axis, distance=1):
    return lax.ppermute(x, axis, [(i, i ^ distance) for i in range(lax.axis_size(axis))])


def pair_gather(x, axis):
    me = lax.axis_index(axis)
    other = swap(x, axis)
    first = me == 0
    return jnp.stack([jnp.where(first, x, other), jnp.where(first, other, x)])


def solution(mesh):
    rows, tp = mesh.shape["rows"], mesh.shape["tp"]
    y_hi, core, y_lo = 2, 2, 2
    fine = Mesh(
        mesh.devices.reshape(y_hi, rows // (y_hi * core), core, tp // y_lo, y_lo), (*ROWS, *TP)
    )
    in_specs = (
        P(ROWS, TP),
        P(ROWS, TP),
        P(TP, None),
        P(None, TP),
        P(TP),
        P(TP, None),
        P((*ROWS, *TP), None),
    )
    out_specs = (
        P((*ROWS, *TP), None),
        P((*TP, *ROWS), None),
        P(TP, None),
        P(None, TP),
        P(TP),
    )
    return jax.shard_map(body, mesh=fine, in_specs=in_specs, out_specs=out_specs, check_vma=False)
```

time: 171 us -> 168 us (0.982)
  the two profiles are of different devices: /device:TPU:32 before, /device:TPU:1 now
where the time goes in v3:
time: 168 us; the launch traced here: 167 us
  starting transfers between devices  79.6 us (47%)
  waiting for transfers between devices  59.4 us (35%)
  local copies, waits for them, and re-layouts  11.3 us (7%)
  Pallas kernels  10.6 us (6%)
  other arithmetic  3.13 us (2%)
  matrix products  1.95 us (1%)
    ppermute x9, starting transfers between devices, swap(): lax.ppermute(x, axis, [(i, i ^ distance) for i in range(lax.axis_size(axi...  46.3 us
    ppermute x9, waiting for transfers between devices, swap(): lax.ppermute(x, axis, [(i, i ^ distance) for i in range(lax.axis_size(axi...  22.2 us
    all_to_all x1, waiting for transfers between devices, body(): lax.all_to_all(jnp.concatenate([value, small], axis=2), 'z', 0, 0, tiled=...  17.5 us
    all_to_all x1, waiting for transfers between devices, body(): lax.all_to_all(jnp.broadcast_to(sent, (tp, *sent.shape)), TP, 0, 0, tiled...  17.5 us
    all_to_all x1, starting transfers between devices, body(): small = lax.all_to_all(small, 'z', 0, 0, tiled=True)  14.5 us
    all_to_all x1, starting transfers between devices, body(): lax.all_to_all(jnp.concatenate([value, small], axis=2), 'z', 0, 0, tiled=...  9.01 us
    unnamed x14, local copies, waits for them, and re-layouts  6.9 us
    pallas_call x1, Pallas kernels, gradients(): pl.pallas_call(gradients_kernel, grid=(features // block,), in_specs=[pl....  6.25 us
  transfers between devices with their start and end apart: 13, of which 11 were waited for; matrix products, arithmetic and copies ran while one was open for 2% of the time, Pallas kernels for 0%

profile of v3, /device:TPU:1, one launch (start us, length us, event | category | flops | bytes accessed | tf_op | source)
XLA Modules:
  0.0 167.0 jit_solution(16732201290642200564)
XLA Ops:
  0.6 0.8 convert_element_type.97
  1.4 1.1 copy.56
  2.5 1.1 copy.57
  3.8 1.4 copy-done.1
  5.2 1.4 copy-done.2
  6.6 3.8 %shard_map.110 = bf16[8,112,640]{2,1,0:T(8,128)(2,1)} custom-call(bf16[768,1024]{1,0:T(8,128)(2,1)S(1)} %copy-done.1, bf16[768,1024]{1,0:T(8,128)(2,1)S(1)} %copy-done.2, f32[1,1024]{1,0:T(1,128)S(1)} %bitcast.39, bf16[1024,512]{1,0:T(8,128)(2,1)S(1)} %copy-done, bf16[1024,128]{1,0:T(8,128)(2,1)S(1)} %pad.8.down_ref, bf16[1024,128]{1,0:T(8,128)(2,1)S(1)} %pad.9.up_ref), custom_call_target="tpu_custom_call" | custom-call | flops 1207959552 | bytes 4194304 | tf_op jit(solution)/shard_map/pallas_call | solution.py:87
  10.5 6.0 %all-to-all-start = ((bf16[8,112,640]{2,1,0:T(8,128)(2,1)}), bf16[8,112,640]{2,1,0:T(8,128)(2,1)S(1)}, u32[]{:S(2)}, u32[]{:S(2)}) async-start(bf16[8,112,640]{2,1,0:T(8,128)(2,1)} %shard_map.110), calls=%async_computation | async-start | bytes 2293760 | tf_op jit(solution)/shard_map/all_to_all | solution.py:214
  16.5 0.5 shard_map.111
  17.0 3.4 %collective-permute-start = (f32[32,640]{1,0:T(8,128)S(1)}, f32[32,640]{1,0:T(8,128)S(1)}, u32[]{:S(2)}, u32[]{:S(2)}) collective-permute-start(f32[32,640]{1,0:T(8,128)S(1)} %shard_map.111), channel_id=1, source_target_pairs={{0,1},{1,0},{2,3},{3,2},{4,5},{5,4},{6,7},{7,6},{8,9},{9,8},{10,11... | collective-permute-start | bytes 245768 | tf_op jit(solution)/shard_map/ppermute | solution.py:285
  20.3 7.7 %collective-permute-done = f32[32,640]{1,0:T(8,128)S(1)} collective-permute-done((f32[32,640]{1,0:T(8,128)S(1)}, f32[32,640]{1,0:T(8,128)S(1)}, u32[]{:S(2)}, u32[]{:S(2)}) %collective-permute-start) | collective-permute-done | bytes 81952 | tf_op jit(solution)/shard_map/ppermute | solution.py:285
  28.0 3.5 %collective-permute-start.1 = (f32[32,640]{1,0:T(8,128)S(1)}, f32[32,640]{1,0:T(8,128)S(1)}, u32[]{:S(2)}, u32[]{:S(2)}) collective-permute-start(f32[32,640]{1,0:T(8,128)S(1)} %add.132), channel_id=1, source_target_pairs={{0,2},{2,0},{4,6},{6,4},{1,3},{3,1},{5,7},{7,5},{8,10},{10,8},{12,... | collective-permute-start | bytes 245768 | tf_op jit(solution)/shard_map/ppermute | solution.py:285
  31.6 2.1 %collective-permute-done.1 = f32[32,640]{1,0:T(8,128)S(1)} collective-permute-done((f32[32,640]{1,0:T(8,128)S(1)}, f32[32,640]{1,0:T(8,128)S(1)}, u32[]{:S(2)}, u32[]{:S(2)}) %collective-permute-start.1) | collective-permute-done | bytes 81952 | tf_op jit(solution)/shard_map/ppermute | solution.py:285
  33.7 7.2 %collective-permute-start.2 = (f32[32,640]{1,0:T(8,128)S(1)}, f32[32,640]{1,0:T(8,128)S(1)}, u32[]{:S(2)}, u32[]{:S(2)}) collective-permute-start(f32[32,640]{1,0:T(8,128)S(1)} %add.133), channel_id=1, source_target_pairs={{0,4},{2,6},{4,0},{6,2},{1,5},{3,7},{5,1},{7,3},{8,12},{10,14},{12... | collective-permute-start | bytes 245768 | tf_op jit(solution)/shard_map/ppermute | solution.py:285
  40.9 1.8 %collective-permute-done.2 = f32[32,640]{1,0:T(8,128)S(1)} collective-permute-done((f32[32,640]{1,0:T(8,128)S(1)}, f32[32,640]{1,0:T(8,128)S(1)}, u32[]{:S(2)}, u32[]{:S(2)}) %collective-permute-start.2) | collective-permute-done | bytes 81952 | tf_op jit(solution)/shard_map/ppermute | solution.py:285
  42.7 7.9 %collective-permute-start.3 = (f32[32,640]{1,0:T(8,128)S(1)}, f32[32,640]{1,0:T(8,128)S(1)}, u32[]{:S(2)}, u32[]{:S(2)}) collective-permute-start(f32[32,640]{1,0:T(8,128)S(1)} %add.134), channel_id=1, source_target_pairs={{0,8},{8,0},{1,9},{9,1},{2,10},{10,2},{3,11},{11,3},{4,12},{12,4},... | collective-permute-start | bytes 245768 | tf_op jit(solution)/shard_map/ppermute | solution.py:285
  50.6 0.9 collective-permute-done.3
  51.6 0.2 convert_reduce_fusion
  52.0 0.2 fusion.14
  52.4 0.9 multiply_convert_fusion
  53.6 0.2 convolution_add_fusion.2
  53.8 0.2 fusion.7
  54.1 1.1 broadcast_in_dim.21
  55.2 3.7 %all-to-all-start.1 = ((bf16[8,96,704]{2,1,0:T(8,128)(2,1)}), bf16[8,96,704]{2,1,0:T(8,128)(2,1)S(1)}, u32[]{:S(2)}, u32[]{:S(2)}) async-start(bf16[8,96,704]{2,1,0:T(8,128)(2,1)} %broadcast_in_dim.21), calls=%async_computation.1 | async-start | bytes 2359296 | tf_op jit(solution)/shard_map/all_to_all | solution.py:244
  58.9 0.2 copy.63.gain_ref
  59.1 17.5 %all-to-all-done.1 = bf16[8,96,704]{2,1,0:T(8,128)(2,1)S(1)} async-done(((bf16[8,96,704]{2,1,0:T(8,128)(2,1)}), bf16[8,96,704]{2,1,0:T(8,128)(2,1)S(1)}, u32[]{:S(2)}, u32[]{:S(2)}) %all-to-all-start.1) | async-done | bytes 1081376 | tf_op jit(solution)/shard_map/all_to_all | solution.py:244
  76.6 6.2 %shard_map.112 = (bf16[32,16,512]{2,1,0:T(8,128)(2,1)S(1)}, bf16[32,16,512]{2,1,0:T(8,128)(2,1)S(1)}, f32[32,32,128]{2,1,0:T(8,128)S(1)}, bf16[32,32,128]{2,1,0:T(8,128)(2,1)S(1)}) custom-call(s32[1]{0:T(128)} %bitcast.6.core_ref, bf16[768,704]{1,0:T(8,128)(2,1)S(1)} %bitcast.36, bf16[768,1024]{1,0:T(8,128)(2,1)} %resid_ref.3, bf16[768,1024]{1,0:T(8,128)(2,1)} %heads_ref.3, ...), custom_call_target="tpu_custom_call" | custom-call | flops 1207959552 | bytes 7340032 | tf_op jit(solution)/shard_map/pallas_call | solution.py:163
  82.9 3.3 %collective-permute-start.5 = (bf16[32,16,512]{2,1,0:T(8,128)(2,1)S(1)}, bf16[32,16,512]{2,1,0:T(8,128)(2,1)S(1)}, u32[]{:S(2)}, u32[]{:S(2)}) collective-permute-start(bf16[32,16,512]{2,1,0:T(8,128)(2,1)S(1)} %get-tuple-element.17), channel_id=1, source_target_pairs={{0,8},{8,0},{1,9},{9,1},{2,10},{10,2},{3,11},{11,3},{4,12},{12,4},... | collective-permute-start | bytes 1572872 | tf_op jit(solution)/shard_map/ppermute | solution.py:285
  86.2 1.9 %collective-permute-start.4 = (bf16[32,32,128]{2,1,0:T(8,128)(2,1)S(1)}, bf16[32,32,128]{2,1,0:T(8,128)(2,1)S(1)}, u32[]{:S(2)}, u32[]{:S(2)}) collective-permute-start(bf16[32,32,128]{2,1,0:T(8,128)(2,1)S(1)} %get-tuple-element.15), channel_id=1, source_target_pairs={{0,8},{8,0},{1,9},{9,1},{2,10},{10,2},{3,11},{11,3},{4,12},{12,4},... | collective-permute-start | bytes 786440 | tf_op jit(solution)/shard_map/ppermute | solution.py:285
  88.2 1.5 collective-permute-done.4
  89.7 0.7 copy.77
  90.4 14.5 %all-to-all-start.2 = ((bf16[16,2,24,128]{3,2,1,0:T(8,128)(2,1)}), bf16[16,2,24,128]{3,2,1,0:T(8,128)(2,1)S(1)}, u32[]{:S(2)}, u32[]{:S(2)}) async-start(bf16[16,2,24,128]{3,2,1,0:T(8,128)(2,1)} %bitcast.35), calls=%async_computation.2 | async-start | bytes 393216 | tf_op jit(solution)/shard_map/all_to_all | solution.py:259
  105.1 4.5 %collective-permute-start.6 = (bf16[16,16,512]{2,1,0:T(8,128)(2,1)S(1)}, bf16[16,16,512]{2,1,0:T(8,128)(2,1)S(1)}, u32[]{:S(2)}, u32[]{:S(2)}) collective-permute-start(bf16[16,16,512]{2,1,0:T(8,128)(2,1)S(1)} %fusion.9), channel_id=1, source_target_pairs={{0,256},{256,0},{1,257},{257,1},{2,258},{258,2},{3,259},{259,3},{4... | collective-permute-start | bytes 786440 | tf_op jit(solution)/shard_map/ppermute | solution.py:285
  109.6 6.3 %collective-permute-done.6 = bf16[16,16,512]{2,1,0:T(8,128)(2,1)S(1)} collective-permute-done((bf16[16,16,512]{2,1,0:T(8,128)(2,1)S(1)}, bf16[16,16,512]{2,1,0:T(8,128)(2,1)S(1)}, u32[]{:S(2)}, u32[]{:S(2)}) %collective-permute-start.6) | collective-permute-done | bytes 262176 | tf_op jit(solution)/shard_map/ppermute | solution.py:285
  116.0 2.1 %all-to-all-done.2 = bf16[16,2,24,128]{3,2,1,0:T(8,128)(2,1)S(1)} async-done(((bf16[16,2,24,128]{3,2,1,0:T(8,128)(2,1)}), bf16[16,2,24,128]{3,2,1,0:T(8,128)(2,1)S(1)}, u32[]{:S(2)}, u32[]{:S(2)}) %all-to-all-start.2) | async-done | bytes 196640 | tf_op jit(solution)/shard_map/all_to_all | solution.py:259
  118.2 4.5 %collective-permute-start.7 = (f32[2,24,128]{2,1,0:T(8,128)S(1)}, f32[2,24,128]{2,1,0:T(8,128)S(1)}, u32[]{:S(2)}, u32[]{:S(2)}) collective-permute-start(f32[2,24,128]{2,1,0:T(8,128)S(1)} %convert_reduce_fusion.2), channel_id=1, source_target_pairs={{0,256},{256,0},{1,257},{257,1},{2,258},{258,2},{3,259},{259,3},{4... | collective-permute-start | bytes 73736 | tf_op jit(solution)/shard_map/ppermute | solution.py:285
  122.7 1.5 collective-permute-done.7
  124.3 0.8 pad_maximum_fusion
  125.1 9.0 %all-to-all-start.3 = ((bf16[16,16,896]{2,1,0:T(8,128)(2,1)}), bf16[16,16,896]{2,1,0:T(8,128)(2,1)S(1)}, u32[]{:S(2)}, u32[]{:S(2)}) async-start(bf16[16,16,896]{2,1,0:T(8,128)(2,1)} %pad_maximum_fusion), calls=%async_computation.3 | async-start | bytes 917504 | tf_op jit(solution)/shard_map/all_to_all | solution.py:272
  134.2 0.8 dynamic_slice.24
  134.9 17.5 %all-to-all-done.3 = bf16[16,16,896]{2,1,0:T(8,128)(2,1)S(1)} async-done(((bf16[16,16,896]{2,1,0:T(8,128)(2,1)}), bf16[16,16,896]{2,1,0:T(8,128)(2,1)S(1)}, u32[]{:S(2)}, u32[]{:S(2)}) %all-to-all-start.3) | async-done | bytes 458784 | tf_op jit(solution)/shard_map/all_to_all | solution.py:272
  152.5 10.1 %collective-permute-start.8 = (bf16[16,16,384]{2,1,0:T(8,128)(2,1)S(1)}, bf16[16,16,384]{2,1,0:T(8,128)(2,1)S(1)}, u32[]{:S(2)}, u32[]{:S(2)}) collective-permute-start(bf16[16,16,384]{2,1,0:T(8,128)(2,1)S(1)} %slice.70), channel_id=1, source_target_pairs={{0,8},{8,0},{1,9},{9,1},{2,10},{10,2},{3,11},{11,3},{4,12},{12,4},... | collective-permute-start | bytes 589832 | tf_op jit(solution)/shard_map/ppermute | solution.py:285
  162.6 0.7 multiply_convert_fusion.1
  163.3 0.3 collective-permute-done.8
  164.1 0.2 copy.67
  164.3 0.2 slice_bitcast_fusion
  164.5 0.9 copy.69
  165.4 0.9 copy.70
  166.3 0.7 reshape.108
  (44 shorter events, 1.9 us)
Async XLA Ops:
  0.6 3.2 %copy-start = (bf16[1024,512]{1,0:T(8,128)(2,1)S(1)}, bf16[1024,512]{1,0:T(8,128)(2,1)}, u32[]{:S(2)}) copy-start(bf16[1024,512]{1,0:T(8,128)(2,1)} %matrix_ref.5) | copy-start | bytes 3145732
  3.8 1.4 copy-start.1
  5.2 1.4 copy-start.2
  10.5 6.0 %copy-start.3 = (bf16[64,1024]{1,0:T(8,128)(2,1)S(1)}, bf16[64,1024]{1,0:T(8,128)(2,1)}, u32[]{:S(2)}) copy-start(bf16[64,1024]{1,0:T(8,128)(2,1)} %up_ref.3) | copy-start | bytes 393220
  10.5 41.1 %all-to-all-start = ((bf16[8,112,640]{2,1,0:T(8,128)(2,1)}), bf16[8,112,640]{2,1,0:T(8,128)(2,1)S(1)}, u32[]{:S(2)}, u32[]{:S(2)}) async-start(bf16[8,112,640]{2,1,0:T(8,128)(2,1)} %shard_map.110), calls=%async_computation | async-start | bytes 2293760 | tf_op jit(solution)/shard_map/all_to_all | solution.py:214
  17.0 11.0 %collective-permute-start = (f32[32,640]{1,0:T(8,128)S(1)}, f32[32,640]{1,0:T(8,128)S(1)}, u32[]{:S(2)}, u32[]{:S(2)}) collective-permute-start(f32[32,640]{1,0:T(8,128)S(1)} %shard_map.111), channel_id=1, source_target_pairs={{0,1},{1,0},{2,3},{3,2},{4,5},{5,4},{6,7},{7,6},{8,9},{9,8},{10,11... | collective-permute-start | bytes 245768 | tf_op jit(solution)/shard_map/ppermute | solution.py:285
  28.0 5.6 %collective-permute-start.1 = (f32[32,640]{1,0:T(8,128)S(1)}, f32[32,640]{1,0:T(8,128)S(1)}, u32[]{:S(2)}, u32[]{:S(2)}) collective-permute-start(f32[32,640]{1,0:T(8,128)S(1)} %add.132), channel_id=1, source_target_pairs={{0,2},{2,0},{4,6},{6,4},{1,3},{3,1},{5,7},{7,5},{8,10},{10,8},{12,... | collective-permute-start | bytes 245768 | tf_op jit(solution)/shard_map/ppermute | solution.py:285
  33.7 9.0 %collective-permute-start.2 = (f32[32,640]{1,0:T(8,128)S(1)}, f32[32,640]{1,0:T(8,128)S(1)}, u32[]{:S(2)}, u32[]{:S(2)}) collective-permute-start(f32[32,640]{1,0:T(8,128)S(1)} %add.133), channel_id=1, source_target_pairs={{0,4},{2,6},{4,0},{6,2},{1,5},{3,7},{5,1},{7,3},{8,12},{10,14},{12... | collective-permute-start | bytes 245768 | tf_op jit(solution)/shard_map/ppermute | solution.py:285
  42.7 8.8 %collective-permute-start.3 = (f32[32,640]{1,0:T(8,128)S(1)}, f32[32,640]{1,0:T(8,128)S(1)}, u32[]{:S(2)}, u32[]{:S(2)}) collective-permute-start(f32[32,640]{1,0:T(8,128)S(1)} %add.134), channel_id=1, source_target_pairs={{0,8},{8,0},{1,9},{9,1},{2,10},{10,2},{3,11},{11,3},{4,12},{12,4},... | collective-permute-start | bytes 245768 | tf_op jit(solution)/shard_map/ppermute | solution.py:285
  51.5 0.9 copy-start.4
  55.2 21.4 %all-to-all-start.1 = ((bf16[8,96,704]{2,1,0:T(8,128)(2,1)}), bf16[8,96,704]{2,1,0:T(8,128)(2,1)S(1)}, u32[]{:S(2)}, u32[]{:S(2)}) async-start(bf16[8,96,704]{2,1,0:T(8,128)(2,1)} %broadcast_in_dim.21), calls=%async_computation.1 | async-start | bytes 2359296 | tf_op jit(solution)/shard_map/all_to_all | solution.py:244
  82.9 7.5 %collective-permute-start.5 = (bf16[32,16,512]{2,1,0:T(8,128)(2,1)S(1)}, bf16[32,16,512]{2,1,0:T(8,128)(2,1)S(1)}, u32[]{:S(2)}, u32[]{:S(2)}) collective-permute-start(bf16[32,16,512]{2,1,0:T(8,128)(2,1)S(1)} %get-tuple-element.17), channel_id=1, source_target_pairs={{0,8},{8,0},{1,9},{9,1},{2,10},{10,2},{3,11},{11,3},{4,12},{12,4},... | collective-permute-start | bytes 1572872 | tf_op jit(solution)/shard_map/ppermute | solution.py:285
  86.2 3.4 %collective-permute-start.4 = (bf16[32,32,128]{2,1,0:T(8,128)(2,1)S(1)}, bf16[32,32,128]{2,1,0:T(8,128)(2,1)S(1)}, u32[]{:S(2)}, u32[]{:S(2)}) collective-permute-start(bf16[32,32,128]{2,1,0:T(8,128)(2,1)S(1)} %get-tuple-element.15), channel_id=1, source_target_pairs={{0,8},{8,0},{1,9},{9,1},{2,10},{10,2},{3,11},{11,3},{4,12},{12,4},... | collective-permute-start | bytes 786440 | tf_op jit(solution)/shard_map/ppermute | solution.py:285
  90.4 27.7 %all-to-all-start.2 = ((bf16[16,2,24,128]{3,2,1,0:T(8,128)(2,1)}), bf16[16,2,24,128]{3,2,1,0:T(8,128)(2,1)S(1)}, u32[]{:S(2)}, u32[]{:S(2)}) async-start(bf16[16,2,24,128]{3,2,1,0:T(8,128)(2,1)} %bitcast.35), calls=%async_computation.2 | async-start | bytes 393216 | tf_op jit(solution)/shard_map/all_to_all | solution.py:259
  105.1 10.8 %collective-permute-start.6 = (bf16[16,16,512]{2,1,0:T(8,128)(2,1)S(1)}, bf16[16,16,512]{2,1,0:T(8,128)(2,1)S(1)}, u32[]{:S(2)}, u32[]{:S(2)}) collective-permute-start(bf16[16,16,512]{2,1,0:T(8,128)(2,1)S(1)} %fusion.9), channel_id=1, source_target_pairs={{0,256},{256,0},{1,257},{257,1},{2,258},{258,2},{3,259},{259,3},{4... | collective-permute-start | bytes 786440 | tf_op jit(solution)/shard_map/ppermute | solution.py:285
  118.2 6.1 %collective-permute-start.7 = (f32[2,24,128]{2,1,0:T(8,128)S(1)}, f32[2,24,128]{2,1,0:T(8,128)S(1)}, u32[]{:S(2)}, u32[]{:S(2)}) collective-permute-start(f32[2,24,128]{2,1,0:T(8,128)S(1)} %convert_reduce_fusion.2), channel_id=1, source_target_pairs={{0,256},{256,0},{1,257},{257,1},{2,258},{258,2},{3,259},{259,3},{4... | collective-permute-start | bytes 73736 | tf_op jit(solution)/shard_map/ppermute | solution.py:285
  125.1 27.3 %all-to-all-start.3 = ((bf16[16,16,896]{2,1,0:T(8,128)(2,1)}), bf16[16,16,896]{2,1,0:T(8,128)(2,1)S(1)}, u32[]{:S(2)}, u32[]{:S(2)}) async-start(bf16[16,16,896]{2,1,0:T(8,128)(2,1)} %pad_maximum_fusion), calls=%async_computation.3 | async-start | bytes 917504 | tf_op jit(solution)/shard_map/all_to_all | solution.py:272
  152.5 11.1 %collective-permute-start.8 = (bf16[16,16,384]{2,1,0:T(8,128)(2,1)S(1)}, bf16[16,16,384]{2,1,0:T(8,128)(2,1)S(1)}, u32[]{:S(2)}, u32[]{:S(2)}) collective-permute-start(bf16[16,16,384]{2,1,0:T(8,128)(2,1)S(1)} %slice.70), channel_id=1, source_target_pairs={{0,8},{8,0},{1,9},{9,1},{2,10},{10,2},{3,11},{11,3},{4,12},{12,4},... | collective-permute-start | bytes 589832 | tf_op jit(solution)/shard_map/ppermute | solution.py:285

commit v4 on v3

v4 whole, which is shorter than its diff:
```python
import functools

import jax
import jax.numpy as jnp
from jax import lax
from jax.experimental import pallas as pl
from jax.experimental.pallas import tpu as pltpu
from jax.sharding import Mesh, PartitionSpec as P

MODEL_WIDTH = 8192
EPSILON = 1e-06
TP = ("x", "y_lo")
ROWS = ("y_hi", "z", "core")
bf16 = jnp.bfloat16
f32 = jnp.float32
NN = (((1,), (0,)), ((), ()))
NT = (((1,), (1,)), ((), ()))
TN = (((0,), (0,)), ((), ()))
LANES = 128
VMEM_LIMIT = 48 * 2**20
VMEM_WHOLE = 60 * 2**20


def dot(a, b, dims=NN):
    return lax.dot_general(a, b, dims, preferred_element_type=f32)


def split(x):
    high = x.astype(bf16)
    return high, (x - high.astype(f32)).astype(bf16)


def dot_split(a, b, dims=NN):
    return dot(a, b[0], dims) + dot(a, b[1], dims)


def project_kernel(
    share, resid_ref, heads_ref, gain_ref, matrix_ref, down_ref, up_ref, out_ref, weights_ref
):
    rank, width = up_ref.shape[0], matrix_ref.shape[1]
    gain = gain_ref[...].astype(f32)

    @pl.when(pl.program_id(0) == 0)
    def _():
        high, low = split(up_ref[...].astype(f32) * gain)
        weights_ref[:, :width] = dot(high, matrix_ref[...]) + dot(low, matrix_ref[...])
        gram = dot(up_ref[...], up_ref[...], NT)
        weights_ref[:, width:] = jnp.concatenate([gram, jnp.zeros_like(gram)], axis=1)

    resid = resid_ref[...]
    wide = resid.astype(f32)
    values = dot((wide * gain).astype(bf16), matrix_ref[...])
    small = [dot(heads_ref[...], down_ref[...], NT), dot(resid, up_ref[...], NT)]
    small = jnp.concatenate(small, axis=1)
    high, low = split(wide * wide)
    ones = jnp.ones((rank, wide.shape[1]), bf16)
    line = lax.broadcasted_iota(jnp.int32, (rank, share // 2), 0)
    for piece in range(out_ref.shape[0]):
        rows = slice(piece * share, (piece + 1) * share)
        out_ref[piece, :share, :width] = values[rows].astype(bf16)
        out_ref[piece, :share, width:] = small[rows].astype(bf16)
        lines = jnp.zeros(line.shape, f32)
        for part in range(2):
            rows = slice(piece * share + part * (share // 2), piece * share + (part + 1) * (share // 2))
            squares = dot(ones, high[rows], NT) + dot(ones, low[rows], NT)
            first = squares.astype(bf16).astype(f32)
            lines = jnp.where(line == part, first, lines)
            lines = jnp.where(line == 2 + part, squares - first, lines)
        blank = [jnp.zeros((rank, rank), f32), lines, jnp.zeros((rank, rank - share // 2), f32)]
        out_ref[piece, share:, :width] = weights_ref[:, :width].astype(bf16)
        tail = weights_ref[:, width:] + jnp.concatenate(blank, axis=1)
        out_ref[piece, share:, width:] = tail.astype(bf16)


def project(resid, heads, gain, matrix, down, up, share):
    tokens, features = resid.shape
    rank, width = up.shape[0], matrix.shape[1]
    pieces, group = tokens // share, 2
    rows, columns = group * share, width + 2 * rank
    whole = lambda i: (0, 0)
    return pl.pallas_call(
        functools.partial(project_kernel, share),
        grid=(pieces // group,),
        in_specs=[
            pl.BlockSpec((rows, features), lambda i: (i, 0)),
            pl.BlockSpec((rows, features), lambda i: (i, 0)),
            pl.BlockSpec((1, features), whole),
            pl.BlockSpec((features, width), whole),
            pl.BlockSpec(down.shape, whole),
            pl.BlockSpec(up.shape, whole),
        ],
        out_specs=pl.BlockSpec((group, share + rank, columns), lambda i: (i, 0, 0)),
        out_shape=jax.ShapeDtypeStruct((pieces, share + rank, columns), bf16),
        scratch_shapes=[pltpu.VMEM((rank, columns), f32)],
        compiler_params=pltpu.CompilerParams(vmem_limit_bytes=VMEM_WHOLE),
        cost_estimate=pl.CostEstimate(
            flops=2 * tokens * features * (width + 256),
            bytes_accessed=4 * tokens * features + 2 * features * width,
            transcendentals=0,
        ),
    )(resid, heads, gain, matrix, down, up)


def owner_kernel(loss_scale, pieces_ref, target_ref, values_ref, every_ref, sent_ref, sems):
    share, width = target_ref.shape
    tp = pieces_ref.shape[0]
    rank = pieces_ref.shape[1] - share
    total = functools.reduce(jnp.add, [pieces_ref[i].astype(f32) for i in range(tp)])
    through = split(total[share:, :width])
    gram = split(total[share:, width : width + rank])
    lines = total[share : share + 8, width + rank : width + rank + share // 2]
    lines = lines[0:2] + lines[2:4]
    diagonal = (share // 2, share // 2)
    diagonal = lax.broadcasted_iota(jnp.int32, diagonal, 0) == lax.broadcasted_iota(jnp.int32, diagonal, 1)
    squares = jnp.concatenate(
        [
            jnp.sum(jnp.where(diagonal, lines[i : i + 1], 0.0), axis=1, keepdims=True)
            for i in range(2)
        ],
        axis=0,
    )

    down_b = total[:share, width : width + rank].astype(bf16)
    down_wide = down_b.astype(f32)
    along = total[:share, width + rank :]
    hidden_up = along + 0.5 * dot_split(down_b, gram)
    squares = squares + 0.5 * jnp.sum(down_wide * (along + hidden_up), axis=1, keepdims=True)
    inverse_rms = lax.rsqrt(squares / MODEL_WIDTH + EPSILON)
    sums = inverse_rms * (total[:share, :width] + 0.5 * dot_split(down_b, through))
    values_ref[...] = sums.astype(bf16)
    error = (sums - target_ref[...].astype(f32)) * loss_scale
    inner = jnp.sum(error * sums, axis=1, keepdims=True) / MODEL_WIDTH
    high, low = split(error)
    down_grad = dot_split(high, through, NT) + dot(low, through[0], NT)
    down_grad = 0.5 * inverse_rms * (down_grad - inner * inverse_rms * hidden_up)
    weighted = down_wide * (inner * inverse_rms * inverse_rms)
    sent_ref[:, :width] = (error * inverse_rms).astype(bf16)
    sent_ref[:, width : width + 2 * rank] = jnp.concatenate([down_wide, down_grad], axis=1).astype(bf16)
    sent_ref[:, width + 2 * rank :] = weighted.astype(bf16)
    copies = [pltpu.make_async_copy(sent_ref, every_ref.at[i], sems.at[i]) for i in range(tp)]
    for copy in copies:
        copy.start()
    for copy in copies:
        copy.wait()


def owner(pieces, target, loss_scale):
    share, width = target.shape
    tp, rank = pieces.shape[0], pieces.shape[1] - share
    sent = (share, width + 3 * rank)
    vmem = pl.BlockSpec(memory_space=pltpu.VMEM)
    return pl.pallas_call(
        functools.partial(owner_kernel, loss_scale),
        in_specs=[vmem, vmem],
        out_specs=[vmem, pl.BlockSpec(memory_space=pl.ANY)],
        out_shape=[
            jax.ShapeDtypeStruct((share, width), bf16),
            jax.ShapeDtypeStruct((tp, *sent), bf16),
        ],
        scratch_shapes=[pltpu.VMEM(sent, bf16), pltpu.SemaphoreType.DMA((tp,))],
        compiler_params=pltpu.CompilerParams(vmem_limit_bytes=VMEM_LIMIT),
    )(pieces, target)


def gradients_kernel(
    core_ref, every_ref, resid_ref, heads_ref, up_ref, gain_ref, matrix_ref,
    kept_ref, small_ref, sent_ref, cross_ref,
):
    width = matrix_ref.shape[1]
    rank = up_ref.shape[0]
    error = every_ref[:, :width]
    down = every_ref[:, width : width + rank]

    @pl.when(pl.program_id(0) == 0)
    def _():
        high, low = split(dot(error, down, TN))
        cross_ref[0] = high
        cross_ref[1] = low

    core = core_ref[0]
    matrix = matrix_ref[...]
    hidden = (resid_ref[...].astype(f32) + 0.5 * dot(down, up_ref[...])).astype(bf16)
    value = dot(hidden, error, TN)
    a_part = dot(heads_ref[...], every_ref[:, width + rank : width + 2 * rank], TN)
    b_part = dot(hidden, every_ref[:, width + 2 * rank :], TN)
    crossed = dot(matrix, cross_ref[0]) + dot(matrix, cross_ref[1])
    b_part = 0.5 * (gain_ref[...] * crossed - b_part)
    small = jnp.concatenate([a_part, b_part], axis=1)
    gain_part = jnp.sum(value * matrix.astype(f32), axis=1, keepdims=True)
    group, own = kept_ref.shape[:2]
    lane = lax.broadcasted_iota(jnp.int32, small.shape, 1)
    line = lax.rem(lax.broadcasted_iota(jnp.int32, small.shape, 0), LANES)
    spread = jnp.where(lane == line, gain_part, 0.0).reshape(2 * group, own, LANES)
    gain_line = jnp.sum(spread, axis=1, keepdims=True)
    row = lax.broadcasted_iota(jnp.int32, (2 * group, own, LANES), 1)
    gain_line = jnp.where(row == 0, gain_line, 0.0)
    small = jnp.concatenate([small.reshape(2 * group, own, -1), gain_line], axis=2)
    small = small.reshape(group, 2, own, -1)
    value = value.reshape(group, 2, own, width)
    first = core == 0
    kept_ref[...] = jnp.where(first, value[:, 0], value[:, 1]).astype(bf16)
    small_ref[...] = jnp.where(first, small[:, 0], small[:, 1])
    sent_ref[:, :, :width] = jnp.where(first, value[:, 1], value[:, 0]).astype(bf16)
    sent_ref[:, :, width:] = jnp.where(first, small[:, 1], small[:, 0]).astype(bf16)


def gradients(core, every, resid, heads, up, gain, matrix, own):
    tokens, features = resid.shape
    width, rank = matrix.shape[1], up.shape[0]
    block = 256
    pieces, group = features // (2 * own), block // (2 * own)
    shapes = [
        jax.ShapeDtypeStruct((pieces, own, width), bf16),
        jax.ShapeDtypeStruct((pieces, own, 2 * rank + LANES), f32),
        jax.ShapeDtypeStruct((pieces, own, width + 2 * rank + LANES), bf16),
    ]
    return pl.pallas_call(
        gradients_kernel,
        grid=(features // block,),
        in_specs=[
            pl.BlockSpec(memory_space=pltpu.SMEM),
            pl.BlockSpec(every.shape, lambda i: (0, 0)),
            pl.BlockSpec((tokens, block), lambda i: (0, i)),
            pl.BlockSpec((tokens, block), lambda i: (0, i)),
            pl.BlockSpec((rank, block), lambda i: (0, i)),
            pl.BlockSpec((block, 1), lambda i: (i, 0)),
            pl.BlockSpec((block, width), lambda i: (i, 0)),
        ],
        out_specs=[pl.BlockSpec((group, *s.shape[1:]), lambda i: (i, 0, 0)) for s in shapes],
        out_shape=shapes,
        scratch_shapes=[pltpu.VMEM((2, width, rank), bf16)],
        compiler_params=pltpu.CompilerParams(vmem_limit_bytes=VMEM_LIMIT),
        cost_estimate=pl.CostEstimate(
            flops=2 * tokens * features * (width + 4 * rank),
            bytes_accessed=4 * tokens * features + 8 * features * width,
            transcendentals=0,
        ),
    )(core, every, resid, heads, up, gain, matrix)


def assemble_kernel(core_ref, mine_ref, got_ref, a_ref, b_ref, gain_ref):
    z_size, own = mine_ref.shape[:2]
    rank, features = a_ref.shape
    together = LANES // (2 * own)
    first = core_ref[0] == 0
    for y in range(2):
        for start in range(0, z_size, together):
            lines, gain_line = [], jnp.zeros((1, LANES), f32)
            for z in range(start, start + together):
                mine = mine_ref[z].astype(f32)
                got = got_ref[z].astype(f32)
                lanes = slice(y * LANES, (y + 1) * LANES)
                lines += [
                    jnp.where(first, mine[:, lanes], got[:, lanes]),
                    jnp.where(first, got[:, lanes], mine[:, lanes]),
                ]
                gain_line += (mine + got)[y * 8 : y * 8 + 1, 2 * LANES :]
            both = jnp.concatenate(lines, axis=0).T
            place = y * (features // 2) + start * 2 * own
            a_ref[:, place : place + LANES] = both[:rank]
            b_ref[:, place : place + LANES] = both[rank:]
            gain_ref[:, place : place + LANES] = gain_line


def assemble(core, mine, got, rank):
    z_size, own = mine.shape[:2]
    features = 2 * z_size * 2 * own
    whole = jax.ShapeDtypeStruct((rank, features), f32)
    vmem = pl.BlockSpec(memory_space=pltpu.VMEM)
    return pl.pallas_call(
        assemble_kernel,
        in_specs=[pl.BlockSpec(memory_space=pltpu.SMEM), vmem, vmem],
        out_specs=[vmem, vmem, vmem],
        out_shape=[whole, whole, jax.ShapeDtypeStruct((1, features), f32)],
        compiler_params=pltpu.CompilerParams(vmem_limit_bytes=VMEM_LIMIT),
    )(core, mine, got)


def body(resid, heads, down_matrix, up, scale, value_matrix, target):
    share, width = target.shape
    tp = resid.shape[0] // share
    tokens = resid.shape[0] * lax.axis_size(ROWS)
    rank, features = up.shape
    core = lax.axis_index("core")
    gain = scale.astype(f32)

    pieces = project(resid, heads, scale.reshape(1, -1), value_matrix, down_matrix.T, up, share)
    pieces = lax.all_to_all(pieces, TP, 0, 0, tiled=True)
    values, every = owner(pieces, target, 1.0 / tokens**0.5)
    every = lax.all_to_all(every, TP, 0, 0, tiled=True)
    every = every.reshape(tp * share, -1)

    y_size, z_size, core_size = (lax.axis_size(a) for a in ROWS)
    own = features // (y_size * z_size * core_size)
    kept, small, sent = gradients(
        core.reshape(1), every, resid, heads, up, gain[:, None], value_matrix, own
    )

    got = swap(sent, "core")
    small = small + got[:, :, width:].astype(f32)
    small = jnp.concatenate([small[:, :, : 2 * rank], small[:, :8, 2 * rank :]], axis=1)
    small = small.astype(bf16).reshape(y_size, z_size, own + 8, -1).transpose(1, 0, 2, 3)
    small = lax.all_to_all(small, "z", 0, 0, tiled=True)

    me = lax.axis_index("y_hi")
    kept = kept.reshape(y_size, z_size, own, width)
    got = got.reshape(y_size, z_size, own, -1)[..., :width]
    pick = lambda x, i: lax.dynamic_index_in_dim(x, i, 0, keepdims=False).astype(f32)
    other = swap((pick(kept, 1 - me) + pick(got, 1 - me)).astype(bf16), "y_hi")
    value = (pick(kept, me) + pick(got, me) + other.astype(f32)).astype(bf16)

    small = jnp.sum(small.astype(f32), axis=0)
    small = (small + swap(small, "y_hi")).astype(bf16)

    gains = small[:, own:].reshape(-1, small.shape[-1])
    small = jnp.concatenate([*small[:, :own], gains], axis=1)
    small = jnp.broadcast_to(small, (z_size, *small.shape))
    value = lax.all_to_all(jnp.concatenate([value, small], axis=2), "z", 0, 0, tiled=True)
    small = value[:, :, width:]
    a_grad, b_grad, gain_grad = assemble(core.reshape(1), small, swap(small, "core"), rank)

    value = jnp.sum(value[:, :, :width].astype(f32), axis=0)
    own_gain = lax.dynamic_slice_in_dim(gain, lax.axis_index(ROWS) * own, own, 0)
    value_grad = (value * own_gain[:, None]).astype(bf16)
    return (values, value_grad, a_grad.T, b_grad, gain_grad.reshape(-1))


def swap(x, axis):
    return lax.ppermute(x, axis, [(0, 1), (1, 0)])


def solution(mesh):
    rows, tp = mesh.shape["rows"], mesh.shape["tp"]
    y_hi, core, y_lo = 2, 2, 2
    fine = Mesh(
        mesh.devices.reshape(y_hi, rows // (y_hi * core), core, tp // y_lo, y_lo), (*ROWS, *TP)
    )
    in_specs = (
        P(ROWS, TP),
        P(ROWS, TP),
        P(TP, None),
        P(None, TP),
        P(TP),
        P(TP, None),
        P((*ROWS, *TP), None),
    )
    out_specs = (
        P((*ROWS, *TP), None),
        P((*TP, *ROWS), None),
        P(TP, None),
        P(None, TP),
        P(TP),
    )
    return jax.shard_map(body, mesh=fine, in_specs=in_specs, out_specs=out_specs, check_vma=False)
```

time: 168 us -> 146 us (0.87)
  blocking collectives: 0 us -> 23.2 us
  starting transfers between devices: 79.6 us -> 56.8 us
  waiting for transfers between devices: 59.4 us -> 43 us
  local copies, waits for them, and re-layouts: 11.3 us -> 1.74 us
  Pallas kernels: 10.6 us -> 16.7 us
  matrix products: 1.95 us -> 0 us
    all_to_all x0 -> x1, blocking collectives: none -> 23.2 us  [body(): pieces = lax.all_to_all(pieces, TP, 0, 0, tiled=True)]
    ppermute x9 -> x4, starting transfers between devices: 46.3 us -> 26.1 us  [swap(): return lax.ppermute(x, axis, [(0, 1), (1, 0)])]
    ppermute x9 -> x4, waiting for transfers between devices: 22.2 us -> 3.6 us  [swap(): return lax.ppermute(x, axis, [(0, 1), (1, 0)])]
    unnamed x14 -> x8, local copies, waits for them, and re-layouts: 6.9 us -> 0.02 us
    all_to_all x1, waiting for transfers between devices: 2.13 us -> 8.18 us  [body(): small = lax.all_to_all(small, 'z', 0, 0, tiled=True)]
    all_to_all x2 -> x1, starting transfers between devices: 9.69 us -> 3.71 us  [body(): every = lax.all_to_all(every, TP, 0, 0, tiled=True)]
    all_to_all x2 -> x1, waiting for transfers between devices: 17.5 us -> 11.8 us  [body(): every = lax.all_to_all(every, TP, 0, 0, tiled=True)]
    all_to_all x1, starting transfers between devices: 14.5 us -> 18.6 us  [body(): small = lax.all_to_all(small, 'z', 0, 0, tiled=True)]
  transfers between devices with their start and end apart: 13 -> 7, of which waited for: 11 -> 6; matrix products, arithmetic and copies ran while one was open for 2% -> 1% of each run, Pallas kernels for 0% -> 0%
where the time goes in v4:
time: 146 us; the launch traced here: 145 us
  starting transfers between devices  56.8 us (39%)
  waiting for transfers between devices  43 us (29%)
  blocking collectives  23.2 us (16%)
  Pallas kernels  16.7 us (11%)
  other arithmetic  2.57 us (2%)
  local copies, waits for them, and re-layouts  1.74 us (1%)
    ppermute x4, starting transfers between devices, swap(): return lax.ppermute(x, axis, [(0, 1), (1, 0)])  26.1 us
    all_to_all x1, blocking collectives, body(): pieces = lax.all_to_all(pieces, TP, 0, 0, tiled=True)  23.2 us
    all_to_all x1, waiting for transfers between devices, body(): lax.all_to_all(jnp.concatenate([value, small], axis=2), 'z', 0, 0, tiled=...  19.4 us
    all_to_all x1, starting transfers between devices, body(): small = lax.all_to_all(small, 'z', 0, 0, tiled=True)  18.6 us
    all_to_all x1, waiting for transfers between devices, body(): every = lax.all_to_all(every, TP, 0, 0, tiled=True)  11.8 us
    all_to_all x1, starting transfers between devices, body(): lax.all_to_all(jnp.concatenate([value, small], axis=2), 'z', 0, 0, tiled=...  8.46 us
    all_to_all x1, waiting for transfers between devices, body(): small = lax.all_to_all(small, 'z', 0, 0, tiled=True)  8.18 us
    pallas_call x1, Pallas kernels, project(): pl.pallas_call(functools.partial(project_kernel, share), grid=(pieces //...  6.9 us
  transfers between devices with their start and end apart: 7, of which 6 were waited for; matrix products, arithmetic and copies ran while one was open for 1% of the time, Pallas kernels for 0%

profile of v4, /device:TPU:1, one launch (start us, length us, event | category | flops | bytes accessed | tf_op | source)
XLA Modules:
  0.0 144.9 jit_solution(12571269385079987064)
XLA Ops:
  0.6 1.3 reshape.45.gain_ref
  1.9 6.9 %shard_map.110 = bf16[8,160,640]{2,1,0:T(8,128)(2,1)} custom-call(bf16[768,1024]{1,0:T(8,128)(2,1)} %resid_ref.3, bf16[768,1024]{1,0:T(8,128)(2,1)} %heads_ref.3, bf16[1,1024]{1,0:T(2,128)(2,1)} %reshape.45.gain_ref, bf16[1024,512]{1,0:T(8,128)(2,1)} %matrix_ref.3, bf16[64,1024]{1,0:T(8,128)(2,1)} %bitcast.30, bf16[64,1024]{1,0:T(8,128)(2,1)} %up_ref.3), custom_call_target="tpu_custom_call" | custom-call | flops 1207959552 | bytes 4194304 | tf_op jit(solution)/shard_map/pallas_call | solution.py:81
  8.8 0.0 copy-start.2
  8.8 23.2 %all_to_all.20.pieces_ref = bf16[8,160,640]{2,1,0:T(8,128)(2,1)S(1)} all-to-all(bf16[8,160,640]{2,1,0:T(8,128)(2,1)} %shard_map.110), channel_id=1, replica_groups=mesh['y_hi'=2,'z'=16,'core'=2,'x'=4,'y_lo'=2] {'x','y_lo'}, dimensions={0} | all-to-all | bytes 3276800 | tf_op jit(solution)/shard_map/all_to_all | solution.py:288
  32.0 0.0 copy-done.2
  32.0 2.6 %shard_map.111 = (bf16[96,512]{1,0:T(8,128)(2,1)}, bf16[8,96,704]{2,1,0:T(8,128)(2,1)}) custom-call(bf16[8,160,640]{2,1,0:T(8,128)(2,1)S(1)} %all_to_all.20.pieces_ref, bf16[96,512]{1,0:T(8,128)(2,1)S(1)} %copy-done.2), custom_call_target="tpu_custom_call" | custom-call | tf_op jit(solution)/shard_map/pallas_call | solution.py:152
  34.6 0.0 copy-start.3
  34.7 0.0 copy-start
  34.7 0.0 copy-start.1
  34.7 3.7 %all-to-all-start.1 = ((bf16[8,96,704]{2,1,0:T(8,128)(2,1)}), bf16[8,96,704]{2,1,0:T(8,128)(2,1)S(1)}, u32[]{:S(2)}, u32[]{:S(2)}) async-start(bf16[8,96,704]{2,1,0:T(8,128)(2,1)} %get-tuple-element.14), calls=%async_computation.1 | async-start | bytes 2359296 | tf_op jit(solution)/shard_map/all_to_all | solution.py:290
  38.4 0.0 copy-done.3
  38.4 0.2 copy.13.gain_ref
  38.6 11.8 %all-to-all-done.1 = bf16[8,96,704]{2,1,0:T(8,128)(2,1)S(1)} async-done(((bf16[8,96,704]{2,1,0:T(8,128)(2,1)}), bf16[8,96,704]{2,1,0:T(8,128)(2,1)S(1)}, u32[]{:S(2)}, u32[]{:S(2)}) %all-to-all-start.1) | async-done | bytes 1081376 | tf_op jit(solution)/shard_map/all_to_all | solution.py:290
  50.4 0.0 copy-done
  50.4 0.0 copy-done.1
  50.4 6.3 %shard_map.112 = (bf16[32,16,512]{2,1,0:T(8,128)(2,1)S(1)}, f32[32,16,256]{2,1,0:T(8,128)S(1)}, bf16[32,16,768]{2,1,0:T(8,128)(2,1)S(1)}) custom-call(s32[1]{0:T(128)} %bitcast.1.core_ref, bf16[768,704]{1,0:T(8,128)(2,1)S(1)} %bitcast.24, bf16[768,1024]{1,0:T(8,128)(2,1)} %resid_ref.3, bf16[768,1024]{1,0:T(8,128)(2,1)} %heads_ref.3, ...), custom_call_target="tpu_custom_call" | custom-call | flops 1207959552 | bytes 7340032 | tf_op jit(solution)/shard_map/pallas_call | solution.py:217
  56.7 8.1 %collective-permute-start = (bf16[32,16,768]{2,1,0:T(8,128)(2,1)S(1)}, bf16[32,16,768]{2,1,0:T(8,128)(2,1)S(1)}, u32[]{:S(2)}, u32[]{:S(2)}) collective-permute-start(bf16[32,16,768]{2,1,0:T(8,128)(2,1)S(1)} %get-tuple-element.16), channel_id=1, source_target_pairs={{0,8},{8,0},{1,9},{9,1},{2,10},{10,2},{3,11},{11,3},{4,12},{12,4},... | collective-permute-start | bytes 2359304 | tf_op jit(solution)/shard_map/ppermute | solution.py:329
  64.8 1.9 %collective-permute-done = bf16[32,16,768]{2,1,0:T(8,128)(2,1)S(1)} collective-permute-done((bf16[32,16,768]{2,1,0:T(8,128)(2,1)S(1)}, bf16[32,16,768]{2,1,0:T(8,128)(2,1)S(1)}, u32[]{:S(2)}, u32[]{:S(2)}) %collective-permute-start) | collective-permute-done | bytes 786464 | tf_op jit(solution)/shard_map/ppermute | solution.py:329
  66.6 0.1 add_convert_fusion
  66.8 0.7 copy_bitcast_fusion
  67.5 18.6 %all-to-all-start.2 = ((bf16[16,2,24,128]{3,2,1,0:T(8,128)(2,1)}), bf16[16,2,24,128]{3,2,1,0:T(8,128)(2,1)S(1)}, u32[]{:S(2)}, u32[]{:S(2)}) async-start(bf16[16,2,24,128]{3,2,1,0:T(8,128)(2,1)} %copy_bitcast_fusion), calls=%async_computation.2 | async-start | bytes 393216 | tf_op jit(solution)/shard_map/all_to_all | solution.py:303
  86.1 0.1 slice.33
  86.1 0.1 fusion.1
  86.2 4.5 %collective-permute-start.1 = (bf16[16,16,512]{2,1,0:T(8,128)(2,1)S(1)}, bf16[16,16,512]{2,1,0:T(8,128)(2,1)S(1)}, u32[]{:S(2)}, u32[]{:S(2)}) collective-permute-start(bf16[16,16,512]{2,1,0:T(8,128)(2,1)S(1)} %fusion.1), channel_id=1, source_target_pairs={{0,256},{256,0},{1,257},{257,1},{2,258},{258,2},{3,259},{259,3},{4... | collective-permute-start | bytes 786440 | tf_op jit(solution)/shard_map/ppermute | solution.py:329
  90.8 8.2 %all-to-all-done.2 = bf16[16,2,24,128]{3,2,1,0:T(8,128)(2,1)S(1)} async-done(((bf16[16,2,24,128]{3,2,1,0:T(8,128)(2,1)}), bf16[16,2,24,128]{3,2,1,0:T(8,128)(2,1)S(1)}, u32[]{:S(2)}, u32[]{:S(2)}) %all-to-all-start.2) | async-done | bytes 196640 | tf_op jit(solution)/shard_map/all_to_all | solution.py:303
  99.0 4.5 %collective-permute-start.2 = (f32[2,24,128]{2,1,0:T(8,128)S(1)}, f32[2,24,128]{2,1,0:T(8,128)S(1)}, u32[]{:S(2)}, u32[]{:S(2)}) collective-permute-start(f32[2,24,128]{2,1,0:T(8,128)S(1)} %convert_reduce_fusion.1), channel_id=1, source_target_pairs={{0,256},{256,0},{1,257},{257,1},{2,258},{258,2},{3,259},{259,3},{4... | collective-permute-start | bytes 73736 | tf_op jit(solution)/shard_map/ppermute | solution.py:329
  103.5 0.0 collective-permute-done.1
  103.5 0.1 fusion
  103.7 1.4 collective-permute-done.2
  105.1 0.8 pad_maximum_fusion
  106.0 8.5 %all-to-all-start.3 = ((bf16[16,16,896]{2,1,0:T(8,128)(2,1)}), bf16[16,16,896]{2,1,0:T(8,128)(2,1)S(1)}, u32[]{:S(2)}, u32[]{:S(2)}) async-start(bf16[16,16,896]{2,1,0:T(8,128)(2,1)} %pad_maximum_fusion), calls=%async_computation.3 | async-start | bytes 917504 | tf_op jit(solution)/shard_map/all_to_all | solution.py:318
  114.4 0.1 dynamic_slice.20
  114.5 19.4 %all-to-all-done.3 = bf16[16,16,896]{2,1,0:T(8,128)(2,1)S(1)} async-done(((bf16[16,16,896]{2,1,0:T(8,128)(2,1)}), bf16[16,16,896]{2,1,0:T(8,128)(2,1)S(1)}, u32[]{:S(2)}, u32[]{:S(2)}) %all-to-all-start.3) | async-done | bytes 458784 | tf_op jit(solution)/shard_map/all_to_all | solution.py:318
  134.0 8.9 %collective-permute-start.3 = (bf16[16,16,384]{2,1,0:T(8,128)(2,1)S(1)}, bf16[16,16,384]{2,1,0:T(8,128)(2,1)S(1)}, u32[]{:S(2)}, u32[]{:S(2)}) collective-permute-start(bf16[16,16,384]{2,1,0:T(8,128)(2,1)S(1)} %slice.39.mine_ref), channel_id=1, source_target_pairs={{0,8},{8,0},{1,9},{9,1},{2,10},{10,2},{3,11},{11,3},{4,12},{12,4},... | collective-permute-start | bytes 589832 | tf_op jit(solution)/shard_map/ppermute | solution.py:329
  142.9 0.7 multiply_convert_fusion
  143.6 0.3 collective-permute-done.3.got_ref
  143.9 0.9 shard_map.113
  (11 shorter events, 0.2 us)
Async XLA Ops:
  8.8 23.2 %copy-start.2 = (bf16[96,512]{1,0:T(8,128)(2,1)S(1)}, bf16[96,512]{1,0:T(8,128)(2,1)}, u32[]{:S(2)}) copy-start(bf16[96,512]{1,0:T(8,128)(2,1)} %target_ref.1) | copy-start | bytes 294916
  34.6 3.8 %copy-start.3 = (bf16[1024]{0:T(1024)(128)(2,1)S(1)}, bf16[1024]{0:T(1024)(128)(2,1)}, u32[]{:S(2)}) copy-start(bf16[1024]{0:T(1024)(128)(2,1)} %param.11) | copy-start | bytes 6148
  34.7 15.8 %copy-start = (bf16[1024,512]{1,0:T(8,128)(2,1)S(1)}, bf16[1024,512]{1,0:T(8,128)(2,1)}, u32[]{:S(2)}) copy-start(bf16[1024,512]{1,0:T(8,128)(2,1)} %matrix_ref.3) | copy-start | bytes 3145732
  34.7 15.7 %copy-start.1 = (bf16[64,1024]{1,0:T(8,128)(2,1)S(1)}, bf16[64,1024]{1,0:T(8,128)(2,1)}, u32[]{:S(2)}) copy-start(bf16[64,1024]{1,0:T(8,128)(2,1)} %up_ref.3) | copy-start | bytes 393220
  34.7 15.7 %all-to-all-start.1 = ((bf16[8,96,704]{2,1,0:T(8,128)(2,1)}), bf16[8,96,704]{2,1,0:T(8,128)(2,1)S(1)}, u32[]{:S(2)}, u32[]{:S(2)}) async-start(bf16[8,96,704]{2,1,0:T(8,128)(2,1)} %get-tuple-element.14), calls=%async_computation.1 | async-start | bytes 2359296 | tf_op jit(solution)/shard_map/all_to_all | solution.py:290
  56.7 10.0 %collective-permute-start = (bf16[32,16,768]{2,1,0:T(8,128)(2,1)S(1)}, bf16[32,16,768]{2,1,0:T(8,128)(2,1)S(1)}, u32[]{:S(2)}, u32[]{:S(2)}) collective-permute-start(bf16[32,16,768]{2,1,0:T(8,128)(2,1)S(1)} %get-tuple-element.16), channel_id=1, source_target_pairs={{0,8},{8,0},{1,9},{9,1},{2,10},{10,2},{3,11},{11,3},{4,12},{12,4},... | collective-permute-start | bytes 2359304 | tf_op jit(solution)/shard_map/ppermute | solution.py:329
  67.5 31.5 %all-to-all-start.2 = ((bf16[16,2,24,128]{3,2,1,0:T(8,128)(2,1)}), bf16[16,2,24,128]{3,2,1,0:T(8,128)(2,1)S(1)}, u32[]{:S(2)}, u32[]{:S(2)}) async-start(bf16[16,2,24,128]{3,2,1,0:T(8,128)(2,1)} %copy_bitcast_fusion), calls=%async_computation.2 | async-start | bytes 393216 | tf_op jit(solution)/shard_map/all_to_all | solution.py:303
  86.2 17.3 %collective-permute-start.1 = (bf16[16,16,512]{2,1,0:T(8,128)(2,1)S(1)}, bf16[16,16,512]{2,1,0:T(8,128)(2,1)S(1)}, u32[]{:S(2)}, u32[]{:S(2)}) collective-permute-start(bf16[16,16,512]{2,1,0:T(8,128)(2,1)S(1)} %fusion.1), channel_id=1, source_target_pairs={{0,256},{256,0},{1,257},{257,1},{2,258},{258,2},{3,259},{259,3},{4... | collective-permute-start | bytes 786440 | tf_op jit(solution)/shard_map/ppermute | solution.py:329
  99.0 6.1 %collective-permute-start.2 = (f32[2,24,128]{2,1,0:T(8,128)S(1)}, f32[2,24,128]{2,1,0:T(8,128)S(1)}, u32[]{:S(2)}, u32[]{:S(2)}) collective-permute-start(f32[2,24,128]{2,1,0:T(8,128)S(1)} %convert_reduce_fusion.1), channel_id=1, source_target_pairs={{0,256},{256,0},{1,257},{257,1},{2,258},{258,2},{3,259},{259,3},{4... | collective-permute-start | bytes 73736 | tf_op jit(solution)/shard_map/ppermute | solution.py:329
  106.0 28.0 %all-to-all-start.3 = ((bf16[16,16,896]{2,1,0:T(8,128)(2,1)}), bf16[16,16,896]{2,1,0:T(8,128)(2,1)S(1)}, u32[]{:S(2)}, u32[]{:S(2)}) async-start(bf16[16,16,896]{2,1,0:T(8,128)(2,1)} %pad_maximum_fusion), calls=%async_computation.3 | async-start | bytes 917504 | tf_op jit(solution)/shard_map/all_to_all | solution.py:318
  134.0 10.0 %collective-permute-start.3 = (bf16[16,16,384]{2,1,0:T(8,128)(2,1)S(1)}, bf16[16,16,384]{2,1,0:T(8,128)(2,1)S(1)}, u32[]{:S(2)}, u32[]{:S(2)}) collective-permute-start(bf16[16,16,384]{2,1,0:T(8,128)(2,1)S(1)} %slice.39.mine_ref), channel_id=1, source_target_pairs={{0,8},{8,0},{1,9},{9,1},{2,10},{10,2},{3,11},{11,3},{4,12},{12,4},... | collective-permute-start | bytes 589832 | tf_op jit(solution)/shard_map/ppermute | solution.py:329

commit v5 on v4

--- a/solution.py
+++ b/solution.py
@@ -10,7 +10,8 @@
 MODEL_WIDTH = 8192
 EPSILON = 1e-06
 TP = ("x", "y_lo")
-ROWS = ("y_hi", "z", "core")
+Z = ("z_pair", "z_odd")
+ROWS = ("y_hi", *Z, "core")
 bf16 = jnp.bfloat16
 f32 = jnp.float32
 NN = (((1,), (0,)), ((), ()))
@@ -38,7 +39,7 @@
     share, resid_ref, heads_ref, gain_ref, matrix_ref, down_ref, up_ref, out_ref, weights_ref
 ):
     rank, width = up_ref.shape[0], matrix_ref.shape[1]
-    gain = gain_ref[...].astype(f32)
+    gain = gain_ref[...].astype(f32).reshape(1, -1)
 
     @pl.when(pl.program_id(0) == 0)
     def _():
@@ -52,9 +53,9 @@
     values = dot((wide * gain).astype(bf16), matrix_ref[...])
     small = [dot(heads_ref[...], down_ref[...], NT), dot(resid, up_ref[...], NT)]
     small = jnp.concatenate(small, axis=1)
-    high, low = split(wide * wide)
-    ones = jnp.ones((rank, wide.shape[1]), bf16)
+    squares = jnp.sum(wide * wide, axis=1, keepdims=True)
     line = lax.broadcasted_iota(jnp.int32, (rank, share // 2), 0)
+    diagonal = line[: share // 2] == lax.broadcasted_iota(jnp.int32, (share // 2, share // 2), 1)
     for piece in range(out_ref.shape[0]):
         rows = slice(piece * share, (piece + 1) * share)
         out_ref[piece, :share, :width] = values[rows].astype(bf16)
@@ -62,10 +63,10 @@
         lines = jnp.zeros(line.shape, f32)
         for part in range(2):
             rows = slice(piece * share + part * (share // 2), piece * share + (part + 1) * (share // 2))
-            squares = dot(ones, high[rows], NT) + dot(ones, low[rows], NT)
-            first = squares.astype(bf16).astype(f32)
+            across = jnp.sum(jnp.where(diagonal, squares[rows], 0.0), axis=0, keepdims=True)
+            first = across.astype(bf16).astype(f32)
             lines = jnp.where(line == part, first, lines)
-            lines = jnp.where(line == 2 + part, squares - first, lines)
+            lines = jnp.where(line == 2 + part, across - first, lines)
         blank = [jnp.zeros((rank, rank), f32), lines, jnp.zeros((rank, rank - share // 2), f32)]
         out_ref[piece, share:, :width] = weights_ref[:, :width].astype(bf16)
         tail = weights_ref[:, width:] + jnp.concatenate(blank, axis=1)
@@ -84,7 +85,7 @@
         in_specs=[
             pl.BlockSpec((rows, features), lambda i: (i, 0)),
             pl.BlockSpec((rows, features), lambda i: (i, 0)),
-            pl.BlockSpec((1, features), whole),
+            pl.BlockSpec((features,), lambda i: (0,)),
             pl.BlockSpec((features, width), whole),
             pl.BlockSpec(down.shape, whole),
             pl.BlockSpec(up.shape, whole),
@@ -163,7 +164,7 @@
 
 
 def gradients_kernel(
-    core_ref, every_ref, resid_ref, heads_ref, up_ref, gain_ref, matrix_ref,
+    z_size, core_ref, every_ref, resid_ref, heads_ref, up_ref, gain_ref, matrix_ref,
     kept_ref, small_ref, sent_ref, cross_ref,
 ):
     width = matrix_ref.shape[1]
@@ -179,10 +180,11 @@
 
     core = core_ref[0]
     matrix = matrix_ref[...]
-    hidden = (resid_ref[...].astype(f32) + 0.5 * dot(down, up_ref[...])).astype(bf16)
-    value = dot(hidden, error, TN)
-    a_part = dot(heads_ref[...], every_ref[:, width + rank : width + 2 * rank], TN)
-    b_part = dot(hidden, every_ref[:, width + 2 * rank :], TN)
+    hidden = lax.dot_general(up_ref[...], down, (((0,), (1,)), ((), ())), preferred_element_type=f32)
+    hidden = (resid_ref[...].astype(f32) + 0.5 * hidden).astype(bf16)
+    value = dot(hidden, error)
+    a_part = dot(heads_ref[...], every_ref[:, width + rank : width + 2 * rank])
+    b_part = dot(hidden, every_ref[:, width + 2 * rank :])
     crossed = dot(matrix, cross_ref[0]) + dot(matrix, cross_ref[1])
     b_part = 0.5 * (gain_ref[...] * crossed - b_part)
     small = jnp.concatenate([a_part, b_part], axis=1)
@@ -193,7 +195,8 @@
     spread = jnp.where(lane == line, gain_part, 0.0).reshape(2 * group, own, LANES)
     gain_line = jnp.sum(spread, axis=1, keepdims=True)
     row = lax.broadcasted_iota(jnp.int32, (2 * group, own, LANES), 1)
-    gain_line = jnp.where(row == 0, gain_line, 0.0)
+    piece = pl.program_id(0) * group + lax.broadcasted_iota(jnp.int32, row.shape, 0) // 2
+    gain_line = jnp.where(row == piece // z_size, gain_line, 0.0)
     small = jnp.concatenate([small.reshape(2 * group, own, -1), gain_line], axis=2)
     small = small.reshape(group, 2, own, -1)
     value = value.reshape(group, 2, own, width)
@@ -204,8 +207,8 @@
     sent_ref[:, :, width:] = jnp.where(first, small[:, 1], small[:, 0]).astype(bf16)
 
 
-def gradients(core, every, resid, heads, up, gain, matrix, own):
-    tokens, features = resid.shape
+def gradients(core, every, resid, heads, up, gain, matrix, own, z_size):
+    features, tokens = resid.shape
     width, rank = matrix.shape[1], up.shape[0]
     block = 256
     pieces, group = features // (2 * own), block // (2 * own)
@@ -215,13 +218,13 @@
         jax.ShapeDtypeStruct((pieces, own, width + 2 * rank + LANES), bf16),
     ]
     return pl.pallas_call(
-        gradients_kernel,
+        functools.partial(gradients_kernel, z_size),
         grid=(features // block,),
         in_specs=[
             pl.BlockSpec(memory_space=pltpu.SMEM),
             pl.BlockSpec(every.shape, lambda i: (0, 0)),
-            pl.BlockSpec((tokens, block), lambda i: (0, i)),
-            pl.BlockSpec((tokens, block), lambda i: (0, i)),
+            pl.BlockSpec((block, tokens), lambda i: (i, 0)),
+            pl.BlockSpec((block, tokens), lambda i: (i, 0)),
             pl.BlockSpec((rank, block), lambda i: (0, i)),
             pl.BlockSpec((block, 1), lambda i: (i, 0)),
             pl.BlockSpec((block, width), lambda i: (i, 0)),
@@ -254,7 +257,7 @@
                     jnp.where(first, mine[:, lanes], got[:, lanes]),
                     jnp.where(first, got[:, lanes], mine[:, lanes]),
                 ]
-                gain_line += (mine + got)[y * 8 : y * 8 + 1, 2 * LANES :]
+                gain_line += (mine + got)[y : y + 1, 2 * LANES :]
             both = jnp.concatenate(lines, axis=0).T
             place = y * (features // 2) + start * 2 * own
             a_ref[:, place : place + LANES] = both[:rank]
@@ -284,42 +287,49 @@
     core = lax.axis_index("core")
     gain = scale.astype(f32)
 
-    pieces = project(resid, heads, scale.reshape(1, -1), value_matrix, down_matrix.T, up, share)
+    pieces = project(resid, heads, scale, value_matrix, down_matrix.T, up, share)
     pieces = lax.all_to_all(pieces, TP, 0, 0, tiled=True)
     values, every = owner(pieces, target, 1.0 / tokens**0.5)
     every = lax.all_to_all(every, TP, 0, 0, tiled=True)
     every = every.reshape(tp * share, -1)
 
-    y_size, z_size, core_size = (lax.axis_size(a) for a in ROWS)
+    y_size, z_size, core_size = (lax.axis_size(a) for a in ("y_hi", Z, "core"))
     own = features // (y_size * z_size * core_size)
     kept, small, sent = gradients(
-        core.reshape(1), every, resid, heads, up, gain[:, None], value_matrix, own
+        core.reshape(1), every, resid.T, heads.T, up, gain[:, None], value_matrix, own, z_size
     )
 
     got = swap(sent, "core")
-    small = small + got[:, :, width:].astype(f32)
-    small = jnp.concatenate([small[:, :, : 2 * rank], small[:, :8, 2 * rank :]], axis=1)
-    small = small.astype(bf16).reshape(y_size, z_size, own + 8, -1).transpose(1, 0, 2, 3)
-    small = lax.all_to_all(small, "z", 0, 0, tiled=True)
-
-    me = lax.axis_index("y_hi")
-    kept = kept.reshape(y_size, z_size, own, width)
-    got = got.reshape(y_size, z_size, own, -1)[..., :width]
-    pick = lambda x, i: lax.dynamic_index_in_dim(x, i, 0, keepdims=False).astype(f32)
-    other = swap((pick(kept, 1 - me) + pick(got, 1 - me)).astype(bf16), "y_hi")
-    value = (pick(kept, me) + pick(got, me) + other.astype(f32)).astype(bf16)
+    small = (small + got[:, :, width:].astype(f32)).astype(bf16)
+    small = small.reshape(y_size, z_size, own, -1)
+    gains = small[0, :, :8, 2 * rank :] + small[1, :, :8, 2 * rank :]
+    small = small[..., : 2 * rank].transpose(1, 0, 2, 3).reshape(z_size, y_size * own, -1)
+    small = jnp.concatenate([small, gains], axis=1)
+    small = lax.all_to_all(small, Z, 0, 0, tiled=True)
+
+    half, got = width // 2, got[:, :, :width]
+    odd, me = lax.axis_index("z_odd"), lax.axis_index("y_hi")
+    columns = lambda x, i: lax.dynamic_slice_in_dim(x, i * half, half, 2).astype(f32)
+    other = swap((columns(kept, 1 - odd) + columns(got, 1 - odd)).astype(bf16), "z_odd")
+    value = columns(kept, odd) + columns(got, odd) + other.astype(f32)
+    value = value.reshape(y_size, z_size, own, half)
+    rows = lambda x, i: lax.dynamic_index_in_dim(x, i, 0, keepdims=False)
+    other = swap(rows(value, 1 - me).astype(bf16), "y_hi")
+    value = (rows(value, me) + other.astype(f32)).astype(bf16)
 
     small = jnp.sum(small.astype(f32), axis=0)
     small = (small + swap(small, "y_hi")).astype(bf16)
 
-    gains = small[:, own:].reshape(-1, small.shape[-1])
-    small = jnp.concatenate([*small[:, :own], gains], axis=1)
+    gains = jnp.pad(small[y_size * own :], ((0, own - 8), (0, 0)))
+    small = [small[i * own : (i + 1) * own] for i in range(y_size)]
+    small = jnp.concatenate([*small, gains], axis=1)
     small = jnp.broadcast_to(small, (z_size, *small.shape))
-    value = lax.all_to_all(jnp.concatenate([value, small], axis=2), "z", 0, 0, tiled=True)
-    small = value[:, :, width:]
+    value = lax.all_to_all(jnp.concatenate([value, small], axis=2), Z, 0, 0, tiled=True)
+    small = value[:, :, half:]
     a_grad, b_grad, gain_grad = assemble(core.reshape(1), small, swap(small, "core"), rank)
 
-    value = jnp.sum(value[:, :, :width].astype(f32), axis=0)
+    value = value[:, :, :half].astype(f32).reshape(-1, 2, own, half)
+    value = jnp.concatenate([*jnp.sum(value, axis=0)], axis=1)
     own_gain = lax.dynamic_slice_in_dim(gain, lax.axis_index(ROWS) * own, own, 0)
     value_grad = (value * own_gain[:, None]).astype(bf16)
     return (values, value_grad, a_grad.T, b_grad, gain_grad.reshape(-1))
@@ -331,9 +341,10 @@
 
 def solution(mesh):
     rows, tp = mesh.shape["rows"], mesh.shape["tp"]
-    y_hi, core, y_lo = 2, 2, 2
+    y_hi, z_odd, core, y_lo = 2, 2, 2, 2
+    z_pair = rows // (y_hi * z_odd * core)
     fine = Mesh(
-        mesh.devices.reshape(y_hi, rows // (y_hi * core), core, tp // y_lo, y_lo), (*ROWS, *TP)
+        mesh.devices.reshape(y_hi, z_pair, z_odd, core, tp // y_lo, y_lo), (*ROWS, *TP)
     )
     in_specs = (
         P(ROWS, TP),

time: 146 us -> 143 us (0.979)
  waiting for transfers between devices: 43 us -> 32.5 us
  local copies, waits for them, and re-layouts: 1.74 us -> 5.59 us
  starting transfers between devices: 56.8 us -> 59.8 us
    ppermute x4 -> x5, starting transfers between devices: 26.1 us -> 34.3 us  [swap(): return lax.ppermute(x, axis, [(0, 1), (1, 0)])]
    all_to_all x2, waiting for transfers between devices: 27.6 us -> 21.2 us  [the longest x1 13.6 us: body(): lax.all_to_all(jnp.concatenate([value, small], axis=2), Z, 0, 0, tiled=True)]
    all_to_all x2, starting transfers between devices: 27 us -> 21.8 us  [the longest x1 14 us: body(): small = lax.all_to_all(small, Z, 0, 0, tiled=True)]
    unnamed x8 -> x14, local copies, waits for them, and re-layouts: 0.02 us -> 5.11 us
    all_to_all x1, waiting for transfers between devices: 11.8 us -> 7.46 us  [body(): every = lax.all_to_all(every, TP, 0, 0, tiled=True)]
    ppermute x4 -> x5, waiting for transfers between devices: 3.6 us -> 3.9 us  [swap(): return lax.ppermute(x, axis, [(0, 1), (1, 0)])]
  transfers between devices with their start and end apart: 7 -> 8, of which waited for: 6 -> 6; matrix products, arithmetic and copies ran while one was open for 1% -> 4% of each run, Pallas kernels for 0% -> 0%
where the time goes in v5:
time: 143 us; the launch traced here: 142 us
  starting transfers between devices  59.8 us (42%)
  waiting for transfers between devices  32.5 us (23%)
  blocking collectives  23.2 us (16%)
  Pallas kernels  16.3 us (11%)
  local copies, waits for them, and re-layouts  5.59 us (4%)
  other arithmetic  3.57 us (2%)
    ppermute x5, starting transfers between devices, swap(): return lax.ppermute(x, axis, [(0, 1), (1, 0)])  34.3 us
    all_to_all x1, blocking collectives, body(): pieces = lax.all_to_all(pieces, TP, 0, 0, tiled=True)  23.2 us
    all_to_all x1, starting transfers between devices, body(): small = lax.all_to_all(small, Z, 0, 0, tiled=True)  14 us
    all_to_all x1, waiting for transfers between devices, body(): lax.all_to_all(jnp.concatenate([value, small], axis=2), Z, 0, 0, tiled=True)  13.6 us
    all_to_all x1, starting transfers between devices, body(): lax.all_to_all(jnp.concatenate([value, small], axis=2), Z, 0, 0, tiled=True)  7.74 us
    all_to_all x1, waiting for transfers between devices, body(): small = lax.all_to_all(small, Z, 0, 0, tiled=True)  7.51 us
    all_to_all x1, waiting for transfers between devices, body(): every = lax.all_to_all(every, TP, 0, 0, tiled=True)  7.46 us
    pallas_call x1, Pallas kernels, gradients(): pl.pallas_call(functools.partial(gradients_kernel, z_size), grid=(feature...  6.6 us
  transfers between devices with their start and end apart: 8, of which 6 were waited for; matrix products, arithmetic and copies ran while one was open for 4% of the time, Pallas kernels for 0%

profile of v5, /device:TPU:1, one launch (start us, length us, event | category | flops | bytes accessed | tf_op | source)
XLA Modules:
  0.0 141.8 jit_solution(14994707916546246534)
XLA Ops:
  0.6 6.2 %shard_map.110 = bf16[8,160,640]{2,1,0:T(8,128)(2,1)} custom-call(bf16[768,1024]{1,0:T(8,128)(2,1)} %resid_ref.1, bf16[768,1024]{1,0:T(8,128)(2,1)} %heads_ref.1, bf16[1024]{0:T(1024)(128)(2,1)} %gain_ref.1, bf16[1024,512]{1,0:T(8,128)(2,1)} %matrix_ref.3, bf16[64,1024]{1,0:T(8,128)(2,1)} %bitcast.36, bf16[64,1024]{1,0:T(8,128)(2,1)} %up_ref.3), custom_call_target="tpu_custom_call" | custom-call | flops 1207959552 | bytes 4194304 | tf_op jit(solution)/shard_map/pallas_call | solution.py:82
  6.8 0.0 copy-start.3
  6.8 23.2 %all_to_all.20.pieces_ref = bf16[8,160,640]{2,1,0:T(8,128)(2,1)S(1)} all-to-all(bf16[8,160,640]{2,1,0:T(8,128)(2,1)} %shard_map.110), channel_id=1, replica_groups=mesh['y_hi'=2,'z_pair'=8,'z_odd'=2,'core'=2,'x'=4,'y_lo'=2] {'x','y_lo'}, dimensions={0} | all-to-all | bytes 3276800 | tf_op jit(solution)/shard_map/all_to_all | solution.py:291
  30.0 0.0 copy-done.3
  30.0 2.6 %shard_map.111 = (bf16[96,512]{1,0:T(8,128)(2,1)}, bf16[8,96,704]{2,1,0:T(8,128)(2,1)}) custom-call(bf16[8,160,640]{2,1,0:T(8,128)(2,1)S(1)} %all_to_all.20.pieces_ref, bf16[96,512]{1,0:T(8,128)(2,1)S(1)} %copy-done.3), custom_call_target="tpu_custom_call" | custom-call | tf_op jit(solution)/shard_map/pallas_call | solution.py:153
  32.6 0.0 copy-start.4
  32.6 3.7 %all-to-all-start.1 = ((bf16[8,96,704]{2,1,0:T(8,128)(2,1)}), bf16[8,96,704]{2,1,0:T(8,128)(2,1)S(1)}, u32[]{:S(2)}, u32[]{:S(2)}) async-start(bf16[8,96,704]{2,1,0:T(8,128)(2,1)} %get-tuple-element.14), calls=%async_computation.1 | async-start | bytes 2359296 | tf_op jit(solution)/shard_map/all_to_all | solution.py:293
  36.3 0.0 copy-done.4
  36.4 1.6 %copy.14 = bf16[768,1024]{0,1:T(8,128)(2,1)} copy(bf16[768,1024]{1,0:T(8,128)(2,1)S(1)} %copy-done.4) | data formatting | bytes 3145728 | tf_op args[0]
  38.0 0.0 copy-start.5
  38.0 0.0 copy-start
  38.0 0.0 copy-start.1
  38.0 2.7 %copy.15 = bf16[768,1024]{0,1:T(8,128)(2,1)} copy(bf16[768,1024]{1,0:T(8,128)(2,1)} %heads_ref.1) | data formatting | bytes 3145728 | tf_op args[1]
  40.7 0.0 copy-done.5
  40.7 0.2 copy.16.gain_ref
  40.9 7.5 %all-to-all-done.1 = bf16[8,96,704]{2,1,0:T(8,128)(2,1)S(1)} async-done(((bf16[8,96,704]{2,1,0:T(8,128)(2,1)}), bf16[8,96,704]{2,1,0:T(8,128)(2,1)S(1)}, u32[]{:S(2)}, u32[]{:S(2)}) %all-to-all-start.1) | async-done | bytes 1081376 | tf_op jit(solution)/shard_map/all_to_all | solution.py:293
  48.3 0.0 copy-done
  48.3 0.0 copy-done.1
  48.4 6.6 %shard_map.112 = (bf16[32,16,512]{2,1,0:T(8,128)(2,1)S(1)}, f32[32,16,256]{2,1,0:T(8,128)S(1)}, bf16[32,16,768]{2,1,0:T(8,128)(2,1)}) custom-call(s32[1]{0:T(128)} %bitcast.1.core_ref, bf16[768,704]{1,0:T(8,128)(2,1)S(1)} %bitcast.27, bf16[1024,768]{1,0:T(8,128)(2,1)} %bitcast.28, bf16[1024,768]{1,0:T(8,128)(2,1)} %bitcast.29, ...), custom_call_target="tpu_custom_call" | custom-call | flops 1207959552 | bytes 7340032 | tf_op jit(solution)/shard_map/pallas_call | solution.py:220
  55.0 0.0 copy-start.2
  55.0 0.8 copy-done.2
  55.7 8.1 %collective-permute-start = (bf16[32,16,768]{2,1,0:T(8,128)(2,1)}, bf16[32,16,768]{2,1,0:T(8,128)(2,1)S(1)}, u32[]{:S(2)}, u32[]{:S(2)}) collective-permute-start(bf16[32,16,768]{2,1,0:T(8,128)(2,1)} %get-tuple-element.16), channel_id=1, source_target_pairs={{0,8},{8,0},{1,9},{9,1},{2,10},{10,2},{3,11},{11,3},{4,12},{12,4},... | collective-permute-start | bytes 2359304 | tf_op jit(solution)/shard_map/ppermute | solution.py:339
  63.8 2.1 %collective-permute-done = bf16[32,16,768]{2,1,0:T(8,128)(2,1)S(1)} collective-permute-done((bf16[32,16,768]{2,1,0:T(8,128)(2,1)}, bf16[32,16,768]{2,1,0:T(8,128)(2,1)S(1)}, u32[]{:S(2)}, u32[]{:S(2)}) %collective-permute-start) | collective-permute-done | bytes 786464 | tf_op jit(solution)/shard_map/ppermute | solution.py:339
  65.9 1.1 add_convert_fusion
  67.1 0.1 slice.40
  67.2 0.1 add_convert_fusion.1
  67.3 7.2 %collective-permute-start.1 = (bf16[32,16,256]{2,1,0:T(8,128)(2,1)S(1)}, bf16[32,16,256]{2,1,0:T(8,128)(2,1)S(1)}, u32[]{:S(2)}, u32[]{:S(2)}) collective-permute-start(bf16[32,16,256]{2,1,0:T(8,128)(2,1)S(1)} %add_convert_fusion.1), channel_id=1, source_target_pairs={{0,16},{16,0},{1,17},{17,1},{2,18},{18,2},{3,19},{19,3},{4,20},{20... | collective-permute-start | bytes 786440 | tf_op jit(solution)/shard_map/ppermute | solution.py:339
  74.5 0.7 pad_maximum_fusion.1
  75.2 14.0 %all-to-all-start.2 = ((bf16[16,40,128]{2,1,0:T(8,128)(2,1)}), bf16[16,40,128]{2,1,0:T(8,128)(2,1)S(1)}, u32[]{:S(2)}, u32[]{:S(2)}) async-start(bf16[16,40,128]{2,1,0:T(8,128)(2,1)} %pad_maximum_fusion.1), calls=%async_computation.2 | async-start | bytes 327680 | tf_op jit(solution)/shard_map/all_to_all | solution.py:308
  89.2 0.0 collective-permute-done.1
  89.2 0.1 convert_add_fusion
  89.4 4.5 %collective-permute-start.2 = (bf16[16,16,256]{2,1,0:T(8,128)(2,1)S(1)}, bf16[16,16,256]{2,1,0:T(8,128)(2,1)S(1)}, u32[]{:S(2)}, u32[]{:S(2)}) collective-permute-start(bf16[16,16,256]{2,1,0:T(8,128)(2,1)S(1)} %fusion.1), channel_id=1, source_target_pairs={{0,256},{256,0},{1,257},{257,1},{2,258},{258,2},{3,259},{259,3},{4... | collective-permute-start | bytes 393224 | tf_op jit(solution)/shard_map/ppermute | solution.py:339
  93.9 7.5 %all-to-all-done.2 = bf16[16,40,128]{2,1,0:T(8,128)(2,1)S(1)} async-done(((bf16[16,40,128]{2,1,0:T(8,128)(2,1)}), bf16[16,40,128]{2,1,0:T(8,128)(2,1)S(1)}, u32[]{:S(2)}, u32[]{:S(2)}) %all-to-all-start.2) | async-done | bytes 163872 | tf_op jit(solution)/shard_map/all_to_all | solution.py:308
  101.5 4.5 %collective-permute-start.3 = (f32[40,128]{1,0:T(8,128)S(1)}, f32[40,128]{1,0:T(8,128)S(1)}, u32[]{:S(2)}, u32[]{:S(2)}) collective-permute-start(f32[40,128]{1,0:T(8,128)S(1)} %convert_reduce_fusion), channel_id=1, source_target_pairs={{0,256},{256,0},{1,257},{257,1},{2,258},{258,2},{3,259},{259,3},{4... | collective-permute-start | bytes 61448 | tf_op jit(solution)/shard_map/ppermute | solution.py:339
  106.0 0.0 collective-permute-done.2
  106.1 1.4 %collective-permute-done.3 = f32[40,128]{1,0:T(8,128)S(1)} collective-permute-done((f32[40,128]{1,0:T(8,128)S(1)}, f32[40,128]{1,0:T(8,128)S(1)}, u32[]{:S(2)}, u32[]{:S(2)}) %collective-permute-start.3) | collective-permute-done | bytes 20512 | tf_op jit(solution)/shard_map/ppermute | solution.py:339
  107.6 0.8 pad_maximum_fusion
  108.3 7.7 %all-to-all-start.3 = ((bf16[16,16,640]{2,1,0:T(8,128)(2,1)}), bf16[16,16,640]{2,1,0:T(8,128)(2,1)S(1)}, u32[]{:S(2)}, u32[]{:S(2)}) async-start(bf16[16,16,640]{2,1,0:T(8,128)(2,1)} %pad_maximum_fusion), calls=%async_computation.3 | async-start | bytes 655360 | tf_op jit(solution)/shard_map/all_to_all | solution.py:327
  116.1 0.1 dynamic_slice.28
  116.2 13.6 %all-to-all-done.3 = bf16[16,16,640]{2,1,0:T(8,128)(2,1)S(1)} async-done(((bf16[16,16,640]{2,1,0:T(8,128)(2,1)}), bf16[16,16,640]{2,1,0:T(8,128)(2,1)S(1)}, u32[]{:S(2)}, u32[]{:S(2)}) %all-to-all-start.3) | async-done | bytes 327712 | tf_op jit(solution)/shard_map/all_to_all | solution.py:327
  129.9 10.0 %collective-permute-start.4 = (bf16[16,16,384]{2,1,0:T(8,128)(2,1)S(1)}, bf16[16,16,384]{2,1,0:T(8,128)(2,1)S(1)}, u32[]{:S(2)}, u32[]{:S(2)}) collective-permute-start(bf16[16,16,384]{2,1,0:T(8,128)(2,1)S(1)} %slice.49.mine_ref), channel_id=1, source_target_pairs={{0,8},{8,0},{1,9},{9,1},{2,10},{10,2},{3,11},{11,3},{4,12},{12,4},... | collective-permute-start | bytes 589832 | tf_op jit(solution)/shard_map/ppermute | solution.py:339
  139.9 0.7 fusion.3
  140.5 0.4 collective-permute-done.4.got_ref
  140.9 0.9 shard_map.113
  (16 shorter events, 0.2 us)
Async XLA Ops:
  6.8 23.2 %copy-start.3 = (bf16[96,512]{1,0:T(8,128)(2,1)S(1)}, bf16[96,512]{1,0:T(8,128)(2,1)}, u32[]{:S(2)}) copy-start(bf16[96,512]{1,0:T(8,128)(2,1)} %target_ref.1) | copy-start | bytes 294916
  32.6 3.7 %copy-start.4 = (bf16[768,1024]{1,0:T(8,128)(2,1)S(1)}, bf16[768,1024]{1,0:T(8,128)(2,1)}, u32[]{:S(2)}) copy-start(bf16[768,1024]{1,0:T(8,128)(2,1)} %resid_ref.1) | copy-start | bytes 4718596
  32.6 15.7 %all-to-all-start.1 = ((bf16[8,96,704]{2,1,0:T(8,128)(2,1)}), bf16[8,96,704]{2,1,0:T(8,128)(2,1)S(1)}, u32[]{:S(2)}, u32[]{:S(2)}) async-start(bf16[8,96,704]{2,1,0:T(8,128)(2,1)} %get-tuple-element.14), calls=%async_computation.1 | async-start | bytes 2359296 | tf_op jit(solution)/shard_map/all_to_all | solution.py:293
  38.0 2.7 %copy-start.5 = (bf16[1024]{0:T(1024)(128)(2,1)S(1)}, bf16[1024]{0:T(1024)(128)(2,1)}, u32[]{:S(2)}) copy-start(bf16[1024]{0:T(1024)(128)(2,1)} %gain_ref.1) | copy-start | bytes 6148
  38.0 10.4 %copy-start = (bf16[1024,512]{1,0:T(8,128)(2,1)S(1)}, bf16[1024,512]{1,0:T(8,128)(2,1)}, u32[]{:S(2)}) copy-start(bf16[1024,512]{1,0:T(8,128)(2,1)} %matrix_ref.3) | copy-start | bytes 3145732
  38.0 10.4 %copy-start.1 = (bf16[64,1024]{1,0:T(8,128)(2,1)S(1)}, bf16[64,1024]{1,0:T(8,128)(2,1)}, u32[]{:S(2)}) copy-start(bf16[64,1024]{1,0:T(8,128)(2,1)} %up_ref.3) | copy-start | bytes 393220
  55.0 0.8 copy-start.2
  55.7 10.2 %collective-permute-start = (bf16[32,16,768]{2,1,0:T(8,128)(2,1)}, bf16[32,16,768]{2,1,0:T(8,128)(2,1)S(1)}, u32[]{:S(2)}, u32[]{:S(2)}) collective-permute-start(bf16[32,16,768]{2,1,0:T(8,128)(2,1)} %get-tuple-element.16), channel_id=1, source_target_pairs={{0,8},{8,0},{1,9},{9,1},{2,10},{10,2},{3,11},{11,3},{4,12},{12,4},... | collective-permute-start | bytes 2359304 | tf_op jit(solution)/shard_map/ppermute | solution.py:339
  67.3 22.0 %collective-permute-start.1 = (bf16[32,16,256]{2,1,0:T(8,128)(2,1)S(1)}, bf16[32,16,256]{2,1,0:T(8,128)(2,1)S(1)}, u32[]{:S(2)}, u32[]{:S(2)}) collective-permute-start(bf16[32,16,256]{2,1,0:T(8,128)(2,1)S(1)} %add_convert_fusion.1), channel_id=1, source_target_pairs={{0,16},{16,0},{1,17},{17,1},{2,18},{18,2},{3,19},{19,3},{4,20},{20... | collective-permute-start | bytes 786440 | tf_op jit(solution)/shard_map/ppermute | solution.py:339
  75.2 26.2 %all-to-all-start.2 = ((bf16[16,40,128]{2,1,0:T(8,128)(2,1)}), bf16[16,40,128]{2,1,0:T(8,128)(2,1)S(1)}, u32[]{:S(2)}, u32[]{:S(2)}) async-start(bf16[16,40,128]{2,1,0:T(8,128)(2,1)} %pad_maximum_fusion.1), calls=%async_computation.2 | async-start | bytes 327680 | tf_op jit(solution)/shard_map/all_to_all | solution.py:308
  89.4 16.6 %collective-permute-start.2 = (bf16[16,16,256]{2,1,0:T(8,128)(2,1)S(1)}, bf16[16,16,256]{2,1,0:T(8,128)(2,1)S(1)}, u32[]{:S(2)}, u32[]{:S(2)}) collective-permute-start(bf16[16,16,256]{2,1,0:T(8,128)(2,1)S(1)} %fusion.1), channel_id=1, source_target_pairs={{0,256},{256,0},{1,257},{257,1},{2,258},{258,2},{3,259},{259,3},{4... | collective-permute-start | bytes 393224 | tf_op jit(solution)/shard_map/ppermute | solution.py:339
  101.5 6.0 %collective-permute-start.3 = (f32[40,128]{1,0:T(8,128)S(1)}, f32[40,128]{1,0:T(8,128)S(1)}, u32[]{:S(2)}, u32[]{:S(2)}) collective-permute-start(f32[40,128]{1,0:T(8,128)S(1)} %convert_reduce_fusion), channel_id=1, source_target_pairs={{0,256},{256,0},{1,257},{257,1},{2,258},{258,2},{3,259},{259,3},{4... | collective-permute-start | bytes 61448 | tf_op jit(solution)/shard_map/ppermute | solution.py:339
  108.3 21.5 %all-to-all-start.3 = ((bf16[16,16,640]{2,1,0:T(8,128)(2,1)}), bf16[16,16,640]{2,1,0:T(8,128)(2,1)S(1)}, u32[]{:S(2)}, u32[]{:S(2)}) async-start(bf16[16,16,640]{2,1,0:T(8,128)(2,1)} %pad_maximum_fusion), calls=%async_computation.3 | async-start | bytes 655360 | tf_op jit(solution)/shard_map/all_to_all | solution.py:327
  129.9 11.0 %collective-permute-start.4 = (bf16[16,16,384]{2,1,0:T(8,128)(2,1)S(1)}, bf16[16,16,384]{2,1,0:T(8,128)(2,1)S(1)}, u32[]{:S(2)}, u32[]{:S(2)}) collective-permute-start(bf16[16,16,384]{2,1,0:T(8,128)(2,1)S(1)} %slice.49.mine_ref), channel_id=1, source_target_pairs={{0,8},{8,0},{1,9},{9,1},{2,10},{10,2},{3,11},{11,3},{4,12},{12,4},... | collective-permute-start | bytes 589832 | tf_op jit(solution)/shard_map/ppermute | solution.py:339

commit v6 on v5

--- a/solution.py
+++ b/solution.py
@@ -20,6 +20,7 @@
 LANES = 128
 VMEM_LIMIT = 48 * 2**20
 VMEM_WHOLE = 60 * 2**20
+VMEM_SOME = 16 * 2**20
 
 
 def dot(a, b, dims=NN):
@@ -76,7 +77,7 @@
 def project(resid, heads, gain, matrix, down, up, share):
     tokens, features = resid.shape
     rank, width = up.shape[0], matrix.shape[1]
-    pieces, group = tokens // share, 2
+    pieces, group = tokens // share, 4
     rows, columns = group * share, width + 2 * rank
     whole = lambda i: (0, 0)
     return pl.pallas_call(
@@ -210,7 +211,7 @@
 def gradients(core, every, resid, heads, up, gain, matrix, own, z_size):
     features, tokens = resid.shape
     width, rank = matrix.shape[1], up.shape[0]
-    block = 256
+    block = 512
     pieces, group = features // (2 * own), block // (2 * own)
     shapes = [
         jax.ShapeDtypeStruct((pieces, own, width), bf16),
@@ -239,6 +240,34 @@
             transcendentals=0,
         ),
     )(core, every, resid, heads, up, gain, matrix)
+
+
+def small_kernel(small_ref, got_ref, out_ref):
+    z_size = out_ref.shape[0]
+    y_size = small_ref.shape[0] // z_size
+    small = small_ref[...] + got_ref[...].astype(f32)
+    for z in range(z_size):
+        places = [y * z_size + z for y in range(y_size)]
+        lines = [small[i, :, :LANES] for i in places]
+        gains = functools.reduce(jnp.add, [small[i, :8, LANES:] for i in places])
+        out_ref[z] = jnp.concatenate([*lines, gains], axis=0).astype(bf16)
+
+
+def small_pieces(small, got, y_size):
+    pieces, own, columns = small.shape
+    z_size = pieces // y_size
+    last = got.shape[2] // columns - 1
+    return pl.pallas_call(
+        small_kernel,
+        grid=(1,),
+        in_specs=[
+            pl.BlockSpec(small.shape, lambda i: (0, 0, 0)),
+            pl.BlockSpec(small.shape, lambda i: (0, 0, last)),
+        ],
+        out_specs=pl.BlockSpec((z_size, y_size * own + 8, LANES), lambda i: (0, 0, 0)),
+        out_shape=jax.ShapeDtypeStruct((z_size, y_size * own + 8, LANES), bf16),
+        compiler_params=pltpu.CompilerParams(vmem_limit_bytes=VMEM_SOME),
+    )(small, got)
 
 
 def assemble_kernel(core_ref, mine_ref, got_ref, a_ref, b_ref, gain_ref):
@@ -300,22 +329,26 @@
     )
 
     got = swap(sent, "core")
-    small = (small + got[:, :, width:].astype(f32)).astype(bf16)
-    small = small.reshape(y_size, z_size, own, -1)
-    gains = small[0, :, :8, 2 * rank :] + small[1, :, :8, 2 * rank :]
-    small = small[..., : 2 * rank].transpose(1, 0, 2, 3).reshape(z_size, y_size * own, -1)
-    small = jnp.concatenate([small, gains], axis=1)
+    small = small_pieces(small, got, y_size)
     small = lax.all_to_all(small, Z, 0, 0, tiled=True)
 
     half, got = width // 2, got[:, :, :width]
     odd, me = lax.axis_index("z_odd"), lax.axis_index("y_hi")
-    columns = lambda x, i: lax.dynamic_slice_in_dim(x, i * half, half, 2).astype(f32)
-    other = swap((columns(kept, 1 - odd) + columns(got, 1 - odd)).astype(bf16), "z_odd")
-    value = columns(kept, odd) + columns(got, odd) + other.astype(f32)
-    value = value.reshape(y_size, z_size, own, half)
-    rows = lambda x, i: lax.dynamic_index_in_dim(x, i, 0, keepdims=False)
-    other = swap(rows(value, 1 - me).astype(bf16), "y_hi")
-    value = (rows(value, me) + other.astype(f32)).astype(bf16)
+
+    def quarter(y, z):
+        parts = [x.reshape(y_size, z_size, own, width) for x in (kept, got)]
+        parts = [lax.dynamic_index_in_dim(x, y, 0, keepdims=False) for x in parts]
+        parts = [lax.dynamic_slice_in_dim(x, z * half, half, 2) for x in parts]
+        return parts[0].astype(f32) + parts[1].astype(f32)
+
+    value = quarter(me, odd)
+    for y, z, axis in (
+        (me, 1 - odd, "z_odd"),
+        (1 - me, odd, "y_hi"),
+        (1 - me, 1 - odd, ("y_hi", "z_odd")),
+    ):
+        value = value + swap(quarter(y, z).astype(bf16), axis).astype(f32)
+    value = value.astype(bf16)
 
     small = jnp.sum(small.astype(f32), axis=0)
     small = (small + swap(small, "y_hi")).astype(bf16)
@@ -336,7 +369,8 @@
 
 
 def swap(x, axis):
-    return lax.ppermute(x, axis, [(0, 1), (1, 0)])
+    last = lax.axis_size(axis) - 1
+    return lax.ppermute(x, axis, [(i, last - i) for i in range(last + 1)])
 
 
 def solution(mesh):

time: 143 us -> 138 us (0.965)
  waiting for transfers between devices: 32.5 us -> 26.5 us
  starting transfers between devices: 59.8 us -> 64.6 us
  other arithmetic: 3.57 us -> 2.01 us
    all_to_all x1, waiting for transfers between devices: 7.51 us -> 2.05 us  [body(): small = lax.all_to_all(small, Z, 0, 0, tiled=True)]
    all_to_all x1, starting transfers between devices: 14 us -> 18.6 us  [body(): small = lax.all_to_all(small, Z, 0, 0, tiled=True)]
    all_to_all x1, starting transfers between devices: 7.74 us -> 9.62 us  [body(): lax.all_to_all(jnp.concatenate([value, small], axis=2), Z, 0, 0, tiled=True)]
    ppermute x5 -> x6, starting transfers between devices: 34.3 us -> 32.6 us  [swap(): return lax.ppermute(x, axis, [(i, last - i) for i in range(last + 1)])]
    unnamed x14 -> x12, local copies, waits for them, and re-layouts: 5.11 us -> 4.3 us
    ppermute x5 -> x6, waiting for transfers between devices: 3.9 us -> 3.56 us  [swap(): return lax.ppermute(x, axis, [(i, last - i) for i in range(last + 1)])]
  transfers between devices with their start and end apart: 8 -> 9, of which waited for: 6 -> 6; matrix products, arithmetic and copies ran while one was open for 4% -> 4% of each run, Pallas kernels for 0% -> 0%
where the time goes in v6:
time: 138 us; the launch traced here: 137 us
  starting transfers between devices  64.6 us (47%)
  waiting for transfers between devices  26.5 us (19%)
  blocking collectives  23.2 us (17%)
  Pallas kernels  15.1 us (11%)
  local copies, waits for them, and re-layouts  4.72 us (3%)
  other arithmetic  2.01 us (1%)
    ppermute x6, starting transfers between devices, swap(): return lax.ppermute(x, axis, [(i, last - i) for i in range(last + 1)])  32.6 us
    all_to_all x1, blocking collectives, body(): pieces = lax.all_to_all(pieces, TP, 0, 0, tiled=True)  23.2 us
    all_to_all x1, starting transfers between devices, body(): small = lax.all_to_all(small, Z, 0, 0, tiled=True)  18.6 us
    all_to_all x1, waiting for transfers between devices, body(): lax.all_to_all(jnp.concatenate([value, small], axis=2), Z, 0, 0, tiled=True)  13.4 us
    all_to_all x1, starting transfers between devices, body(): lax.all_to_all(jnp.concatenate([value, small], axis=2), Z, 0, 0, tiled=True)  9.62 us
    all_to_all x1, waiting for transfers between devices, body(): every = lax.all_to_all(every, TP, 0, 0, tiled=True)  7.47 us
    pallas_call x1, Pallas kernels, gradients(): pl.pallas_call(functools.partial(gradients_kernel, z_size), grid=(feature...  5.52 us
    pallas_call x1, Pallas kernels, project(): pl.pallas_call(functools.partial(project_kernel, share), grid=(pieces //...  5.38 us
  transfers between devices with their start and end apart: 9, of which 6 were waited for; matrix products, arithmetic and copies ran while one was open for 4% of the time, Pallas kernels for 0%

profile of v6, /device:TPU:1, one launch (start us, length us, event | category | flops | bytes accessed | tf_op | source)
XLA Modules:
  0.0 137.0 jit_solution(3080342842351024101)
XLA Ops:
  0.6 5.4 %shard_map.110 = bf16[8,160,640]{2,1,0:T(8,128)(2,1)} custom-call(bf16[768,1024]{1,0:T(8,128)(2,1)} %resid_ref.1, bf16[768,1024]{1,0:T(8,128)(2,1)} %heads_ref.1, bf16[1024]{0:T(1024)(128)(2,1)} %gain_ref.1, bf16[1024,512]{1,0:T(8,128)(2,1)} %matrix_ref.3, bf16[64,1024]{1,0:T(8,128)(2,1)} %bitcast.38, bf16[64,1024]{1,0:T(8,128)(2,1)} %up_ref.3), custom_call_target="tpu_custom_call" | custom-call | flops 1207959552 | bytes 4194304 | tf_op jit(solution)/shard_map/pallas_call | solution.py:83
  6.0 0.0 copy-start.2
  6.0 23.2 %all_to_all.20.pieces_ref = bf16[8,160,640]{2,1,0:T(8,128)(2,1)S(1)} all-to-all(bf16[8,160,640]{2,1,0:T(8,128)(2,1)} %shard_map.110), channel_id=1, replica_groups=mesh['y_hi'=2,'z_pair'=8,'z_odd'=2,'core'=2,'x'=4,'y_lo'=2] {'x','y_lo'}, dimensions={0} | all-to-all | bytes 3276800 | tf_op jit(solution)/shard_map/all_to_all | solution.py:320
  29.2 0.0 copy-done.2
  29.2 2.6 %shard_map.111 = (bf16[96,512]{1,0:T(8,128)(2,1)}, bf16[8,96,704]{2,1,0:T(8,128)(2,1)}) custom-call(bf16[8,160,640]{2,1,0:T(8,128)(2,1)S(1)} %all_to_all.20.pieces_ref, bf16[96,512]{1,0:T(8,128)(2,1)S(1)} %copy-done.2), custom_call_target="tpu_custom_call" | custom-call | tf_op jit(solution)/shard_map/pallas_call | solution.py:154
  31.8 0.0 copy-start.3
  31.8 3.7 %all-to-all-start.1 = ((bf16[8,96,704]{2,1,0:T(8,128)(2,1)}), bf16[8,96,704]{2,1,0:T(8,128)(2,1)S(1)}, u32[]{:S(2)}, u32[]{:S(2)}) async-start(bf16[8,96,704]{2,1,0:T(8,128)(2,1)} %get-tuple-element.14), calls=%async_computation.1 | async-start | bytes 2359296 | tf_op jit(solution)/shard_map/all_to_all | solution.py:322
  35.6 0.0 copy-done.3
  35.6 1.6 %copy.14 = bf16[768,1024]{0,1:T(8,128)(2,1)} copy(bf16[768,1024]{1,0:T(8,128)(2,1)S(1)} %copy-done.3) | data formatting | bytes 3145728 | tf_op args[0]
  37.2 0.0 copy-start.4
  37.2 0.0 copy-start
  37.2 0.0 copy-start.1
  37.2 2.7 %copy.15 = bf16[768,1024]{0,1:T(8,128)(2,1)} copy(bf16[768,1024]{1,0:T(8,128)(2,1)} %heads_ref.1) | data formatting | bytes 3145728 | tf_op args[1]
  39.9 0.0 copy-done.4
  39.9 0.2 copy.16.gain_ref
  40.1 7.5 %all-to-all-done.1 = bf16[8,96,704]{2,1,0:T(8,128)(2,1)S(1)} async-done(((bf16[8,96,704]{2,1,0:T(8,128)(2,1)}), bf16[8,96,704]{2,1,0:T(8,128)(2,1)S(1)}, u32[]{:S(2)}, u32[]{:S(2)}) %all-to-all-start.1) | async-done | bytes 1081376 | tf_op jit(solution)/shard_map/all_to_all | solution.py:322
  47.6 0.0 copy-done
  47.6 0.0 copy-done.1
  47.6 5.5 %shard_map.112 = (bf16[32,16,512]{2,1,0:T(8,128)(2,1)S(1)}, f32[32,16,256]{2,1,0:T(8,128)S(1)}, bf16[32,16,768]{2,1,0:T(8,128)(2,1)S(1)}) custom-call(s32[1]{0:T(128)} %bitcast.1.core_ref, bf16[768,704]{1,0:T(8,128)(2,1)S(1)} %bitcast.30, bf16[1024,768]{1,0:T(8,128)(2,1)} %bitcast.33, bf16[1024,768]{1,0:T(8,128)(2,1)} %bitcast.34, ...), custom_call_target="tpu_custom_call" | custom-call | flops 1207959552 | bytes 7340032 | tf_op jit(solution)/shard_map/pallas_call | solution.py:221
  53.1 8.1 %collective-permute-start = (bf16[32,16,768]{2,1,0:T(8,128)(2,1)S(1)}, bf16[32,16,768]{2,1,0:T(8,128)(2,1)S(1)}, u32[]{:S(2)}, u32[]{:S(2)}) collective-permute-start(bf16[32,16,768]{2,1,0:T(8,128)(2,1)S(1)} %get-tuple-element.16), channel_id=1, source_target_pairs={{0,8},{8,0},{1,9},{9,1},{2,10},{10,2},{3,11},{11,3},{4,12},{12,4},... | collective-permute-start | bytes 2359304 | tf_op jit(solution)/shard_map/ppermute | solution.py:373
  61.2 1.9 %collective-permute-done.got_ref = bf16[32,16,768]{2,1,0:T(8,128)(2,1)S(1)} collective-permute-done((bf16[32,16,768]{2,1,0:T(8,128)(2,1)S(1)}, bf16[32,16,768]{2,1,0:T(8,128)(2,1)S(1)}, u32[]{:S(2)}, u32[]{:S(2)}) %collective-permute-start) | collective-permute-done | bytes 786464 | tf_op jit(solution)/shard_map/ppermute | solution.py:373
  63.0 0.7 shard_map.113
  63.8 18.6 %all-to-all-start.2 = ((bf16[16,40,128]{2,1,0:T(8,128)(2,1)}), bf16[16,40,128]{2,1,0:T(8,128)(2,1)S(1)}, u32[]{:S(2)}, u32[]{:S(2)}) async-start(bf16[16,40,128]{2,1,0:T(8,128)(2,1)} %shard_map.113), calls=%async_computation.2 | async-start | bytes 327680 | tf_op jit(solution)/shard_map/all_to_all | solution.py:333
  82.4 0.1 slice.24
  82.5 0.3 fusion.3
  82.8 5.6 %collective-permute-start.3 = (bf16[16,16,256]{2,1,0:T(8,128)(2,1)S(1)}, bf16[16,16,256]{2,1,0:T(8,128)(2,1)S(1)}, u32[]{:S(2)}, u32[]{:S(2)}) collective-permute-start(bf16[16,16,256]{2,1,0:T(8,128)(2,1)S(1)} %get-tuple-element.22), channel_id=1, source_target_pairs={{0,272},{16,256},{256,16},{272,0},{1,273},{17,257},{257,17},{273,1... | collective-permute-start | bytes 393224 | tf_op jit(solution)/shard_map/ppermute | solution.py:373
  88.4 2.3 %collective-permute-start.2 = (bf16[16,16,256]{2,1,0:T(8,128)(2,1)S(1)}, bf16[16,16,256]{2,1,0:T(8,128)(2,1)S(1)}, u32[]{:S(2)}, u32[]{:S(2)}) collective-permute-start(bf16[16,16,256]{2,1,0:T(8,128)(2,1)S(1)} %get-tuple-element.23), channel_id=1, source_target_pairs={{0,256},{256,0},{1,257},{257,1},{2,258},{258,2},{3,259},{259,3},{4... | collective-permute-start | bytes 393224 | tf_op jit(solution)/shard_map/ppermute | solution.py:373
  90.7 2.0 %collective-permute-start.1 = (bf16[16,16,256]{2,1,0:T(8,128)(2,1)S(1)}, bf16[16,16,256]{2,1,0:T(8,128)(2,1)S(1)}, u32[]{:S(2)}, u32[]{:S(2)}) collective-permute-start(bf16[16,16,256]{2,1,0:T(8,128)(2,1)S(1)} %get-tuple-element.21), channel_id=1, source_target_pairs={{0,16},{16,0},{1,17},{17,1},{2,18},{18,2},{3,19},{19,3},{4,20},{20... | collective-permute-start | bytes 393224 | tf_op jit(solution)/shard_map/ppermute | solution.py:373
  92.7 2.0 %all-to-all-done.2 = bf16[16,40,128]{2,1,0:T(8,128)(2,1)S(1)} async-done(((bf16[16,40,128]{2,1,0:T(8,128)(2,1)}), bf16[16,40,128]{2,1,0:T(8,128)(2,1)S(1)}, u32[]{:S(2)}, u32[]{:S(2)}) %all-to-all-start.2) | async-done | bytes 163872 | tf_op jit(solution)/shard_map/all_to_all | solution.py:333
  94.8 4.5 %collective-permute-start.4 = (f32[40,128]{1,0:T(8,128)S(1)}, f32[40,128]{1,0:T(8,128)S(1)}, u32[]{:S(2)}, u32[]{:S(2)}) collective-permute-start(f32[40,128]{1,0:T(8,128)S(1)} %convert_reduce_fusion), channel_id=1, source_target_pairs={{0,256},{256,0},{1,257},{257,1},{2,258},{258,2},{3,259},{259,3},{4... | collective-permute-start | bytes 61448 | tf_op jit(solution)/shard_map/ppermute | solution.py:373
  99.3 0.0 collective-permute-done.3
  99.3 0.0 collective-permute-done.2
  99.3 0.0 collective-permute-done.1
  99.3 0.2 fusion.2
  99.5 1.3 collective-permute-done.4
  100.9 0.7 pad_maximum_fusion
  101.6 9.6 %all-to-all-start.3 = ((bf16[16,16,640]{2,1,0:T(8,128)(2,1)}), bf16[16,16,640]{2,1,0:T(8,128)(2,1)S(1)}, u32[]{:S(2)}, u32[]{:S(2)}) async-start(bf16[16,16,640]{2,1,0:T(8,128)(2,1)} %pad_maximum_fusion), calls=%async_computation.3 | async-start | bytes 655360 | tf_op jit(solution)/shard_map/all_to_all | solution.py:360
  111.3 0.1 dynamic_slice.44
  111.4 13.4 %all-to-all-done.3 = bf16[16,16,640]{2,1,0:T(8,128)(2,1)S(1)} async-done(((bf16[16,16,640]{2,1,0:T(8,128)(2,1)}), bf16[16,16,640]{2,1,0:T(8,128)(2,1)S(1)}, u32[]{:S(2)}, u32[]{:S(2)}) %all-to-all-start.3) | async-done | bytes 327712 | tf_op jit(solution)/shard_map/all_to_all | solution.py:360
  124.9 10.2 %collective-permute-start.5 = (bf16[16,16,384]{2,1,0:T(8,128)(2,1)S(1)}, bf16[16,16,384]{2,1,0:T(8,128)(2,1)S(1)}, u32[]{:S(2)}, u32[]{:S(2)}) collective-permute-start(bf16[16,16,384]{2,1,0:T(8,128)(2,1)S(1)} %slice.29.mine_ref), channel_id=1, source_target_pairs={{0,8},{8,0},{1,9},{9,1},{2,10},{10,2},{3,11},{11,3},{4,12},{12,4},... | collective-permute-start | bytes 589832 | tf_op jit(solution)/shard_map/ppermute | solution.py:373
  135.0 0.7 fusion.6
  135.7 0.4 collective-permute-done.5.got_ref
  136.1 0.9 shard_map.114
  (11 shorter events, 0.1 us)
Async XLA Ops:
  6.0 23.2 %copy-start.2 = (bf16[96,512]{1,0:T(8,128)(2,1)S(1)}, bf16[96,512]{1,0:T(8,128)(2,1)}, u32[]{:S(2)}) copy-start(bf16[96,512]{1,0:T(8,128)(2,1)} %target_ref.1) | copy-start | bytes 294916
  31.8 3.7 %copy-start.3 = (bf16[768,1024]{1,0:T(8,128)(2,1)S(1)}, bf16[768,1024]{1,0:T(8,128)(2,1)}, u32[]{:S(2)}) copy-start(bf16[768,1024]{1,0:T(8,128)(2,1)} %resid_ref.1) | copy-start | bytes 4718596
  31.8 15.7 %all-to-all-start.1 = ((bf16[8,96,704]{2,1,0:T(8,128)(2,1)}), bf16[8,96,704]{2,1,0:T(8,128)(2,1)S(1)}, u32[]{:S(2)}, u32[]{:S(2)}) async-start(bf16[8,96,704]{2,1,0:T(8,128)(2,1)} %get-tuple-element.14), calls=%async_computation.1 | async-start | bytes 2359296 | tf_op jit(solution)/shard_map/all_to_all | solution.py:322
  37.2 2.7 %copy-start.4 = (bf16[1024]{0:T(1024)(128)(2,1)S(1)}, bf16[1024]{0:T(1024)(128)(2,1)}, u32[]{:S(2)}) copy-start(bf16[1024]{0:T(1024)(128)(2,1)} %gain_ref.1) | copy-start | bytes 6148
  37.2 10.4 %copy-start = (bf16[1024,512]{1,0:T(8,128)(2,1)S(1)}, bf16[1024,512]{1,0:T(8,128)(2,1)}, u32[]{:S(2)}) copy-start(bf16[1024,512]{1,0:T(8,128)(2,1)} %matrix_ref.3) | copy-start | bytes 3145732
  37.2 10.4 %copy-start.1 = (bf16[64,1024]{1,0:T(8,128)(2,1)S(1)}, bf16[64,1024]{1,0:T(8,128)(2,1)}, u32[]{:S(2)}) copy-start(bf16[64,1024]{1,0:T(8,128)(2,1)} %up_ref.3) | copy-start | bytes 393220
  53.1 9.9 %collective-permute-start = (bf16[32,16,768]{2,1,0:T(8,128)(2,1)S(1)}, bf16[32,16,768]{2,1,0:T(8,128)(2,1)S(1)}, u32[]{:S(2)}, u32[]{:S(2)}) collective-permute-start(bf16[32,16,768]{2,1,0:T(8,128)(2,1)S(1)} %get-tuple-element.16), channel_id=1, source_target_pairs={{0,8},{8,0},{1,9},{9,1},{2,10},{10,2},{3,11},{11,3},{4,12},{12,4},... | collective-permute-start | bytes 2359304 | tf_op jit(solution)/shard_map/ppermute | solution.py:373
  63.8 31.0 %all-to-all-start.2 = ((bf16[16,40,128]{2,1,0:T(8,128)(2,1)}), bf16[16,40,128]{2,1,0:T(8,128)(2,1)S(1)}, u32[]{:S(2)}, u32[]{:S(2)}) async-start(bf16[16,40,128]{2,1,0:T(8,128)(2,1)} %shard_map.113), calls=%async_computation.2 | async-start | bytes 327680 | tf_op jit(solution)/shard_map/all_to_all | solution.py:333
  82.8 16.5 %collective-permute-start.3 = (bf16[16,16,256]{2,1,0:T(8,128)(2,1)S(1)}, bf16[16,16,256]{2,1,0:T(8,128)(2,1)S(1)}, u32[]{:S(2)}, u32[]{:S(2)}) collective-permute-start(bf16[16,16,256]{2,1,0:T(8,128)(2,1)S(1)} %get-tuple-element.22), channel_id=1, source_target_pairs={{0,272},{16,256},{256,16},{272,0},{1,273},{17,257},{257,17},{273,1... | collective-permute-start | bytes 393224 | tf_op jit(solution)/shard_map/ppermute | solution.py:373
  88.4 10.9 %collective-permute-start.2 = (bf16[16,16,256]{2,1,0:T(8,128)(2,1)S(1)}, bf16[16,16,256]{2,1,0:T(8,128)(2,1)S(1)}, u32[]{:S(2)}, u32[]{:S(2)}) collective-permute-start(bf16[16,16,256]{2,1,0:T(8,128)(2,1)S(1)} %get-tuple-element.23), channel_id=1, source_target_pairs={{0,256},{256,0},{1,257},{257,1},{2,258},{258,2},{3,259},{259,3},{4... | collective-permute-start | bytes 393224 | tf_op jit(solution)/shard_map/ppermute | solution.py:373
  90.7 8.7 %collective-permute-start.1 = (bf16[16,16,256]{2,1,0:T(8,128)(2,1)S(1)}, bf16[16,16,256]{2,1,0:T(8,128)(2,1)S(1)}, u32[]{:S(2)}, u32[]{:S(2)}) collective-permute-start(bf16[16,16,256]{2,1,0:T(8,128)(2,1)S(1)} %get-tuple-element.21), channel_id=1, source_target_pairs={{0,16},{16,0},{1,17},{17,1},{2,18},{18,2},{3,19},{19,3},{4,20},{20... | collective-permute-start | bytes 393224 | tf_op jit(solution)/shard_map/ppermute | solution.py:373
  94.8 6.0 %collective-permute-start.4 = (f32[40,128]{1,0:T(8,128)S(1)}, f32[40,128]{1,0:T(8,128)S(1)}, u32[]{:S(2)}, u32[]{:S(2)}) collective-permute-start(f32[40,128]{1,0:T(8,128)S(1)} %convert_reduce_fusion), channel_id=1, source_target_pairs={{0,256},{256,0},{1,257},{257,1},{2,258},{258,2},{3,259},{259,3},{4... | collective-permute-start | bytes 61448 | tf_op jit(solution)/shard_map/ppermute | solution.py:373
  101.6 23.1 %all-to-all-start.3 = ((bf16[16,16,640]{2,1,0:T(8,128)(2,1)}), bf16[16,16,640]{2,1,0:T(8,128)(2,1)S(1)}, u32[]{:S(2)}, u32[]{:S(2)}) async-start(bf16[16,16,640]{2,1,0:T(8,128)(2,1)} %pad_maximum_fusion), calls=%async_computation.3 | async-start | bytes 655360 | tf_op jit(solution)/shard_map/all_to_all | solution.py:360
  124.9 11.2 %collective-permute-start.5 = (bf16[16,16,384]{2,1,0:T(8,128)(2,1)S(1)}, bf16[16,16,384]{2,1,0:T(8,128)(2,1)S(1)}, u32[]{:S(2)}, u32[]{:S(2)}) collective-permute-start(bf16[16,16,384]{2,1,0:T(8,128)(2,1)S(1)} %slice.29.mine_ref), channel_id=1, source_target_pairs={{0,8},{8,0},{1,9},{9,1},{2,10},{10,2},{3,11},{11,3},{4,12},{12,4},... | collective-permute-start | bytes 589832 | tf_op jit(solution)/shard_map/ppermute | solution.py:373

commit v7 on v6

--- a/solution.py
+++ b/solution.py
@@ -103,7 +103,7 @@
     )(resid, heads, gain, matrix, down, up)
 
 
-def owner_kernel(loss_scale, pieces_ref, target_ref, values_ref, every_ref, sent_ref, sems):
+def owner_kernel(loss_scale, pieces_ref, target_ref, values_ref, every_ref):
     share, width = target_ref.shape
     tp = pieces_ref.shape[0]
     rank = pieces_ref.shape[1] - share
@@ -136,14 +136,12 @@
     down_grad = dot_split(high, through, NT) + dot(low, through[0], NT)
     down_grad = 0.5 * inverse_rms * (down_grad - inner * inverse_rms * hidden_up)
     weighted = down_wide * (inner * inverse_rms * inverse_rms)
-    sent_ref[:, :width] = (error * inverse_rms).astype(bf16)
-    sent_ref[:, width : width + 2 * rank] = jnp.concatenate([down_wide, down_grad], axis=1).astype(bf16)
-    sent_ref[:, width + 2 * rank :] = weighted.astype(bf16)
-    copies = [pltpu.make_async_copy(sent_ref, every_ref.at[i], sems.at[i]) for i in range(tp)]
-    for copy in copies:
-        copy.start()
-    for copy in copies:
-        copy.wait()
+    small = jnp.concatenate([down_wide, down_grad], axis=1).astype(bf16)
+    error, weighted = (error * inverse_rms).astype(bf16), weighted.astype(bf16)
+    for i in range(tp):
+        every_ref[i, :, :width] = error
+        every_ref[i, :, width : width + 2 * rank] = small
+        every_ref[i, :, width + 2 * rank :] = weighted
 
 
 def owner(pieces, target, loss_scale):
@@ -154,13 +152,12 @@
     return pl.pallas_call(
         functools.partial(owner_kernel, loss_scale),
         in_specs=[vmem, vmem],
-        out_specs=[vmem, pl.BlockSpec(memory_space=pl.ANY)],
+        out_specs=[vmem, vmem],
         out_shape=[
             jax.ShapeDtypeStruct((share, width), bf16),
             jax.ShapeDtypeStruct((tp, *sent), bf16),
         ],
-        scratch_shapes=[pltpu.VMEM(sent, bf16), pltpu.SemaphoreType.DMA((tp,))],
-        compiler_params=pltpu.CompilerParams(vmem_limit_bytes=VMEM_LIMIT),
+        compiler_params=pltpu.CompilerParams(vmem_limit_bytes=VMEM_SOME),
     )(pieces, target)
 
 
@@ -270,37 +267,35 @@
     )(small, got)
 
 
-def assemble_kernel(core_ref, mine_ref, got_ref, a_ref, b_ref, gain_ref):
-    z_size, own = mine_ref.shape[:2]
+def assemble_kernel(own, core_ref, mine_ref, got_ref, a_ref, b_ref, gain_ref):
+    z_size = mine_ref.shape[0]
     rank, features = a_ref.shape
     together = LANES // (2 * own)
     first = core_ref[0] == 0
-    for y in range(2):
-        for start in range(0, z_size, together):
-            lines, gain_line = [], jnp.zeros((1, LANES), f32)
-            for z in range(start, start + together):
-                mine = mine_ref[z].astype(f32)
-                got = got_ref[z].astype(f32)
-                lanes = slice(y * LANES, (y + 1) * LANES)
+    for start in range(0, z_size, together):
+        pairs = [(mine_ref[z].astype(f32), got_ref[z].astype(f32)) for z in range(start, start + together)]
+        gains = functools.reduce(jnp.add, [mine[2 * own :] + got[2 * own :] for mine, got in pairs])
+        for y in range(2):
+            lines, rows = [], slice(y * own, (y + 1) * own)
+            for mine, got in pairs:
                 lines += [
-                    jnp.where(first, mine[:, lanes], got[:, lanes]),
-                    jnp.where(first, got[:, lanes], mine[:, lanes]),
+                    jnp.where(first, mine[rows], got[rows]),
+                    jnp.where(first, got[rows], mine[rows]),
                 ]
-                gain_line += (mine + got)[y : y + 1, 2 * LANES :]
             both = jnp.concatenate(lines, axis=0).T
             place = y * (features // 2) + start * 2 * own
             a_ref[:, place : place + LANES] = both[:rank]
             b_ref[:, place : place + LANES] = both[rank:]
-            gain_ref[:, place : place + LANES] = gain_line
+            gain_ref[:, place : place + LANES] = gains[y : y + 1]
 
 
 def assemble(core, mine, got, rank):
-    z_size, own = mine.shape[:2]
+    z_size, own = mine.shape[0], (mine.shape[1] - 8) // 2
     features = 2 * z_size * 2 * own
     whole = jax.ShapeDtypeStruct((rank, features), f32)
     vmem = pl.BlockSpec(memory_space=pltpu.VMEM)
     return pl.pallas_call(
-        assemble_kernel,
+        functools.partial(assemble_kernel, own),
         in_specs=[pl.BlockSpec(memory_space=pltpu.SMEM), vmem, vmem],
         out_specs=[vmem, vmem, vmem],
         out_shape=[whole, whole, jax.ShapeDtypeStruct((1, features), f32)],
@@ -341,7 +336,7 @@
         parts = [lax.dynamic_slice_in_dim(x, z * half, half, 2) for x in parts]
         return parts[0].astype(f32) + parts[1].astype(f32)
 
-    value = quarter(me, odd)
+    small, value = lax.optimization_barrier((jnp.sum(small.astype(f32), axis=0), quarter(me, odd)))
     for y, z, axis in (
         (me, 1 - odd, "z_odd"),
         (1 - me, odd, "y_hi"),
@@ -350,19 +345,17 @@
         value = value + swap(quarter(y, z).astype(bf16), axis).astype(f32)
     value = value.astype(bf16)
 
-    small = jnp.sum(small.astype(f32), axis=0)
     small = (small + swap(small, "y_hi")).astype(bf16)
 
-    gains = jnp.pad(small[y_size * own :], ((0, own - 8), (0, 0)))
-    small = [small[i * own : (i + 1) * own] for i in range(y_size)]
-    small = jnp.concatenate([*small, gains], axis=1)
+    tiles = [value[:, :, i : i + LANES] for i in range(0, half, LANES)]
     small = jnp.broadcast_to(small, (z_size, *small.shape))
-    value = lax.all_to_all(jnp.concatenate([value, small], axis=2), Z, 0, 0, tiled=True)
-    small = value[:, :, half:]
+    value = lax.all_to_all(jnp.concatenate([*tiles, small], axis=1), Z, 0, 0, tiled=True)
+    lines = len(tiles) * own
+    small = value[:, lines:]
     a_grad, b_grad, gain_grad = assemble(core.reshape(1), small, swap(small, "core"), rank)
 
-    value = value[:, :, :half].astype(f32).reshape(-1, 2, own, half)
-    value = jnp.concatenate([*jnp.sum(value, axis=0)], axis=1)
+    value = value[:, :lines].astype(f32).reshape(-1, 2, len(tiles), own, LANES)
+    value = jnp.sum(value, axis=0).transpose(2, 0, 1, 3).reshape(own, width)
     own_gain = lax.dynamic_slice_in_dim(gain, lax.axis_index(ROWS) * own, own, 0)
     value_grad = (value * own_gain[:, None]).astype(bf16)
     return (values, value_grad, a_grad.T, b_grad, gain_grad.reshape(-1))

time: 138 us -> 136 us (0.986)
  no operation moved by 1% of the time
where the time goes in v7:
time: 136 us
  starting transfers between devices  64.2 us (47%)
  waiting for transfers between devices  26 us (19%)
  blocking collectives  23.2 us (17%)
  Pallas kernels  14.4 us (11%)
  local copies, waits for them, and re-layouts  4.79 us (4%)
  other arithmetic  2.01 us (1%)
    ppermute x6, starting transfers between devices, swap(): return lax.ppermute(x, axis, [(i, last - i) for i in range(last + 1)])  32.2 us
    all_to_all x1, blocking collectives, body(): pieces = lax.all_to_all(pieces, TP, 0, 0, tiled=True)  23.2 us
    all_to_all x1, starting transfers between devices, body(): small = lax.all_to_all(small, Z, 0, 0, tiled=True)  18.6 us
    all_to_all x1, waiting for transfers between devices, body(): lax.all_to_all(jnp.concatenate([*tiles, small], axis=1), Z, 0, 0, tiled=T...  13 us
    all_to_all x1, starting transfers between devices, body(): lax.all_to_all(jnp.concatenate([*tiles, small], axis=1), Z, 0, 0, tiled=T...  9.75 us
    all_to_all x1, waiting for transfers between devices, body(): every = lax.all_to_all(every, TP, 0, 0, tiled=True)  7.46 us
    pallas_call x1, Pallas kernels, gradients(): pl.pallas_call(functools.partial(gradients_kernel, z_size), grid=(feature...  5.52 us
    pallas_call x1, Pallas kernels, project(): pl.pallas_call(functools.partial(project_kernel, share), grid=(pieces //...  5.39 us
  transfers between devices with their start and end apart: 9, of which 6 were waited for; matrix products, arithmetic and copies ran while one was open for 4% of the time, Pallas kernels for 0%

profile of v7, /device:TPU:1, one launch (start us, length us, event | category | flops | bytes accessed | tf_op | source)
XLA Modules:
  0.0 135.5 jit_solution(3099881488504786159)
XLA Ops:
  0.6 5.4 %shard_map.110 = bf16[8,160,640]{2,1,0:T(8,128)(2,1)} custom-call(bf16[768,1024]{1,0:T(8,128)(2,1)} %resid_ref.1, bf16[768,1024]{1,0:T(8,128)(2,1)} %heads_ref.1, bf16[1024]{0:T(1024)(128)(2,1)} %gain_ref.1, bf16[1024,512]{1,0:T(8,128)(2,1)} %matrix_ref.3, bf16[64,1024]{1,0:T(8,128)(2,1)} %bitcast.27, bf16[64,1024]{1,0:T(8,128)(2,1)} %up_ref.3), custom_call_target="tpu_custom_call" | custom-call | flops 1207959552 | bytes 4194304 | tf_op jit(solution)/shard_map/pallas_call | solution.py:83
  6.0 0.0 copy-start.2
  6.0 23.2 %all_to_all.20.pieces_ref = bf16[8,160,640]{2,1,0:T(8,128)(2,1)S(1)} all-to-all(bf16[8,160,640]{2,1,0:T(8,128)(2,1)} %shard_map.110), channel_id=1, replica_groups=mesh['y_hi'=2,'z_pair'=8,'z_odd'=2,'core'=2,'x'=4,'y_lo'=2] {'x','y_lo'}, dimensions={0} | all-to-all | bytes 3276800 | tf_op jit(solution)/shard_map/all_to_all | solution.py:315
  29.2 0.0 copy-done.2
  29.2 1.9 %shard_map.111 = (bf16[96,512]{1,0:T(8,128)(2,1)}, bf16[8,96,704]{2,1,0:T(8,128)(2,1)}) custom-call(bf16[8,160,640]{2,1,0:T(8,128)(2,1)S(1)} %all_to_all.20.pieces_ref, bf16[96,512]{1,0:T(8,128)(2,1)S(1)} %copy-done.2), custom_call_target="tpu_custom_call" | custom-call | tf_op jit(solution)/shard_map/pallas_call | solution.py:152
  31.1 0.0 copy-start.3
  31.1 3.7 %all-to-all-start.1 = ((bf16[8,96,704]{2,1,0:T(8,128)(2,1)}), bf16[8,96,704]{2,1,0:T(8,128)(2,1)S(1)}, u32[]{:S(2)}, u32[]{:S(2)}) async-start(bf16[8,96,704]{2,1,0:T(8,128)(2,1)} %get-tuple-element.16), calls=%async_computation.1 | async-start | bytes 2359296 | tf_op jit(solution)/shard_map/all_to_all | solution.py:317
  34.9 0.0 copy-done.3
  34.9 1.6 %copy.20 = bf16[768,1024]{0,1:T(8,128)(2,1)} copy(bf16[768,1024]{1,0:T(8,128)(2,1)S(1)} %copy-done.3) | data formatting | bytes 3145728 | tf_op args[0]
  36.5 0.0 copy-start.4
  36.5 0.0 copy-start
  36.5 0.0 copy-start.1
  36.5 2.7 %copy.21 = bf16[768,1024]{0,1:T(8,128)(2,1)} copy(bf16[768,1024]{1,0:T(8,128)(2,1)} %heads_ref.1) | data formatting | bytes 3145728 | tf_op args[1]
  39.2 0.0 copy-done.4
  39.2 0.2 copy.22.gain_ref
  39.4 7.5 %all-to-all-done.1 = bf16[8,96,704]{2,1,0:T(8,128)(2,1)S(1)} async-done(((bf16[8,96,704]{2,1,0:T(8,128)(2,1)}), bf16[8,96,704]{2,1,0:T(8,128)(2,1)S(1)}, u32[]{:S(2)}, u32[]{:S(2)}) %all-to-all-start.1) | async-done | bytes 1081376 | tf_op jit(solution)/shard_map/all_to_all | solution.py:317
  46.9 0.0 copy-done
  46.9 0.0 copy-done.1
  46.9 5.5 %shard_map.112 = (bf16[32,16,512]{2,1,0:T(8,128)(2,1)S(1)}, f32[32,16,256]{2,1,0:T(8,128)S(1)}, bf16[32,16,768]{2,1,0:T(8,128)(2,1)S(1)}) custom-call(s32[1]{0:T(128)} %bitcast.1.core_ref, bf16[768,704]{1,0:T(8,128)(2,1)S(1)} %bitcast.21, bf16[1024,768]{1,0:T(8,128)(2,1)} %bitcast.23, bf16[1024,768]{1,0:T(8,128)(2,1)} %bitcast.24, ...), custom_call_target="tpu_custom_call" | custom-call | flops 1207959552 | bytes 7340032 | tf_op jit(solution)/shard_map/pallas_call | solution.py:218
  52.4 8.1 %collective-permute-start = (bf16[32,16,768]{2,1,0:T(8,128)(2,1)S(1)}, bf16[32,16,768]{2,1,0:T(8,128)(2,1)S(1)}, u32[]{:S(2)}, u32[]{:S(2)}) collective-permute-start(bf16[32,16,768]{2,1,0:T(8,128)(2,1)S(1)} %get-tuple-element.18), channel_id=1, source_target_pairs={{0,8},{8,0},{1,9},{9,1},{2,10},{10,2},{3,11},{11,3},{4,12},{12,4},... | collective-permute-start | bytes 2359304 | tf_op jit(solution)/shard_map/ppermute | solution.py:366
  60.5 1.9 %collective-permute-done.got_ref = bf16[32,16,768]{2,1,0:T(8,128)(2,1)S(1)} collective-permute-done((bf16[32,16,768]{2,1,0:T(8,128)(2,1)S(1)}, bf16[32,16,768]{2,1,0:T(8,128)(2,1)S(1)}, u32[]{:S(2)}, u32[]{:S(2)}) %collective-permute-start) | collective-permute-done | bytes 786464 | tf_op jit(solution)/shard_map/ppermute | solution.py:366
  62.4 0.7 shard_map.113
  63.1 18.6 %all-to-all-start.2 = ((bf16[16,40,128]{2,1,0:T(8,128)(2,1)}), bf16[16,40,128]{2,1,0:T(8,128)(2,1)S(1)}, u32[]{:S(2)}, u32[]{:S(2)}) async-start(bf16[16,40,128]{2,1,0:T(8,128)(2,1)} %shard_map.113), calls=%async_computation.2 | async-start | bytes 327680 | tf_op jit(solution)/shard_map/all_to_all | solution.py:328
  81.7 0.1 slice.20
  81.8 0.5 fusion
  82.2 5.6 %collective-permute-start.3 = (bf16[16,16,256]{2,1,0:T(8,128)(2,1)S(1)}, bf16[16,16,256]{2,1,0:T(8,128)(2,1)S(1)}, u32[]{:S(2)}, u32[]{:S(2)}) collective-permute-start(bf16[16,16,256]{2,1,0:T(8,128)(2,1)S(1)} %get-tuple-element.26), channel_id=1, source_target_pairs={{0,272},{16,256},{256,16},{272,0},{1,273},{17,257},{257,17},{273,1... | collective-permute-start | bytes 393224 | tf_op jit(solution)/shard_map/ppermute | solution.py:366
  87.8 2.3 %collective-permute-start.2 = (bf16[16,16,256]{2,1,0:T(8,128)(2,1)S(1)}, bf16[16,16,256]{2,1,0:T(8,128)(2,1)S(1)}, u32[]{:S(2)}, u32[]{:S(2)}) collective-permute-start(bf16[16,16,256]{2,1,0:T(8,128)(2,1)S(1)} %get-tuple-element.27), channel_id=1, source_target_pairs={{0,256},{256,0},{1,257},{257,1},{2,258},{258,2},{3,259},{259,3},{4... | collective-permute-start | bytes 393224 | tf_op jit(solution)/shard_map/ppermute | solution.py:366
  90.1 2.0 %collective-permute-start.1 = (bf16[16,16,256]{2,1,0:T(8,128)(2,1)S(1)}, bf16[16,16,256]{2,1,0:T(8,128)(2,1)S(1)}, u32[]{:S(2)}, u32[]{:S(2)}) collective-permute-start(bf16[16,16,256]{2,1,0:T(8,128)(2,1)S(1)} %get-tuple-element.25), channel_id=1, source_target_pairs={{0,16},{16,0},{1,17},{17,1},{2,18},{18,2},{3,19},{19,3},{4,20},{20... | collective-permute-start | bytes 393224 | tf_op jit(solution)/shard_map/ppermute | solution.py:366
  92.1 1.9 %all-to-all-done.2 = bf16[16,40,128]{2,1,0:T(8,128)(2,1)S(1)} async-done(((bf16[16,40,128]{2,1,0:T(8,128)(2,1)}), bf16[16,40,128]{2,1,0:T(8,128)(2,1)S(1)}, u32[]{:S(2)}, u32[]{:S(2)}) %all-to-all-start.2) | async-done | bytes 163872 | tf_op jit(solution)/shard_map/all_to_all | solution.py:328
  94.1 4.5 %collective-permute-start.4 = (f32[40,128]{1,0:T(8,128)S(1)}, f32[40,128]{1,0:T(8,128)S(1)}, u32[]{:S(2)}, u32[]{:S(2)}) collective-permute-start(f32[40,128]{1,0:T(8,128)S(1)} %convert_reduce_fusion), channel_id=1, source_target_pairs={{0,256},{256,0},{1,257},{257,1},{2,258},{258,2},{3,259},{259,3},{4... | collective-permute-start | bytes 61448 | tf_op jit(solution)/shard_map/ppermute | solution.py:366
  98.6 0.0 collective-permute-done.3
  98.6 0.0 collective-permute-done.2
  98.6 0.0 collective-permute-done.1
  98.6 0.1 add_convert_fusion
  98.7 1.4 %collective-permute-done.4 = f32[40,128]{1,0:T(8,128)S(1)} collective-permute-done((f32[40,128]{1,0:T(8,128)S(1)}, f32[40,128]{1,0:T(8,128)S(1)}, u32[]{:S(2)}, u32[]{:S(2)}) %collective-permute-start.4) | collective-permute-done | bytes 20512 | tf_op jit(solution)/shard_map/ppermute | solution.py:366
  100.2 0.7 pad_maximum_fusion
  100.9 9.8 %all-to-all-start.3 = ((bf16[16,72,128]{2,1,0:T(8,128)(2,1)}), bf16[16,72,128]{2,1,0:T(8,128)(2,1)S(1)}, u32[]{:S(2)}, u32[]{:S(2)}) async-start(bf16[16,72,128]{2,1,0:T(8,128)(2,1)} %pad_maximum_fusion), calls=%async_computation.3 | async-start | bytes 589824 | tf_op jit(solution)/shard_map/all_to_all | solution.py:352
  110.7 0.1 dynamic_slice.44
  110.8 13.0 %all-to-all-done.3 = bf16[16,72,128]{2,1,0:T(8,128)(2,1)S(1)} async-done(((bf16[16,72,128]{2,1,0:T(8,128)(2,1)}), bf16[16,72,128]{2,1,0:T(8,128)(2,1)S(1)}, u32[]{:S(2)}, u32[]{:S(2)}) %all-to-all-start.3) | async-done | bytes 294944 | tf_op jit(solution)/shard_map/all_to_all | solution.py:352
  123.9 9.7 %collective-permute-start.5 = (bf16[16,40,128]{2,1,0:T(8,128)(2,1)S(1)}, bf16[16,40,128]{2,1,0:T(8,128)(2,1)S(1)}, u32[]{:S(2)}, u32[]{:S(2)}) collective-permute-start(bf16[16,40,128]{2,1,0:T(8,128)(2,1)S(1)} %slice.24.mine_ref), channel_id=1, source_target_pairs={{0,8},{8,0},{1,9},{9,1},{2,10},{10,2},{3,11},{11,3},{4,12},{12,4},... | collective-permute-start | bytes 491528 | tf_op jit(solution)/shard_map/ppermute | solution.py:366
  133.6 0.7 multiply_convert_fusion
  134.3 0.3 collective-permute-done.5.got_ref
  134.6 0.9 shard_map.114
  (10 shorter events, 0.2 us)
Async XLA Ops:
  6.0 23.2 %copy-start.2 = (bf16[96,512]{1,0:T(8,128)(2,1)S(1)}, bf16[96,512]{1,0:T(8,128)(2,1)}, u32[]{:S(2)}) copy-start(bf16[96,512]{1,0:T(8,128)(2,1)} %target_ref.1) | copy-start | bytes 294916
  31.1 3.7 %copy-start.3 = (bf16[768,1024]{1,0:T(8,128)(2,1)S(1)}, bf16[768,1024]{1,0:T(8,128)(2,1)}, u32[]{:S(2)}) copy-start(bf16[768,1024]{1,0:T(8,128)(2,1)} %resid_ref.1) | copy-start | bytes 4718596
  31.1 15.7 %all-to-all-start.1 = ((bf16[8,96,704]{2,1,0:T(8,128)(2,1)}), bf16[8,96,704]{2,1,0:T(8,128)(2,1)S(1)}, u32[]{:S(2)}, u32[]{:S(2)}) async-start(bf16[8,96,704]{2,1,0:T(8,128)(2,1)} %get-tuple-element.16), calls=%async_computation.1 | async-start | bytes 2359296 | tf_op jit(solution)/shard_map/all_to_all | solution.py:317
  36.5 2.7 %copy-start.4 = (bf16[1024]{0:T(1024)(128)(2,1)S(1)}, bf16[1024]{0:T(1024)(128)(2,1)}, u32[]{:S(2)}) copy-start(bf16[1024]{0:T(1024)(128)(2,1)} %gain_ref.1) | copy-start | bytes 6148
  36.5 10.4 %copy-start = (bf16[1024,512]{1,0:T(8,128)(2,1)S(1)}, bf16[1024,512]{1,0:T(8,128)(2,1)}, u32[]{:S(2)}) copy-start(bf16[1024,512]{1,0:T(8,128)(2,1)} %matrix_ref.3) | copy-start | bytes 3145732
  36.5 10.4 %copy-start.1 = (bf16[64,1024]{1,0:T(8,128)(2,1)S(1)}, bf16[64,1024]{1,0:T(8,128)(2,1)}, u32[]{:S(2)}) copy-start(bf16[64,1024]{1,0:T(8,128)(2,1)} %up_ref.3) | copy-start | bytes 393220
  52.4 10.0 %collective-permute-start = (bf16[32,16,768]{2,1,0:T(8,128)(2,1)S(1)}, bf16[32,16,768]{2,1,0:T(8,128)(2,1)S(1)}, u32[]{:S(2)}, u32[]{:S(2)}) collective-permute-start(bf16[32,16,768]{2,1,0:T(8,128)(2,1)S(1)} %get-tuple-element.18), channel_id=1, source_target_pairs={{0,8},{8,0},{1,9},{9,1},{2,10},{10,2},{3,11},{11,3},{4,12},{12,4},... | collective-permute-start | bytes 2359304 | tf_op jit(solution)/shard_map/ppermute | solution.py:366
  63.1 31.0 %all-to-all-start.2 = ((bf16[16,40,128]{2,1,0:T(8,128)(2,1)}), bf16[16,40,128]{2,1,0:T(8,128)(2,1)S(1)}, u32[]{:S(2)}, u32[]{:S(2)}) async-start(bf16[16,40,128]{2,1,0:T(8,128)(2,1)} %shard_map.113), calls=%async_computation.2 | async-start | bytes 327680 | tf_op jit(solution)/shard_map/all_to_all | solution.py:328
  82.2 16.4 %collective-permute-start.3 = (bf16[16,16,256]{2,1,0:T(8,128)(2,1)S(1)}, bf16[16,16,256]{2,1,0:T(8,128)(2,1)S(1)}, u32[]{:S(2)}, u32[]{:S(2)}) collective-permute-start(bf16[16,16,256]{2,1,0:T(8,128)(2,1)S(1)} %get-tuple-element.26), channel_id=1, source_target_pairs={{0,272},{16,256},{256,16},{272,0},{1,273},{17,257},{257,17},{273,1... | collective-permute-start | bytes 393224 | tf_op jit(solution)/shard_map/ppermute | solution.py:366
  87.8 10.8 %collective-permute-start.2 = (bf16[16,16,256]{2,1,0:T(8,128)(2,1)S(1)}, bf16[16,16,256]{2,1,0:T(8,128)(2,1)S(1)}, u32[]{:S(2)}, u32[]{:S(2)}) collective-permute-start(bf16[16,16,256]{2,1,0:T(8,128)(2,1)S(1)} %get-tuple-element.27), channel_id=1, source_target_pairs={{0,256},{256,0},{1,257},{257,1},{2,258},{258,2},{3,259},{259,3},{4... | collective-permute-start | bytes 393224 | tf_op jit(solution)/shard_map/ppermute | solution.py:366
  90.1 8.5 %collective-permute-start.1 = (bf16[16,16,256]{2,1,0:T(8,128)(2,1)S(1)}, bf16[16,16,256]{2,1,0:T(8,128)(2,1)S(1)}, u32[]{:S(2)}, u32[]{:S(2)}) collective-permute-start(bf16[16,16,256]{2,1,0:T(8,128)(2,1)S(1)} %get-tuple-element.25), channel_id=1, source_target_pairs={{0,16},{16,0},{1,17},{17,1},{2,18},{18,2},{3,19},{19,3},{4,20},{20... | collective-permute-start | bytes 393224 | tf_op jit(solution)/shard_map/ppermute | solution.py:366
  94.1 6.0 %collective-permute-start.4 = (f32[40,128]{1,0:T(8,128)S(1)}, f32[40,128]{1,0:T(8,128)S(1)}, u32[]{:S(2)}, u32[]{:S(2)}) collective-permute-start(f32[40,128]{1,0:T(8,128)S(1)} %convert_reduce_fusion), channel_id=1, source_target_pairs={{0,256},{256,0},{1,257},{257,1},{2,258},{258,2},{3,259},{259,3},{4... | collective-permute-start | bytes 61448 | tf_op jit(solution)/shard_map/ppermute | solution.py:366
  100.9 22.8 %all-to-all-start.3 = ((bf16[16,72,128]{2,1,0:T(8,128)(2,1)}), bf16[16,72,128]{2,1,0:T(8,128)(2,1)S(1)}, u32[]{:S(2)}, u32[]{:S(2)}) async-start(bf16[16,72,128]{2,1,0:T(8,128)(2,1)} %pad_maximum_fusion), calls=%async_computation.3 | async-start | bytes 589824 | tf_op jit(solution)/shard_map/all_to_all | solution.py:352
  123.9 10.8 %collective-permute-start.5 = (bf16[16,40,128]{2,1,0:T(8,128)(2,1)S(1)}, bf16[16,40,128]{2,1,0:T(8,128)(2,1)S(1)}, u32[]{:S(2)}, u32[]{:S(2)}) collective-permute-start(bf16[16,40,128]{2,1,0:T(8,128)(2,1)S(1)} %slice.24.mine_ref), channel_id=1, source_target_pairs={{0,8},{8,0},{1,9},{9,1},{2,10},{10,2},{3,11},{11,3},{4,12},{12,4},... | collective-permute-start | bytes 491528 | tf_op jit(solution)/shard_map/ppermute | solution.py:366

commit v8 on v7

--- a/solution.py
+++ b/solution.py
@@ -336,7 +336,10 @@
         parts = [lax.dynamic_slice_in_dim(x, z * half, half, 2) for x in parts]
         return parts[0].astype(f32) + parts[1].astype(f32)
 
-    small, value = lax.optimization_barrier((jnp.sum(small.astype(f32), axis=0), quarter(me, odd)))
+    own_gain = lax.dynamic_slice_in_dim(gain, lax.axis_index(ROWS) * own, own, 0)
+    small, value, own_gain = lax.optimization_barrier(
+        (jnp.sum(small.astype(f32), axis=0), quarter(me, odd), own_gain)
+    )
     for y, z, axis in (
         (me, 1 - odd, "z_odd"),
         (1 - me, odd, "y_hi"),
@@ -356,7 +359,6 @@
 
     value = value[:, :lines].astype(f32).reshape(-1, 2, len(tiles), own, LANES)
     value = jnp.sum(value, axis=0).transpose(2, 0, 1, 3).reshape(own, width)
-    own_gain = lax.dynamic_slice_in_dim(gain, lax.axis_index(ROWS) * own, own, 0)
     value_grad = (value * own_gain[:, None]).astype(bf16)
     return (values, value_grad, a_grad.T, b_grad, gain_grad.reshape(-1))
 

time: 136 us -> 135 us (level)
  blocking collectives: 23.2 us -> 45.9 us
  waiting for transfers between devices: 26 us -> 12.9 us
  starting transfers between devices: 64.2 us -> 54.5 us
    all_to_all x0 -> x1, blocking collectives: none -> 22.6 us  [body(): lax.all_to_all(jnp.concatenate([*tiles, small], axis=1), Z, 0, 0, tiled=T...]
    all_to_all x1 -> x0, waiting for transfers between devices: 13 us -> none  [body(): lax.all_to_all(jnp.concatenate([*tiles, small], axis=1), Z, 0, 0, tiled=T...]
    all_to_all x1 -> x0, starting transfers between devices: 9.75 us -> none  [body(): lax.all_to_all(jnp.concatenate([*tiles, small], axis=1), Z, 0, 0, tiled=T...]
  transfers between devices with their start and end apart: 9 -> 8, of which waited for: 6 -> 5; matrix products, arithmetic and copies ran while one was open for 4% -> 4% of each run, Pallas kernels for 0% -> 0%
where the time goes in v8:
time: 135 us
  starting transfers between devices  54.5 us (40%)
  blocking collectives  45.9 us (34%)
  Pallas kernels  14.4 us (11%)
  waiting for transfers between devices  12.9 us (10%)
  local copies, waits for them, and re-layouts  4.8 us (4%)
    ppermute x6, starting transfers between devices, swap(): return lax.ppermute(x, axis, [(i, last - i) for i in range(last + 1)])  32.2 us
    all_to_all x1, blocking collectives, body(): pieces = lax.all_to_all(pieces, TP, 0, 0, tiled=True)  23.2 us
    all_to_all x1, blocking collectives, body(): lax.all_to_all(jnp.concatenate([*tiles, small], axis=1), Z, 0, 0, tiled=T...  22.6 us
    all_to_all x1, starting transfers between devices, body(): small = lax.all_to_all(small, Z, 0, 0, tiled=True)  18.6 us
    all_to_all x1, waiting for transfers between devices, body(): every = lax.all_to_all(every, TP, 0, 0, tiled=True)  7.45 us
    pallas_call x1, Pallas kernels, gradients(): pl.pallas_call(functools.partial(gradients_kernel, z_size), grid=(feature...  5.52 us
    pallas_call x1, Pallas kernels, project(): pl.pallas_call(functools.partial(project_kernel, share), grid=(pieces //...  5.38 us
    unnamed x12, local copies, waits for them, and re-layouts  4.32 us
  transfers between devices with their start and end apart: 8, of which 5 were waited for; matrix products, arithmetic and copies ran while one was open for 4% of the time, Pallas kernels for 0%

profile of v8, /device:TPU:1, one launch (start us, length us, event | category | flops | bytes accessed | tf_op | source)
XLA Modules:
  0.0 134.6 jit_solution(8223900554216721328)
XLA Ops:
  0.6 5.4 %shard_map.110 = bf16[8,160,640]{2,1,0:T(8,128)(2,1)} custom-call(bf16[768,1024]{1,0:T(8,128)(2,1)} %resid_ref.1, bf16[768,1024]{1,0:T(8,128)(2,1)} %heads_ref.1, bf16[1024]{0:T(1024)(128)(2,1)} %gain_ref.1, bf16[1024,512]{1,0:T(8,128)(2,1)} %matrix_ref.3, bf16[64,1024]{1,0:T(8,128)(2,1)} %bitcast.27, bf16[64,1024]{1,0:T(8,128)(2,1)} %up_ref.3), custom_call_target="tpu_custom_call" | custom-call | flops 1207959552 | bytes 4194304 | tf_op jit(solution)/shard_map/pallas_call | solution.py:83
  6.0 0.0 copy-start.2
  6.0 23.2 %all_to_all.20.pieces_ref = bf16[8,160,640]{2,1,0:T(8,128)(2,1)S(1)} all-to-all(bf16[8,160,640]{2,1,0:T(8,128)(2,1)} %shard_map.110), channel_id=1, replica_groups=mesh['y_hi'=2,'z_pair'=8,'z_odd'=2,'core'=2,'x'=4,'y_lo'=2] {'x','y_lo'}, dimensions={0} | all-to-all | bytes 3276800 | tf_op jit(solution)/shard_map/all_to_all | solution.py:315
  29.2 0.0 copy-done.2
  29.2 1.9 %shard_map.111 = (bf16[96,512]{1,0:T(8,128)(2,1)}, bf16[8,96,704]{2,1,0:T(8,128)(2,1)}) custom-call(bf16[8,160,640]{2,1,0:T(8,128)(2,1)S(1)} %all_to_all.20.pieces_ref, bf16[96,512]{1,0:T(8,128)(2,1)S(1)} %copy-done.2), custom_call_target="tpu_custom_call" | custom-call | tf_op jit(solution)/shard_map/pallas_call | solution.py:152
  31.1 0.0 copy-start.3
  31.1 3.7 %all-to-all-start.1 = ((bf16[8,96,704]{2,1,0:T(8,128)(2,1)}), bf16[8,96,704]{2,1,0:T(8,128)(2,1)S(1)}, u32[]{:S(2)}, u32[]{:S(2)}) async-start(bf16[8,96,704]{2,1,0:T(8,128)(2,1)} %get-tuple-element.17), calls=%async_computation.1 | async-start | bytes 2359296 | tf_op jit(solution)/shard_map/all_to_all | solution.py:317
  34.8 0.0 copy-done.3
  34.8 1.6 %copy.20 = bf16[768,1024]{0,1:T(8,128)(2,1)} copy(bf16[768,1024]{1,0:T(8,128)(2,1)S(1)} %copy-done.3) | data formatting | bytes 3145728 | tf_op args[0]
  36.5 0.0 copy-start.4
  36.5 0.0 copy-start
  36.5 0.0 copy-start.1
  36.5 2.7 %copy.21 = bf16[768,1024]{0,1:T(8,128)(2,1)} copy(bf16[768,1024]{1,0:T(8,128)(2,1)} %heads_ref.1) | data formatting | bytes 3145728 | tf_op args[1]
  39.2 0.0 copy-done.4
  39.2 0.2 copy.22.gain_ref
  39.4 7.4 %all-to-all-done.1 = bf16[8,96,704]{2,1,0:T(8,128)(2,1)S(1)} async-done(((bf16[8,96,704]{2,1,0:T(8,128)(2,1)}), bf16[8,96,704]{2,1,0:T(8,128)(2,1)S(1)}, u32[]{:S(2)}, u32[]{:S(2)}) %all-to-all-start.1) | async-done | bytes 1081376 | tf_op jit(solution)/shard_map/all_to_all | solution.py:317
  46.8 0.0 copy-done
  46.8 0.0 copy-done.1
  46.8 5.5 %shard_map.112 = (bf16[32,16,512]{2,1,0:T(8,128)(2,1)S(1)}, f32[32,16,256]{2,1,0:T(8,128)S(1)}, bf16[32,16,768]{2,1,0:T(8,128)(2,1)S(1)}) custom-call(s32[1]{0:T(128)} %bitcast.1.core_ref, bf16[768,704]{1,0:T(8,128)(2,1)S(1)} %bitcast.21, bf16[1024,768]{1,0:T(8,128)(2,1)} %bitcast.23, bf16[1024,768]{1,0:T(8,128)(2,1)} %bitcast.24, ...), custom_call_target="tpu_custom_call" | custom-call | flops 1207959552 | bytes 7340032 | tf_op jit(solution)/shard_map/pallas_call | solution.py:218
  52.4 8.1 %collective-permute-start = (bf16[32,16,768]{2,1,0:T(8,128)(2,1)S(1)}, bf16[32,16,768]{2,1,0:T(8,128)(2,1)S(1)}, u32[]{:S(2)}, u32[]{:S(2)}) collective-permute-start(bf16[32,16,768]{2,1,0:T(8,128)(2,1)S(1)} %get-tuple-element.19), channel_id=1, source_target_pairs={{0,8},{8,0},{1,9},{9,1},{2,10},{10,2},{3,11},{11,3},{4,12},{12,4},... | collective-permute-start | bytes 2359304 | tf_op jit(solution)/shard_map/ppermute | solution.py:368
  60.4 1.9 %collective-permute-done.got_ref = bf16[32,16,768]{2,1,0:T(8,128)(2,1)S(1)} collective-permute-done((bf16[32,16,768]{2,1,0:T(8,128)(2,1)S(1)}, bf16[32,16,768]{2,1,0:T(8,128)(2,1)S(1)}, u32[]{:S(2)}, u32[]{:S(2)}) %collective-permute-start) | collective-permute-done | bytes 786464 | tf_op jit(solution)/shard_map/ppermute | solution.py:368
  62.3 0.7 shard_map.113
  63.0 18.6 %all-to-all-start.2 = ((bf16[16,40,128]{2,1,0:T(8,128)(2,1)}), bf16[16,40,128]{2,1,0:T(8,128)(2,1)S(1)}, u32[]{:S(2)}, u32[]{:S(2)}) async-start(bf16[16,40,128]{2,1,0:T(8,128)(2,1)} %shard_map.113), calls=%async_computation.2 | async-start | bytes 327680 | tf_op jit(solution)/shard_map/all_to_all | solution.py:328
  81.7 0.1 slice.20
  81.7 0.5 fusion
  82.2 5.6 %collective-permute-start.3 = (bf16[16,16,256]{2,1,0:T(8,128)(2,1)S(1)}, bf16[16,16,256]{2,1,0:T(8,128)(2,1)S(1)}, u32[]{:S(2)}, u32[]{:S(2)}) collective-permute-start(bf16[16,16,256]{2,1,0:T(8,128)(2,1)S(1)} %get-tuple-element.28), channel_id=1, source_target_pairs={{0,272},{16,256},{256,16},{272,0},{1,273},{17,257},{257,17},{273,1... | collective-permute-start | bytes 393224 | tf_op jit(solution)/shard_map/ppermute | solution.py:368
  87.8 2.3 %collective-permute-start.2 = (bf16[16,16,256]{2,1,0:T(8,128)(2,1)S(1)}, bf16[16,16,256]{2,1,0:T(8,128)(2,1)S(1)}, u32[]{:S(2)}, u32[]{:S(2)}) collective-permute-start(bf16[16,16,256]{2,1,0:T(8,128)(2,1)S(1)} %get-tuple-element.29), channel_id=1, source_target_pairs={{0,256},{256,0},{1,257},{257,1},{2,258},{258,2},{3,259},{259,3},{4... | collective-permute-start | bytes 393224 | tf_op jit(solution)/shard_map/ppermute | solution.py:368
  90.1 2.0 %collective-permute-start.1 = (bf16[16,16,256]{2,1,0:T(8,128)(2,1)S(1)}, bf16[16,16,256]{2,1,0:T(8,128)(2,1)S(1)}, u32[]{:S(2)}, u32[]{:S(2)}) collective-permute-start(bf16[16,16,256]{2,1,0:T(8,128)(2,1)S(1)} %get-tuple-element.27), channel_id=1, source_target_pairs={{0,16},{16,0},{1,17},{17,1},{2,18},{18,2},{3,19},{19,3},{4,20},{20... | collective-permute-start | bytes 393224 | tf_op jit(solution)/shard_map/ppermute | solution.py:368
  92.1 0.1 dynamic_slice.38
  92.2 1.8 %all-to-all-done.2 = bf16[16,40,128]{2,1,0:T(8,128)(2,1)S(1)} async-done(((bf16[16,40,128]{2,1,0:T(8,128)(2,1)}), bf16[16,40,128]{2,1,0:T(8,128)(2,1)S(1)}, u32[]{:S(2)}, u32[]{:S(2)}) %all-to-all-start.2) | async-done | bytes 163872 | tf_op jit(solution)/shard_map/all_to_all | solution.py:328
  94.1 4.5 %collective-permute-start.4 = (f32[40,128]{1,0:T(8,128)S(1)}, f32[40,128]{1,0:T(8,128)S(1)}, u32[]{:S(2)}, u32[]{:S(2)}) collective-permute-start(f32[40,128]{1,0:T(8,128)S(1)} %convert_reduce_fusion), channel_id=1, source_target_pairs={{0,256},{256,0},{1,257},{257,1},{2,258},{258,2},{3,259},{259,3},{4... | collective-permute-start | bytes 61448 | tf_op jit(solution)/shard_map/ppermute | solution.py:368
  98.6 0.0 collective-permute-done.3
  98.6 0.0 collective-permute-done.2
  98.6 0.0 collective-permute-done.1
  98.6 0.1 add_convert_fusion
  98.7 1.4 %collective-permute-done.4 = f32[40,128]{1,0:T(8,128)S(1)} collective-permute-done((f32[40,128]{1,0:T(8,128)S(1)}, f32[40,128]{1,0:T(8,128)S(1)}, u32[]{:S(2)}, u32[]{:S(2)}) %collective-permute-start.4) | collective-permute-done | bytes 20512 | tf_op jit(solution)/shard_map/ppermute | solution.py:368
  100.2 22.6 %all_to_all.21 = bf16[16,72,128]{2,1,0:T(8,128)(2,1)S(1)} all-to-all(bf16[16,72,128]{2,1,0:T(8,128)(2,1)S(1)} %pad_maximum_fusion), channel_id=1, replica_groups=mesh['y_hi'=2,'z_pair'=8,'z_odd'=2,'core'=2,'x'=4,'y_lo'=2] {'z_pair','z..., dimensions={0} | all-to-all | bytes 589824 | tf_op jit(solution)/shard_map/all_to_all | solution.py:355
  122.9 9.7 %collective-permute-start.5 = (bf16[16,40,128]{2,1,0:T(8,128)(2,1)S(1)}, bf16[16,40,128]{2,1,0:T(8,128)(2,1)S(1)}, u32[]{:S(2)}, u32[]{:S(2)}) collective-permute-start(bf16[16,40,128]{2,1,0:T(8,128)(2,1)S(1)} %slice.24.mine_ref), channel_id=1, source_target_pairs={{0,8},{8,0},{1,9},{9,1},{2,10},{10,2},{3,11},{11,3},{4,12},{12,4},... | collective-permute-start | bytes 491528 | tf_op jit(solution)/shard_map/ppermute | solution.py:368
  132.7 0.7 multiply_convert_fusion
  133.4 0.3 collective-permute-done.5.got_ref
  133.7 0.9 shard_map.114
  (11 shorter events, 0.2 us)
Async XLA Ops:
  6.0 23.2 %copy-start.2 = (bf16[96,512]{1,0:T(8,128)(2,1)S(1)}, bf16[96,512]{1,0:T(8,128)(2,1)}, u32[]{:S(2)}) copy-start(bf16[96,512]{1,0:T(8,128)(2,1)} %target_ref.1) | copy-start | bytes 294916
  31.1 3.7 %copy-start.3 = (bf16[768,1024]{1,0:T(8,128)(2,1)S(1)}, bf16[768,1024]{1,0:T(8,128)(2,1)}, u32[]{:S(2)}) copy-start(bf16[768,1024]{1,0:T(8,128)(2,1)} %resid_ref.1) | copy-start | bytes 4718596
  31.1 15.7 %all-to-all-start.1 = ((bf16[8,96,704]{2,1,0:T(8,128)(2,1)}), bf16[8,96,704]{2,1,0:T(8,128)(2,1)S(1)}, u32[]{:S(2)}, u32[]{:S(2)}) async-start(bf16[8,96,704]{2,1,0:T(8,128)(2,1)} %get-tuple-element.17), calls=%async_computation.1 | async-start | bytes 2359296 | tf_op jit(solution)/shard_map/all_to_all | solution.py:317
  36.5 2.7 %copy-start.4 = (bf16[1024]{0:T(1024)(128)(2,1)S(1)}, bf16[1024]{0:T(1024)(128)(2,1)}, u32[]{:S(2)}) copy-start(bf16[1024]{0:T(1024)(128)(2,1)} %gain_ref.1) | copy-start | bytes 6148
  36.5 10.4 %copy-start = (bf16[1024,512]{1,0:T(8,128)(2,1)S(1)}, bf16[1024,512]{1,0:T(8,128)(2,1)}, u32[]{:S(2)}) copy-start(bf16[1024,512]{1,0:T(8,128)(2,1)} %matrix_ref.3) | copy-start | bytes 3145732
  36.5 10.4 %copy-start.1 = (bf16[64,1024]{1,0:T(8,128)(2,1)S(1)}, bf16[64,1024]{1,0:T(8,128)(2,1)}, u32[]{:S(2)}) copy-start(bf16[64,1024]{1,0:T(8,128)(2,1)} %up_ref.3) | copy-start | bytes 393220
  52.4 10.0 %collective-permute-start = (bf16[32,16,768]{2,1,0:T(8,128)(2,1)S(1)}, bf16[32,16,768]{2,1,0:T(8,128)(2,1)S(1)}, u32[]{:S(2)}, u32[]{:S(2)}) collective-permute-start(bf16[32,16,768]{2,1,0:T(8,128)(2,1)S(1)} %get-tuple-element.19), channel_id=1, source_target_pairs={{0,8},{8,0},{1,9},{9,1},{2,10},{10,2},{3,11},{11,3},{4,12},{12,4},... | collective-permute-start | bytes 2359304 | tf_op jit(solution)/shard_map/ppermute | solution.py:368
  63.0 31.0 %all-to-all-start.2 = ((bf16[16,40,128]{2,1,0:T(8,128)(2,1)}), bf16[16,40,128]{2,1,0:T(8,128)(2,1)S(1)}, u32[]{:S(2)}, u32[]{:S(2)}) async-start(bf16[16,40,128]{2,1,0:T(8,128)(2,1)} %shard_map.113), calls=%async_computation.2 | async-start | bytes 327680 | tf_op jit(solution)/shard_map/all_to_all | solution.py:328
  82.2 16.4 %collective-permute-start.3 = (bf16[16,16,256]{2,1,0:T(8,128)(2,1)S(1)}, bf16[16,16,256]{2,1,0:T(8,128)(2,1)S(1)}, u32[]{:S(2)}, u32[]{:S(2)}) collective-permute-start(bf16[16,16,256]{2,1,0:T(8,128)(2,1)S(1)} %get-tuple-element.28), channel_id=1, source_target_pairs={{0,272},{16,256},{256,16},{272,0},{1,273},{17,257},{257,17},{273,1... | collective-permute-start | bytes 393224 | tf_op jit(solution)/shard_map/ppermute | solution.py:368
  87.8 10.8 %collective-permute-start.2 = (bf16[16,16,256]{2,1,0:T(8,128)(2,1)S(1)}, bf16[16,16,256]{2,1,0:T(8,128)(2,1)S(1)}, u32[]{:S(2)}, u32[]{:S(2)}) collective-permute-start(bf16[16,16,256]{2,1,0:T(8,128)(2,1)S(1)} %get-tuple-element.29), channel_id=1, source_target_pairs={{0,256},{256,0},{1,257},{257,1},{2,258},{258,2},{3,259},{259,3},{4... | collective-permute-start | bytes 393224 | tf_op jit(solution)/shard_map/ppermute | solution.py:368
  90.1 8.5 %collective-permute-start.1 = (bf16[16,16,256]{2,1,0:T(8,128)(2,1)S(1)}, bf16[16,16,256]{2,1,0:T(8,128)(2,1)S(1)}, u32[]{:S(2)}, u32[]{:S(2)}) collective-permute-start(bf16[16,16,256]{2,1,0:T(8,128)(2,1)S(1)} %get-tuple-element.27), channel_id=1, source_target_pairs={{0,16},{16,0},{1,17},{17,1},{2,18},{18,2},{3,19},{19,3},{4,20},{20... | collective-permute-start | bytes 393224 | tf_op jit(solution)/shard_map/ppermute | solution.py:368
  94.1 6.0 %collective-permute-start.4 = (f32[40,128]{1,0:T(8,128)S(1)}, f32[40,128]{1,0:T(8,128)S(1)}, u32[]{:S(2)}, u32[]{:S(2)}) collective-permute-start(f32[40,128]{1,0:T(8,128)S(1)} %convert_reduce_fusion), channel_id=1, source_target_pairs={{0,256},{256,0},{1,257},{257,1},{2,258},{258,2},{3,259},{259,3},{4... | collective-permute-start | bytes 61448 | tf_op jit(solution)/shard_map/ppermute | solution.py:368
  122.9 10.7 %collective-permute-start.5 = (bf16[16,40,128]{2,1,0:T(8,128)(2,1)S(1)}, bf16[16,40,128]{2,1,0:T(8,128)(2,1)S(1)}, u32[]{:S(2)}, u32[]{:S(2)}) collective-permute-start(bf16[16,40,128]{2,1,0:T(8,128)(2,1)S(1)} %slice.24.mine_ref), channel_id=1, source_target_pairs={{0,8},{8,0},{1,9},{9,1},{2,10},{10,2},{3,11},{11,3},{4,12},{12,4},... | collective-permute-start | bytes 491528 | tf_op jit(solution)/shard_map/ppermute | solution.py:368

commit v9 on v8

--- a/solution.py
+++ b/solution.py
@@ -341,9 +341,9 @@
         (jnp.sum(small.astype(f32), axis=0), quarter(me, odd), own_gain)
     )
     for y, z, axis in (
+        (1 - me, 1 - odd, ("y_hi", "z_odd")),
         (me, 1 - odd, "z_odd"),
         (1 - me, odd, "y_hi"),
-        (1 - me, 1 - odd, ("y_hi", "z_odd")),
     ):
         value = value + swap(quarter(y, z).astype(bf16), axis).astype(f32)
     value = value.astype(bf16)

time: 135 us -> 136 us (level)
  no operation moved by 1% of the time
where the time goes in v9:
time: 136 us; the launch traced here: 135 us
  starting transfers between devices  54.3 us (40%)
  blocking collectives  46.6 us (34%)
  Pallas kernels  14.4 us (11%)
  waiting for transfers between devices  13.1 us (10%)
  local copies, waits for them, and re-layouts  4.8 us (4%)
    ppermute x6, starting transfers between devices, swap(): return lax.ppermute(x, axis, [(i, last - i) for i in range(last + 1)])  32 us
    all_to_all x1, blocking collectives, body(): lax.all_to_all(jnp.concatenate([*tiles, small], axis=1), Z, 0, 0, tiled=T...  23.3 us
    all_to_all x1, blocking collectives, body(): pieces = lax.all_to_all(pieces, TP, 0, 0, tiled=True)  23.2 us
    all_to_all x1, starting transfers between devices, body(): small = lax.all_to_all(small, Z, 0, 0, tiled=True)  18.6 us
    all_to_all x1, waiting for transfers between devices, body(): every = lax.all_to_all(every, TP, 0, 0, tiled=True)  7.45 us
    pallas_call x1, Pallas kernels, gradients(): pl.pallas_call(functools.partial(gradients_kernel, z_size), grid=(feature...  5.52 us
    pallas_call x1, Pallas kernels, project(): pl.pallas_call(functools.partial(project_kernel, share), grid=(pieces //...  5.38 us
    unnamed x12, local copies, waits for them, and re-layouts  4.32 us
  transfers between devices with their start and end apart: 8, of which 5 were waited for; matrix products, arithmetic and copies ran while one was open for 4% of the time, Pallas kernels for 0%

profile of v9, /device:TPU:1, one launch (start us, length us, event | category | flops | bytes accessed | tf_op | source)
XLA Modules:
  0.0 135.3 jit_solution(6043340566692691052)
XLA Ops:
  0.6 5.4 %shard_map.110 = bf16[8,160,640]{2,1,0:T(8,128)(2,1)} custom-call(bf16[768,1024]{1,0:T(8,128)(2,1)} %resid_ref.1, bf16[768,1024]{1,0:T(8,128)(2,1)} %heads_ref.1, bf16[1024]{0:T(1024)(128)(2,1)} %gain_ref.1, bf16[1024,512]{1,0:T(8,128)(2,1)} %matrix_ref.3, bf16[64,1024]{1,0:T(8,128)(2,1)} %bitcast.27, bf16[64,1024]{1,0:T(8,128)(2,1)} %up_ref.3), custom_call_target="tpu_custom_call" | custom-call | flops 1207959552 | bytes 4194304 | tf_op jit(solution)/shard_map/pallas_call | solution.py:83
  6.0 0.0 copy-start.2
  6.0 23.2 %all_to_all.20.pieces_ref = bf16[8,160,640]{2,1,0:T(8,128)(2,1)S(1)} all-to-all(bf16[8,160,640]{2,1,0:T(8,128)(2,1)} %shard_map.110), channel_id=1, replica_groups=mesh['y_hi'=2,'z_pair'=8,'z_odd'=2,'core'=2,'x'=4,'y_lo'=2] {'x','y_lo'}, dimensions={0} | all-to-all | bytes 3276800 | tf_op jit(solution)/shard_map/all_to_all | solution.py:315
  29.2 0.0 copy-done.2
  29.2 1.9 %shard_map.111 = (bf16[96,512]{1,0:T(8,128)(2,1)}, bf16[8,96,704]{2,1,0:T(8,128)(2,1)}) custom-call(bf16[8,160,640]{2,1,0:T(8,128)(2,1)S(1)} %all_to_all.20.pieces_ref, bf16[96,512]{1,0:T(8,128)(2,1)S(1)} %copy-done.2), custom_call_target="tpu_custom_call" | custom-call | tf_op jit(solution)/shard_map/pallas_call | solution.py:152
  31.1 0.0 copy-start.3
  31.1 3.7 %all-to-all-start.1 = ((bf16[8,96,704]{2,1,0:T(8,128)(2,1)}), bf16[8,96,704]{2,1,0:T(8,128)(2,1)S(1)}, u32[]{:S(2)}, u32[]{:S(2)}) async-start(bf16[8,96,704]{2,1,0:T(8,128)(2,1)} %get-tuple-element.17), calls=%async_computation.1 | async-start | bytes 2359296 | tf_op jit(solution)/shard_map/all_to_all | solution.py:317
  34.8 0.0 copy-done.3
  34.8 1.6 %copy.20 = bf16[768,1024]{0,1:T(8,128)(2,1)} copy(bf16[768,1024]{1,0:T(8,128)(2,1)S(1)} %copy-done.3) | data formatting | bytes 3145728 | tf_op args[0]
  36.5 0.0 copy-start.4
  36.5 0.0 copy-start
  36.5 0.0 copy-start.1
  36.5 2.7 %copy.21 = bf16[768,1024]{0,1:T(8,128)(2,1)} copy(bf16[768,1024]{1,0:T(8,128)(2,1)} %heads_ref.1) | data formatting | bytes 3145728 | tf_op args[1]
  39.2 0.0 copy-done.4
  39.2 0.2 copy.22.gain_ref
  39.4 7.4 %all-to-all-done.1 = bf16[8,96,704]{2,1,0:T(8,128)(2,1)S(1)} async-done(((bf16[8,96,704]{2,1,0:T(8,128)(2,1)}), bf16[8,96,704]{2,1,0:T(8,128)(2,1)S(1)}, u32[]{:S(2)}, u32[]{:S(2)}) %all-to-all-start.1) | async-done | bytes 1081376 | tf_op jit(solution)/shard_map/all_to_all | solution.py:317
  46.8 0.0 copy-done
  46.8 0.0 copy-done.1
  46.8 5.5 %shard_map.112 = (bf16[32,16,512]{2,1,0:T(8,128)(2,1)S(1)}, f32[32,16,256]{2,1,0:T(8,128)S(1)}, bf16[32,16,768]{2,1,0:T(8,128)(2,1)S(1)}) custom-call(s32[1]{0:T(128)} %bitcast.1.core_ref, bf16[768,704]{1,0:T(8,128)(2,1)S(1)} %bitcast.21, bf16[1024,768]{1,0:T(8,128)(2,1)} %bitcast.23, bf16[1024,768]{1,0:T(8,128)(2,1)} %bitcast.24, ...), custom_call_target="tpu_custom_call" | custom-call | flops 1207959552 | bytes 7340032 | tf_op jit(solution)/shard_map/pallas_call | solution.py:218
  52.4 8.1 %collective-permute-start = (bf16[32,16,768]{2,1,0:T(8,128)(2,1)S(1)}, bf16[32,16,768]{2,1,0:T(8,128)(2,1)S(1)}, u32[]{:S(2)}, u32[]{:S(2)}) collective-permute-start(bf16[32,16,768]{2,1,0:T(8,128)(2,1)S(1)} %get-tuple-element.19), channel_id=1, source_target_pairs={{0,8},{8,0},{1,9},{9,1},{2,10},{10,2},{3,11},{11,3},{4,12},{12,4},... | collective-permute-start | bytes 2359304 | tf_op jit(solution)/shard_map/ppermute | solution.py:368
  60.4 1.9 %collective-permute-done.got_ref = bf16[32,16,768]{2,1,0:T(8,128)(2,1)S(1)} collective-permute-done((bf16[32,16,768]{2,1,0:T(8,128)(2,1)S(1)}, bf16[32,16,768]{2,1,0:T(8,128)(2,1)S(1)}, u32[]{:S(2)}, u32[]{:S(2)}) %collective-permute-start) | collective-permute-done | bytes 786464 | tf_op jit(solution)/shard_map/ppermute | solution.py:368
  62.3 0.7 shard_map.113
  63.0 18.6 %all-to-all-start.2 = ((bf16[16,40,128]{2,1,0:T(8,128)(2,1)}), bf16[16,40,128]{2,1,0:T(8,128)(2,1)S(1)}, u32[]{:S(2)}, u32[]{:S(2)}) async-start(bf16[16,40,128]{2,1,0:T(8,128)(2,1)} %shard_map.113), calls=%async_computation.2 | async-start | bytes 327680 | tf_op jit(solution)/shard_map/all_to_all | solution.py:328
  81.7 0.1 slice.20
  81.7 0.5 fusion
  82.2 4.5 %collective-permute-start.3 = (bf16[16,16,256]{2,1,0:T(8,128)(2,1)S(1)}, bf16[16,16,256]{2,1,0:T(8,128)(2,1)S(1)}, u32[]{:S(2)}, u32[]{:S(2)}) collective-permute-start(bf16[16,16,256]{2,1,0:T(8,128)(2,1)S(1)} %get-tuple-element.28), channel_id=1, source_target_pairs={{0,256},{256,0},{1,257},{257,1},{2,258},{258,2},{3,259},{259,3},{4... | collective-permute-start | bytes 393224 | tf_op jit(solution)/shard_map/ppermute | solution.py:368
  86.8 3.3 %collective-permute-start.2 = (bf16[16,16,256]{2,1,0:T(8,128)(2,1)S(1)}, bf16[16,16,256]{2,1,0:T(8,128)(2,1)S(1)}, u32[]{:S(2)}, u32[]{:S(2)}) collective-permute-start(bf16[16,16,256]{2,1,0:T(8,128)(2,1)S(1)} %get-tuple-element.29), channel_id=1, source_target_pairs={{0,16},{16,0},{1,17},{17,1},{2,18},{18,2},{3,19},{19,3},{4,20},{20... | collective-permute-start | bytes 393224 | tf_op jit(solution)/shard_map/ppermute | solution.py:368
  90.0 2.1 %collective-permute-start.1 = (bf16[16,16,256]{2,1,0:T(8,128)(2,1)S(1)}, bf16[16,16,256]{2,1,0:T(8,128)(2,1)S(1)}, u32[]{:S(2)}, u32[]{:S(2)}) collective-permute-start(bf16[16,16,256]{2,1,0:T(8,128)(2,1)S(1)} %get-tuple-element.27), channel_id=1, source_target_pairs={{0,272},{16,256},{256,16},{272,0},{1,273},{17,257},{257,17},{273,1... | collective-permute-start | bytes 393224 | tf_op jit(solution)/shard_map/ppermute | solution.py:368
  92.1 0.1 dynamic_slice.38
  92.2 1.8 %all-to-all-done.2 = bf16[16,40,128]{2,1,0:T(8,128)(2,1)S(1)} async-done(((bf16[16,40,128]{2,1,0:T(8,128)(2,1)}), bf16[16,40,128]{2,1,0:T(8,128)(2,1)S(1)}, u32[]{:S(2)}, u32[]{:S(2)}) %all-to-all-start.2) | async-done | bytes 163872 | tf_op jit(solution)/shard_map/all_to_all | solution.py:328
  94.1 4.6 %collective-permute-start.4 = (f32[40,128]{1,0:T(8,128)S(1)}, f32[40,128]{1,0:T(8,128)S(1)}, u32[]{:S(2)}, u32[]{:S(2)}) collective-permute-start(f32[40,128]{1,0:T(8,128)S(1)} %convert_reduce_fusion), channel_id=1, source_target_pairs={{0,256},{256,0},{1,257},{257,1},{2,258},{258,2},{3,259},{259,3},{4... | collective-permute-start | bytes 61448 | tf_op jit(solution)/shard_map/ppermute | solution.py:368
  98.6 0.0 collective-permute-done.3
  98.7 0.0 collective-permute-done.2
  98.7 0.0 collective-permute-done.1
  98.7 0.1 add_convert_fusion
  98.8 1.6 %collective-permute-done.4 = f32[40,128]{1,0:T(8,128)S(1)} collective-permute-done((f32[40,128]{1,0:T(8,128)S(1)}, f32[40,128]{1,0:T(8,128)S(1)}, u32[]{:S(2)}, u32[]{:S(2)}) %collective-permute-start.4) | collective-permute-done | bytes 20512 | tf_op jit(solution)/shard_map/ppermute | solution.py:368
  100.4 23.3 %all_to_all.21 = bf16[16,72,128]{2,1,0:T(8,128)(2,1)S(1)} all-to-all(bf16[16,72,128]{2,1,0:T(8,128)(2,1)S(1)} %pad_maximum_fusion), channel_id=1, replica_groups=mesh['y_hi'=2,'z_pair'=8,'z_odd'=2,'core'=2,'x'=4,'y_lo'=2] {'z_pair','z..., dimensions={0} | all-to-all | bytes 589824 | tf_op jit(solution)/shard_map/all_to_all | solution.py:355
  123.9 9.5 %collective-permute-start.5 = (bf16[16,40,128]{2,1,0:T(8,128)(2,1)S(1)}, bf16[16,40,128]{2,1,0:T(8,128)(2,1)S(1)}, u32[]{:S(2)}, u32[]{:S(2)}) collective-permute-start(bf16[16,40,128]{2,1,0:T(8,128)(2,1)S(1)} %slice.24.mine_ref), channel_id=1, source_target_pairs={{0,8},{8,0},{1,9},{9,1},{2,10},{10,2},{3,11},{11,3},{4,12},{12,4},... | collective-permute-start | bytes 491528 | tf_op jit(solution)/shard_map/ppermute | solution.py:368
  133.4 0.7 multiply_convert_fusion
  134.1 0.3 collective-permute-done.5.got_ref
  134.4 0.9 shard_map.114
  (11 shorter events, 0.2 us)
Async XLA Ops:
  6.0 23.2 %copy-start.2 = (bf16[96,512]{1,0:T(8,128)(2,1)S(1)}, bf16[96,512]{1,0:T(8,128)(2,1)}, u32[]{:S(2)}) copy-start(bf16[96,512]{1,0:T(8,128)(2,1)} %target_ref.1) | copy-start | bytes 294916
  31.1 3.7 %copy-start.3 = (bf16[768,1024]{1,0:T(8,128)(2,1)S(1)}, bf16[768,1024]{1,0:T(8,128)(2,1)}, u32[]{:S(2)}) copy-start(bf16[768,1024]{1,0:T(8,128)(2,1)} %resid_ref.1) | copy-start | bytes 4718596
  31.1 15.7 %all-to-all-start.1 = ((bf16[8,96,704]{2,1,0:T(8,128)(2,1)}), bf16[8,96,704]{2,1,0:T(8,128)(2,1)S(1)}, u32[]{:S(2)}, u32[]{:S(2)}) async-start(bf16[8,96,704]{2,1,0:T(8,128)(2,1)} %get-tuple-element.17), calls=%async_computation.1 | async-start | bytes 2359296 | tf_op jit(solution)/shard_map/all_to_all | solution.py:317
  36.5 2.7 %copy-start.4 = (bf16[1024]{0:T(1024)(128)(2,1)S(1)}, bf16[1024]{0:T(1024)(128)(2,1)}, u32[]{:S(2)}) copy-start(bf16[1024]{0:T(1024)(128)(2,1)} %gain_ref.1) | copy-start | bytes 6148
  36.5 10.4 %copy-start = (bf16[1024,512]{1,0:T(8,128)(2,1)S(1)}, bf16[1024,512]{1,0:T(8,128)(2,1)}, u32[]{:S(2)}) copy-start(bf16[1024,512]{1,0:T(8,128)(2,1)} %matrix_ref.3) | copy-start | bytes 3145732
  36.5 10.4 %copy-start.1 = (bf16[64,1024]{1,0:T(8,128)(2,1)S(1)}, bf16[64,1024]{1,0:T(8,128)(2,1)}, u32[]{:S(2)}) copy-start(bf16[64,1024]{1,0:T(8,128)(2,1)} %up_ref.3) | copy-start | bytes 393220
  52.4 10.0 %collective-permute-start = (bf16[32,16,768]{2,1,0:T(8,128)(2,1)S(1)}, bf16[32,16,768]{2,1,0:T(8,128)(2,1)S(1)}, u32[]{:S(2)}, u32[]{:S(2)}) collective-permute-start(bf16[32,16,768]{2,1,0:T(8,128)(2,1)S(1)} %get-tuple-element.19), channel_id=1, source_target_pairs={{0,8},{8,0},{1,9},{9,1},{2,10},{10,2},{3,11},{11,3},{4,12},{12,4},... | collective-permute-start | bytes 2359304 | tf_op jit(solution)/shard_map/ppermute | solution.py:368
  63.0 31.0 %all-to-all-start.2 = ((bf16[16,40,128]{2,1,0:T(8,128)(2,1)}), bf16[16,40,128]{2,1,0:T(8,128)(2,1)S(1)}, u32[]{:S(2)}, u32[]{:S(2)}) async-start(bf16[16,40,128]{2,1,0:T(8,128)(2,1)} %shard_map.113), calls=%async_computation.2 | async-start | bytes 327680 | tf_op jit(solution)/shard_map/all_to_all | solution.py:328
  82.2 16.4 %collective-permute-start.3 = (bf16[16,16,256]{2,1,0:T(8,128)(2,1)S(1)}, bf16[16,16,256]{2,1,0:T(8,128)(2,1)S(1)}, u32[]{:S(2)}, u32[]{:S(2)}) collective-permute-start(bf16[16,16,256]{2,1,0:T(8,128)(2,1)S(1)} %get-tuple-element.28), channel_id=1, source_target_pairs={{0,256},{256,0},{1,257},{257,1},{2,258},{258,2},{3,259},{259,3},{4... | collective-permute-start | bytes 393224 | tf_op jit(solution)/shard_map/ppermute | solution.py:368
  86.8 11.9 %collective-permute-start.2 = (bf16[16,16,256]{2,1,0:T(8,128)(2,1)S(1)}, bf16[16,16,256]{2,1,0:T(8,128)(2,1)S(1)}, u32[]{:S(2)}, u32[]{:S(2)}) collective-permute-start(bf16[16,16,256]{2,1,0:T(8,128)(2,1)S(1)} %get-tuple-element.29), channel_id=1, source_target_pairs={{0,16},{16,0},{1,17},{17,1},{2,18},{18,2},{3,19},{19,3},{4,20},{20... | collective-permute-start | bytes 393224 | tf_op jit(solution)/shard_map/ppermute | solution.py:368
  90.0 8.6 %collective-permute-start.1 = (bf16[16,16,256]{2,1,0:T(8,128)(2,1)S(1)}, bf16[16,16,256]{2,1,0:T(8,128)(2,1)S(1)}, u32[]{:S(2)}, u32[]{:S(2)}) collective-permute-start(bf16[16,16,256]{2,1,0:T(8,128)(2,1)S(1)} %get-tuple-element.27), channel_id=1, source_target_pairs={{0,272},{16,256},{256,16},{272,0},{1,273},{17,257},{257,17},{273,1... | collective-permute-start | bytes 393224 | tf_op jit(solution)/shard_map/ppermute | solution.py:368
  94.1 6.3 %collective-permute-start.4 = (f32[40,128]{1,0:T(8,128)S(1)}, f32[40,128]{1,0:T(8,128)S(1)}, u32[]{:S(2)}, u32[]{:S(2)}) collective-permute-start(f32[40,128]{1,0:T(8,128)S(1)} %convert_reduce_fusion), channel_id=1, source_target_pairs={{0,256},{256,0},{1,257},{257,1},{2,258},{258,2},{3,259},{259,3},{4... | collective-permute-start | bytes 61448 | tf_op jit(solution)/shard_map/ppermute | solution.py:368
  123.9 10.5 %collective-permute-start.5 = (bf16[16,40,128]{2,1,0:T(8,128)(2,1)S(1)}, bf16[16,40,128]{2,1,0:T(8,128)(2,1)S(1)}, u32[]{:S(2)}, u32[]{:S(2)}) collective-permute-start(bf16[16,40,128]{2,1,0:T(8,128)(2,1)S(1)} %slice.24.mine_ref), channel_id=1, source_target_pairs={{0,8},{8,0},{1,9},{9,1},{2,10},{10,2},{3,11},{11,3},{4,12},{12,4},... | collective-permute-start | bytes 491528 | tf_op jit(solution)/shard_map/ppermute | solution.py:368
